TPU v7x, 128 devices: a whole 4x4x4 slice. The times are simulated.
128 devices in a mesh: dp: 16 (over x_hi, y, core), ctx: 8 (over x_lo, z).
Axes of the slice: x: 4 (x_hi: 2, x_lo: 2; x = x_hi * 2 + x_lo), y: 4, z: 4, core: 2. Of those that a mesh axis runs over, the one named last changes fastest.
Arguments:
- tokens: bfloat16 [16, 2048, 8192], P('dp', 'ctx'), may hold values from -16 to 16
- positions: int32 [2048], replicated, may hold values from 0 to 2047, as said below
- query_weight: float32 [8192, 512], P(('dp', 'ctx')), may hold values from -0.5 to 0.5
- key_weight: float32 [8192, 128], P(('dp', 'ctx')), may hold values from -0.5 to 0.5
- value_weight: float32 [8192, 128], P(('dp', 'ctx')), may hold values from -0.0625 to 0.0625
- grad_output: bfloat16 [16, 2048, 512], P('dp', 'ctx'), may hold values from -6 to 6
Outputs:
- attention: bfloat16 [16, 2048, 512], P('dp', 'ctx')
- grad_tokens: bfloat16 [16, 2048, 8192], P('dp', 'ctx')
- query_grad: float32 [8192, 512], P(('dp', 'ctx'))
- key_grad: float32 [8192, 128], P(('dp', 'ctx'))
- value_grad: float32 [8192, 128], P(('dp', 'ctx'))
Inputs may be any that keep to these rules, and one draw needn't show every extreme that they name: Stored rows come in runs of 128; each run holds consecutive increasing positions starting at a multiple of 128; together the runs hold every position of the sequence once.
All inputs are finite; a program needn't handle non-finite values.
Results may differ from a plain program's by a relative error of at most 0.034.
Values may be sent and summed in bfloat16 or wider, within the bound.
A program may use at most 192 MiB of HBM per device.

v0:
```python
import jax
import jax.numpy as jnp
from jax import lax
from jax.sharding import PartitionSpec as P

ROPE_BASE = 1000000.0
MASKED = -1e30


def rope_tables(positions_in, head_dim):
    half_width = head_dim // 2
    exponent = jnp.arange(half_width).astype(jnp.float32) * (2.0 / head_dim)
    frequency = jnp.power(ROPE_BASE, -exponent)
    angles = positions_in.astype(jnp.float32)[:, None] * frequency[None, :]
    angles = jnp.concatenate([angles, angles], axis=1)
    return (jnp.cos(angles), jnp.sin(angles))


def rotate(field, cos_table, sin_table):
    half_width = field.shape[-1] // 2
    turned = jnp.concatenate([-field[..., half_width:], field[..., :half_width]], axis=-1)
    return field * cos_table + turned * sin_table


def unrotate(field, cos_table, sin_table):
    half_width = field.shape[-1] // 2
    turned = jnp.concatenate([field[..., half_width:], -field[..., :half_width]], axis=-1)
    return field * cos_table + turned * sin_table


def body(tokens, positions, query_weight, key_weight, value_weight, grad_output):
    token_rows = tokens[0]
    local_rows = token_rows.shape[0]
    head_dim = key_weight.shape[1]
    query_width = query_weight.shape[1]
    head_count = query_width // head_dim
    score_scale = head_dim ** (-0.5)
    local_weights = jnp.concatenate([query_weight, key_weight, value_weight], axis=1).astype(
        jnp.bfloat16
    )
    weights_all = lax.all_gather(local_weights, ("dp", "ctx"), axis=0, tiled=True)
    projected = jnp.dot(token_rows, weights_all, preferred_element_type=jnp.float32)
    place_index = lax.axis_index("ctx")
    own_positions = lax.dynamic_slice_in_dim(positions, place_index * local_rows, local_rows)
    cos_table, sin_table = rope_tables(own_positions, head_dim)
    query = projected[:, :query_width].reshape(local_rows, head_count, head_dim)
    query_heads = rotate(query, cos_table[:, None, :], sin_table[:, None, :]).astype(jnp.bfloat16)
    key_rot = rotate(
        projected[:, query_width : query_width + head_dim], cos_table, sin_table
    ).astype(jnp.bfloat16)
    value_b = projected[:, query_width + head_dim :].astype(jnp.bfloat16)
    key_value = jnp.concatenate([key_rot, value_b], axis=1)
    key_piece = lax.all_gather(key_value, "ctx", axis=0, tiled=True)
    running_max = jnp.full((local_rows, head_count), MASKED, jnp.float32)
    allowed = positions[None, :] <= own_positions[:, None]
    scores = (
        jnp.einsum(
            "qhd,kd->qhk", query_heads, key_piece[:, :head_dim], preferred_element_type=jnp.float32
        )
        * score_scale
    )
    scores = jnp.where(allowed[:, None, :], scores, MASKED)
    new_max = jnp.maximum(running_max, jnp.max(scores, axis=-1))
    weight = jnp.where(allowed[:, None, :], jnp.exp(scores - new_max[..., None]), 0.0)
    denominator = jnp.sum(weight, axis=-1)
    weighted = jnp.einsum(
        "qhk,kd->qhd",
        weight.astype(jnp.bfloat16),
        key_piece[:, head_dim:],
        preferred_element_type=jnp.float32,
    )
    running_max, denominator, weighted = (new_max, denominator, weighted)
    keys_values = lax.all_gather(key_value, "ctx", axis=0, tiled=True)
    log_total = running_max + jnp.log(denominator)
    attention = (weighted / denominator[..., None]).astype(jnp.bfloat16)
    grad_heads = grad_output[0].reshape(local_rows, head_count, head_dim)
    row_delta = jnp.sum(grad_heads.astype(jnp.float32) * attention.astype(jnp.float32), axis=-1)
    key_all = keys_values[:, :head_dim]
    value_all = keys_values[:, head_dim:]
    allowed = positions[None, :] <= own_positions[:, None]
    scores = (
        jnp.einsum("qhd,kd->qhk", query_heads, key_all, preferred_element_type=jnp.float32)
        * score_scale
    )
    probs = jnp.where(allowed[:, None, :], jnp.exp(scores - log_total[..., None]), 0.0)
    grad_probs = jnp.einsum(
        "qhd,kd->qhk", grad_heads, value_all, preferred_element_type=jnp.float32
    )
    dscore = (probs * (grad_probs - row_delta[..., None])).astype(jnp.bfloat16)
    probs_b = probs.astype(jnp.bfloat16)
    grad_query_rot = (
        jnp.einsum("qhk,kd->qhd", dscore, key_all, preferred_element_type=jnp.float32) * score_scale
    )
    key_term = (
        jnp.einsum("qhk,qhd->kd", dscore, query_heads, preferred_element_type=jnp.float32)
        * score_scale
    )
    value_term = jnp.einsum("qhk,qhd->kd", probs_b, grad_heads, preferred_element_type=jnp.float32)
    keyval_term = jnp.concatenate([key_term, value_term], axis=1)
    keyval_grad = lax.psum_scatter(
        keyval_term.astype(jnp.bfloat16), "ctx", scatter_dimension=0, tiled=True
    ).astype(jnp.float32)
    grad_query = unrotate(grad_query_rot, cos_table[:, None, :], sin_table[:, None, :]).reshape(
        local_rows, query_width
    )
    grad_key = unrotate(keyval_grad[:, :head_dim], cos_table, sin_table)
    grad_proj = jnp.concatenate([grad_query, grad_key, keyval_grad[:, head_dim:]], axis=1).astype(
        jnp.bfloat16
    )
    grad_input = lax.dot_general(
        grad_proj, weights_all, (((1,), (1,)), ((), ())), preferred_element_type=jnp.float32
    ).astype(jnp.bfloat16)
    weight_grads = lax.psum_scatter(
        lax.dot_general(
            token_rows, grad_proj, (((0,), (0,)), ((), ())), preferred_element_type=jnp.float32
        ),
        ("dp", "ctx"),
        scatter_dimension=0,
        tiled=True,
    )
    query_grad = weight_grads[:, :query_width]
    key_grad = weight_grads[:, query_width : query_width + head_dim]
    value_grad = weight_grads[:, query_width + head_dim :]
    attention_rows = attention.reshape(local_rows, query_width)
    return (attention_rows[None], grad_input[None], query_grad, key_grad, value_grad)


def solution(mesh):
    in_specs = (
        P("dp", "ctx", None),
        P(),
        P(("dp", "ctx"), None),
        P(("dp", "ctx"), None),
        P(("dp", "ctx"), None),
        P("dp", "ctx", None),
    )
    out_specs = (
        P("dp", "ctx", None),
        P("dp", "ctx", None),
        P(("dp", "ctx"), None),
        P(("dp", "ctx"), None),
        P(("dp", "ctx"), None),
    )
    return jax.shard_map(body, mesh=mesh, in_specs=in_specs, out_specs=out_specs, check_vma=False)
```

profile of v0, /device:TPU:0, one launch (start us, length us, event | category | flops | bytes accessed | tf_op | source)
XLA Modules:
  0.0 1176.2 jit_solution(5239057661142810609)
XLA Ops:
  8.7 0.9 convert.27
  10.4 0.8 fusion.50
  11.3 322.9 %all-gather.3.cloned.1.call-done = bf16[8192,768]{1,0:T(8,128)(2,1)} async-done(((bf16[64,768]{1,0:T(8,128)(2,1)}), bf16[8192,768]{1,0:T(8,128)(2,1)}) %all-gather.3.cloned.1.call-update) | async-done | bytes 12582928 | tf_op jit(solution)/shard_map/all_gather | solution.py:41
  334.2 7.7 fusion.22
  344.1 37.3 %all-gather.5.cloned.1.call-done = bf16[2048,256]{0,1:T(8,128)(2,1)} async-done(((bf16[256,256]{0,1:T(8,128)(2,1)}), bf16[2048,256]{0,1:T(8,128)(2,1)}) %all-gather.5.cloned.1.call-update) | async-done | bytes 1048592 | tf_op jit(solution)/shard_map/all_gather | solution.py:53
  381.4 2.8 select_reduce_fusion
  384.2 2.5 fusion.3
  386.8 2.1 fusion.19
  389.0 2.5 multiply_reduce_fusion
  391.5 3.2 fusion.1
  394.7 2.0 copy-done
  397.4 1.1 pad_maximum_fusion
  398.8 3.7 broadcast_multiply_fusion
  402.7 36.8 %reduce-scatter.5.cloned.1.call-done = bf16[256,256]{0,1:T(8,128)(2,1)} async-done(((bf16[2048,256]{0,1:T(8,128)(2,1)}), bf16[256,256]{0,1:T(8,128)(2,1)}) %reduce-scatter.5.cloned.1.call-update) | async-done | bytes 131088 | tf_op jit(solution)/shard_map/reduce_scatter | solution.py:100
  439.5 0.9 convert_element_type.54
  440.4 0.8 slice.92
  441.7 0.8 slice.94
  442.5 12.5 %convolution_bitcast_fusion = f32[8192,768]{0,1:T(8,128)} fusion(bf16[1,256,8192]{2,1,0:T(8,128)(2,1)} %param.6, bf16[256,128]{0,1:T(8,128)(2,1)S(1)} %slice.94, bf16[256,128]{0,1:T(8,128)(2,1)S(1)} %fusion.38, bf16[256,512]{0,1:T(8,128)(2,1)S(1)} %bitcast.58), kind=kOutput, calls=%fused_computation | convolution fusion | flops 3222405120 | bytes 29753344 | tf_op jit(solution)/shard_map/dot_general | solution.py:114
  455.1 24.7 %copy.38 = f32[8192,768]{1,0:T(8,128)} copy(f32[8192,768]{0,1:T(8,128)} %convolution_bitcast_fusion) | data formatting | bytes 50331648
  479.7 0.8 copy.27
  480.6 14.4 %fusion = bf16[1,256,8192]{2,1,0:T(8,128)(2,1)} fusion(bf16[8192,768]{1,0:T(8,128)(2,1)} %all-gather.3.cloned.1.call-done, bf16[256,128]{0,1:T(8,128)(2,1)S(1)} %slice.94, bf16[256,128]{0,1:T(8,128)(2,1)S(1)} %fusion.38, bf16[256,512]{0,1:T(8,128)(2,1)S(1)} %bitcast.59), kind=kOutput, calls=%fused_computation.2 | convolution fusion | flops 3224502272 | bytes 17170432 | tf_op jit(solution)/shard_map/dot_general | solution.py:110
  495.0 671.7 %reduce-scatter.7.cloned.1.call-done = f32[64,768]{1,0:T(8,128)} async-done(((f32[8192,768]{1,0:T(8,128)}), f32[64,768]{1,0:T(8,128)}) %reduce-scatter.7.cloned.1.call-update) | async-done | bytes 196624
  1166.7 1.4 fusion.52
  1168.1 1.6 slice.95
  (36 shorter events, 6.1 us)
Async XLA Ops:
  7.2 327.0 %all-gather.3.cloned.1.call-start = ((), (), s32[]{:S(2)}) async-start(), calls=%async_computation.2 | async-start | bytes 12681216 | tf_op jit(solution)/shard_map/all_gather | solution.py:41
  10.3 371.1 %all-gather.5.cloned.1.call-start = ((), (), s32[]{:S(2)}) async-start(), calls=%async_computation.3 | async-start | bytes 1179648 | tf_op jit(solution)/shard_map/all_gather | solution.py:53
  11.2 332.1 %copy-start.2 = (bf16[1,256,512]{2,1,0:T(8,128)(2,1)S(1)}, bf16[1,256,512]{2,1,0:T(8,128)(2,1)}, u32[]{:S(2)}) copy-start(bf16[1,256,512]{2,1,0:T(8,128)(2,1)} %param.11) | copy-start | bytes 786436
  11.2 332.2 %copy-start.3 = (s32[2048]{0:T(1024)S(1)}, s32[2048]{0:T(1024)}, u32[]{:S(2)}) copy-start(s32[2048]{0:T(1024)} %param.7) | copy-start | bytes 24580
  343.1 96.4 %reduce-scatter.5.cloned.1.call-start = ((), (), s32[]{:S(2)}) async-start(), calls=%async_computation.4 | async-start | bytes 1179648 | tf_op jit(solution)/shard_map/reduce_scatter | solution.py:100
  386.8 2.2 copy-start.1
  394.7 2.0 copy-start
  398.5 768.2 %reduce-scatter.7.cloned.1.call-start = ((), (), s32[]{:S(2)}) async-start(), calls=%async_computation.5 | async-start | bytes 25362432
Sparse Core Ops, SparseCore 0:
  10.4 323.6 all-gather.2
  343.2 38.1 all-gather.4
  398.6 40.7 reduce-scatter.4
  479.9 686.7 reduce-scatter.6
where the time goes:
time: 1180 us
  waiting for transfers between devices  1070 us (91%)
  matrix products  49.8 us (4%)
  local copies, waits for them, and re-layouts  32.3 us (3%)
  between operations  14 us (1%)
    unnamed x5, waiting for transfers between devices  672 us
    all_gather x1, waiting for transfers between devices, body(): lax.all_gather(local_weights, ('dp', 'ctx'), axis=0, tiled=True)  323 us
    all_gather x1, waiting for transfers between devices, body(): key_piece = lax.all_gather(key_value, 'ctx', axis=0, tiled=True)  37.3 us
    reduce_scatter x1, waiting for transfers between devices, body(): lax.psum_scatter(keyval_term.astype(jnp.bfloat16), 'ctx', scatter_dimensi...  36.8 us
    unnamed x11, local copies, waits for them, and re-layouts  27.7 us
  transfers between devices with their start and end apart: 4, of which 4 were waited for; matrix products, arithmetic and copies ran while one was open for 2% of the time, Pallas kernels for 0%

commit v1 on v0

v1 whole, which is shorter than its diff:
```python
import functools

import jax
import jax.numpy as jnp
from jax import lax
from jax.experimental import pallas as pl
from jax.experimental.pallas import tpu as pltpu
from jax.sharding import PartitionSpec as P

ROPE_BASE = 1000000.0
MASKED = -1e30
MESH = pl.DeviceIdType.MESH
BF16 = jnp.bfloat16
F32 = jnp.float32
AXES = ("x", "y", "z")
ORDERS = (("z", "y", "x"), ("x", "z", "y"), ("y", "x", "z"))


def place():
    dp, ctx = lax.axis_index("dp"), lax.axis_index("ctx")
    return {
        "x": lax.div(dp, 8) * 2 + lax.div(ctx, 4),
        "y": lax.rem(lax.div(dp, 2), 4),
        "z": lax.rem(ctx, 4),
        "core": lax.rem(dp, 2),
    }


def device(at):
    return (
        lax.div(at["x"], 2) * 8 + at["y"] * 2 + at["core"],
        lax.rem(at["x"], 2) * 4 + at["z"],
    )


def moved(at, axis, by):
    return {**at, axis: lax.rem(at[axis] + 4 + by, 4)}


def sibling(at):
    return {**at, "core": 1 - at["core"]}


def greet(targets):
    barrier = pltpu.get_barrier_semaphore()
    for target in targets:
        pl.semaphore_signal(barrier, inc=1, device_id=target, device_id_type=MESH)
    pl.semaphore_wait(barrier, len(targets))


def torus_neighbours(at):
    near = [device(moved(at, axis, by)) for axis in AXES for by in (1, -1)]
    return near + [device(sibling(at))]


def remote(src, dst, send, recv, target):
    return pltpu.make_async_remote_copy(
        src_ref=src, dst_ref=dst, send_sem=send, recv_sem=recv, device_id=target, device_id_type=MESH
    )


def gather_kernel(
    tokens, wq, wk, wv, w_all, tokens_twin,
    own, own_sem, send, recv, twin_send, twin_recv, token_send, token_recv,
):
    me = place()
    core = me["core"]
    twin = device(sibling(me))
    own[0] = wq[:, 0:256].astype(BF16)
    own[1] = wq[:, 256:512].astype(BF16)
    own[2, :, 0:128] = wk[...].astype(BF16)
    own[2, :, 128:256] = wv[...].astype(BF16)

    def block(part, where, core_at, rows=None):
        x, y, z = where.get("x"), where.get("y"), where.get("z")
        x_hi = slice(None) if x is None else lax.div(x, 2)
        x_lo = slice(None) if x is None else lax.rem(x, 2)
        y = slice(None) if y is None else y
        z = slice(None) if z is None else z
        rows = slice(None) if rows is None else pl.ds(rows * 32, 32)
        return w_all.at[part, x_hi, y, core_at, x_lo, z, rows]

    placed = []
    for part in range(3):
        copy = pltpu.make_async_copy(own.at[part], block(part, me, core), own_sem.at[part])
        copy.start()
        placed.append(copy)
    greet(torus_neighbours(me))
    started = []

    def send_to(src, dst, sems, k, target):
        copy = remote(src, dst, sems[0].at[k], sems[1].at[k], target)
        copy.start()
        started.append(copy)

    def arrival(ref, sems, k):
        remote(ref, ref, sems[0].at[k], sems[1].at[k], twin).wait_recv()

    ici = (send, recv)
    pair = (twin_send, twin_recv)
    for k in range(8):
        columns = tokens.at[:, pl.ds(pl.multiple_of(k * 1024 + (1 - core) * 512, 512), 512)]
        send_to(columns, tokens_twin.at[:, pl.ds(k * 512, 512)], (token_send, token_recv), k, twin)
    for copy in placed:
        copy.wait()

    def where_of(part, phase, index):
        order = ORDERS[part]
        where = {axis: me[axis] for axis in order[phase:]}
        where[order[phase]] = index
        return where

    for phase in range(3):
        for part in range(3):
            axis = ORDERS[part][phase]
            mine = block(part, where_of(part, phase, me[axis]), core)
            for d, by in enumerate((1, -1)):
                send_to(mine, mine, ici, (part * 3 + phase) * 4 + d, device(moved(me, axis, by)))
            if phase == 2:
                send_to(mine, mine, pair, part * 5, twin)
        for part in range(3):
            axis = ORDERS[part][phase]
            for d, by in enumerate((1, -1)):
                source = moved(me, axis, -by)[axis]
                where = where_of(part, phase, source)
                arrival(block(part, where, core), ici, (part * 3 + phase) * 4 + d)
                half = block(part, where, core, d)
                send_to(half, half, ici, (part * 3 + phase) * 4 + 2 + d, device(moved(me, axis, by)))
                if phase == 2:
                    whole = block(part, where, core)
                    send_to(whole, whole, pair, part * 5 + 1 + d, twin)
        for part in range(3):
            axis = ORDERS[part][phase]
            far = where_of(part, phase, moved(me, axis, 2)[axis])
            for d in range(2):
                half = block(part, far, core, d)
                arrival(half, ici, (part * 3 + phase) * 4 + 2 + d)
                if phase == 2:
                    send_to(half, half, pair, part * 5 + 3 + d, twin)
    for part in range(3):
        axis = ORDERS[part][2]
        for k in range(5):
            shift = (0, -1, 1, 2, 2)[k]
            where = where_of(part, 2, moved(me, axis, shift)[axis])
            arrival(block(part, where, 1 - core, None if k < 3 else k - 3), pair, part * 5 + k)
    for k in range(8):
        arrival(tokens_twin.at[:, pl.ds(k * 512, 512)], (token_send, token_recv), k)
    for copy in started:
        copy.wait_send()


def gather_weights(tokens, wq, wk, wv):
    vmem, anywhere = pl.BlockSpec(memory_space=pltpu.VMEM), pl.BlockSpec(memory_space=pl.ANY)
    w_all, tokens_twin = pl.pallas_call(
        gather_kernel,
        out_shape=(
            jax.ShapeDtypeStruct((3, 2, 4, 2, 2, 4, 64, 256), BF16),
            jax.ShapeDtypeStruct((256, 4096), BF16),
        ),
        in_specs=[anywhere, vmem, vmem, vmem],
        out_specs=(anywhere, anywhere),
        scratch_shapes=[
            pltpu.VMEM((3, 64, 256), BF16),
            pltpu.SemaphoreType.DMA((3,)),
            pltpu.SemaphoreType.DMA((36,)),
            pltpu.SemaphoreType.DMA((36,)),
            pltpu.SemaphoreType.DMA((15,)),
            pltpu.SemaphoreType.DMA((15,)),
            pltpu.SemaphoreType.DMA((8,)),
            pltpu.SemaphoreType.DMA((8,)),
        ],
        compiler_params=pltpu.CompilerParams(
            collective_id=0, has_side_effects=True, vmem_limit_bytes=16 * 2**20
        ),
        name="gather_weights",
    )(tokens, wq, wk, wv)
    return w_all.reshape(3, 8192, 256), tokens_twin


def ctx_peers():
    dp, ctx = lax.axis_index("dp"), lax.axis_index("ctx")
    return [(dp, lax.rem(ctx + k, 8)) for k in range(1, 8)]


def gather_kv_kernel(kv, kv_all, local_sem, send, recv):
    ctx = lax.axis_index("ctx")
    peers = ctx_peers()
    greet(peers)
    copies = []
    for k in (4, 2, 6, 1, 3, 5, 7):
        copy = remote(kv, kv_all.at[ctx], send.at[k - 1], recv.at[k - 1], peers[k - 1])
        copy.start()
        copies.append(copy)
    keep = pltpu.make_async_copy(kv, kv_all.at[ctx], local_sem.at[0])
    keep.start()
    keep.wait()
    for k in range(1, 8):
        source = lax.rem(ctx + 8 - k, 8)
        remote(kv, kv_all.at[source], send.at[k - 1], recv.at[k - 1], peers[k - 1]).wait_recv()
    for copy in copies:
        copy.wait_send()


def gather_kv(kv):
    vmem = pl.BlockSpec(memory_space=pltpu.VMEM)
    out = pl.pallas_call(
        gather_kv_kernel,
        out_shape=jax.ShapeDtypeStruct((8, 256, 256), BF16),
        in_specs=[vmem],
        out_specs=vmem,
        scratch_shapes=[
            pltpu.SemaphoreType.DMA((1,)),
            pltpu.SemaphoreType.DMA((7,)),
            pltpu.SemaphoreType.DMA((7,)),
        ],
        compiler_params=pltpu.CompilerParams(
            collective_id=1, has_side_effects=True, vmem_limit_bytes=16 * 2**20
        ),
        name="gather_kv",
    )(kv)
    return out.reshape(2048, 256)


def scatter_kv_kernel(terms, out, landed, send, recv):
    ctx = lax.axis_index("ctx")
    peers = ctx_peers()
    greet(peers)
    copies = []
    for k in (4, 2, 6, 1, 3, 5, 7):
        to = lax.rem(ctx + k, 8)
        copy = remote(terms.at[to], landed.at[k - 1], send.at[k - 1], recv.at[k - 1], peers[k - 1])
        copy.start()
        copies.append(copy)
    out[...] = terms[ctx].astype(F32)
    for copy in copies:
        copy.wait_recv()
    for k in range(7):
        out[...] += landed[k].astype(F32)
    for copy in copies:
        copy.wait_send()


def scatter_kv(terms):
    vmem = pl.BlockSpec(memory_space=pltpu.VMEM)
    return pl.pallas_call(
        scatter_kv_kernel,
        out_shape=jax.ShapeDtypeStruct((256, 256), F32),
        in_specs=[vmem],
        out_specs=vmem,
        scratch_shapes=[
            pltpu.VMEM((7, 256, 256), BF16),
            pltpu.SemaphoreType.DMA((7,)),
            pltpu.SemaphoreType.DMA((7,)),
        ],
        compiler_params=pltpu.CompilerParams(
            collective_id=2, has_side_effects=True, vmem_limit_bytes=16 * 2**20
        ),
        name="scatter_kv",
    )(terms.reshape(8, 256, 256))


def scatter_kernel(
    tokens, tokens_twin, grad_proj, out,
    held, grads, acc1, acc2, acc3, via1, via2, via3, end1, end2, end3,
    load_sem, twin_sem, send, recv,
):
    me = place()
    core = me["core"]
    twin = device(sibling(me))
    greet(torus_neighbours(me))
    swap = remote(grad_proj, grads.at[1], twin_sem.at[0], twin_sem.at[1], twin)
    swap.start()
    loads = []
    for k in range(8):
        columns = tokens.at[:, pl.ds(pl.multiple_of(k * 1024 + core * 512, 512), 512)]
        loads.append(pltpu.make_async_copy(columns, held.at[k, pl.ds(0, 256)], load_sem.at[2 * k]))
        columns = tokens_twin.at[:, pl.ds(k * 512, 512)]
        loads.append(pltpu.make_async_copy(columns, held.at[k, pl.ds(256, 256)], load_sem.at[2 * k + 1]))
    for copy in loads:
        copy.start()
    grads[0] = grad_proj[...]
    for copy in loads:
        copy.wait()
    swap.wait_recv()

    def product(k, _):
        x_hi, y = lax.div(k, 4), lax.rem(k, 4)
        for x_lo in range(2):
            lhs = held[k, :, x_lo * 256 : x_lo * 256 + 256]
            x = x_hi * 2 + x_lo
            for part in range(3):
                cols = slice(part * 256, part * 256 + 256)
                rhs = grads[:, :, cols].reshape(512, 256)
                term = lax.dot_general(lhs, rhs, (((0,), (0,)), ((), ())), preferred_element_type=F32)
                term = term.astype(BF16).reshape(4, 2, 32, 256)
                for z in range(4):
                    at = {"x": x, "y": y, "z": z}
                    first, second, third = (at[axis] for axis in reversed(ORDERS[part]))
                    for half in range(2):
                        acc1[part, first, half, second, third] = term[z, half]
        return 0

    lax.fori_loop(0, 8, product, 0)

    started = []

    def launch(src, dst, k, target):
        copy = remote(src, dst, send.at[k], recv.at[k], target)
        copy.start()
        started.append(copy)

    def arrival(ref, k):
        remote(ref, ref, send.at[k], recv.at[k], twin).wait_recv()

    accs, vias, ends = (acc1, acc2, acc3), (via1, via2, via3), (end1, end2, end3)

    def add_into(dst, src):
        def one(r, _):
            dst[r] = (dst[r].astype(F32) + src[r].astype(F32)).astype(BF16)
            return 0

        lax.fori_loop(0, dst.shape[0], one, 0)

    for phase in range(3):
        acc, via, end = accs[phase], vias[phase], ends[phase]
        for part in range(3):
            axis = ORDERS[part][2 - phase]
            base = (part * 3 + phase) * 6
            for d, by in enumerate((1, -1)):
                near, far = moved(me, axis, by), moved(me, axis, 2)
                launch(acc.at[part, far[axis], d], via.at[part, d], base + d, device(near))
            for d, by in enumerate((1, -1)):
                near = moved(me, axis, by)
                launch(acc.at[part, near[axis], 1 - d], end.at[part, d, 1 - d], base + 2 + d, device(near))
        for part in range(3):
            axis = ORDERS[part][2 - phase]
            base = (part * 3 + phase) * 6
            for d, by in enumerate((1, -1)):
                near = moved(me, axis, by)
                arrival(via.at[part, d], base + d)
                if phase == 0:
                    for j in range(4):
                        add_into(acc.at[part, near[axis], d, j], via.at[part, d, j])
                elif phase == 1:
                    add_into(acc.at[part, near[axis], d], via.at[part, d])
                else:
                    total = acc[part, near[axis], d].astype(F32) + via[part, d].astype(F32)
                    acc[part, near[axis], d] = total.astype(BF16)
                launch(acc.at[part, near[axis], d], end.at[part, d, d], base + 4 + d, device(near))
        for part in range(3):
            axis = ORDERS[part][2 - phase]
            base = (part * 3 + phase) * 6
            mine = me[axis]
            for half in range(2):
                arrival(end.at[part, 1 - half, half], base + 2 + (1 - half))
                arrival(end.at[part, half, half], base + 4 + half)

                def total(*index):
                    at = (half, *index)
                    return (
                        acc[(part, mine, *at)].astype(F32)
                        + end[(part, 0, *at)].astype(F32)
                        + end[(part, 1, *at)].astype(F32)
                    )

                if phase == 0:
                    for j in range(4):

                        def one(r, _):
                            acc2[part, j, half, r] = total(j, r).astype(BF16)
                            return 0

                        lax.fori_loop(0, 4, one, 0)
                elif phase == 1:
                    for j in range(4):
                        acc3[part, j, half] = total(j).astype(BF16)
                else:
                    out[half * 32 : half * 32 + 32, part * 256 : part * 256 + 256] = total()
    for copy in started:
        copy.wait_send()
    swap.wait_send()


def scatter_grads(tokens, tokens_twin, grad_proj):
    vmem, anywhere = pl.BlockSpec(memory_space=pltpu.VMEM), pl.BlockSpec(memory_space=pl.ANY)
    tile = (32, 256)
    return pl.pallas_call(
        scatter_kernel,
        out_shape=jax.ShapeDtypeStruct((64, 768), F32),
        in_specs=[anywhere, anywhere, vmem],
        out_specs=vmem,
        scratch_shapes=[
            pltpu.VMEM((8, 512, 512), BF16),
            pltpu.VMEM((2, 256, 768), BF16),
            pltpu.VMEM((3, 4, 2, 4, 4) + tile, BF16),
            pltpu.VMEM((3, 4, 2, 4) + tile, BF16),
            pltpu.VMEM((3, 4, 2) + tile, BF16),
            pltpu.VMEM((3, 2, 4, 4) + tile, BF16),
            pltpu.VMEM((3, 2, 4) + tile, BF16),
            pltpu.VMEM((3, 2) + tile, BF16),
            pltpu.VMEM((3, 2, 2, 4, 4) + tile, BF16),
            pltpu.VMEM((3, 2, 2, 4) + tile, BF16),
            pltpu.VMEM((3, 2, 2) + tile, BF16),
            pltpu.SemaphoreType.DMA((16,)),
            pltpu.SemaphoreType.DMA((2,)),
            pltpu.SemaphoreType.DMA((54,)),
            pltpu.SemaphoreType.DMA((54,)),
        ],
        compiler_params=pltpu.CompilerParams(
            collective_id=3, has_side_effects=True, vmem_limit_bytes=40 * 2**20
        ),
        name="scatter_grads",
    )(tokens, tokens_twin, grad_proj)


def rope_tables(positions_in, head_dim):
    half_width = head_dim // 2
    exponent = jnp.arange(half_width).astype(jnp.float32) * (2.0 / head_dim)
    frequency = jnp.power(ROPE_BASE, -exponent)
    angles = positions_in.astype(jnp.float32)[:, None] * frequency[None, :]
    angles = jnp.concatenate([angles, angles], axis=1)
    return (jnp.cos(angles), jnp.sin(angles))


def rotate(field, cos_table, sin_table):
    half_width = field.shape[-1] // 2
    turned = jnp.concatenate([-field[..., half_width:], field[..., :half_width]], axis=-1)
    return field * cos_table + turned * sin_table


def unrotate(field, cos_table, sin_table):
    half_width = field.shape[-1] // 2
    turned = jnp.concatenate([field[..., half_width:], -field[..., :half_width]], axis=-1)
    return field * cos_table + turned * sin_table


def body(tokens, positions, query_weight, key_weight, value_weight, grad_output):
    token_rows = tokens[0]
    local_rows = token_rows.shape[0]
    head_dim = key_weight.shape[1]
    query_width = query_weight.shape[1]
    head_count = query_width // head_dim
    score_scale = head_dim ** (-0.5)
    w_all, tokens_twin = gather_weights(token_rows, query_weight, key_weight, value_weight)
    projected = jnp.concatenate(
        [jnp.dot(token_rows, w_all[k], preferred_element_type=jnp.float32) for k in range(3)], axis=1
    )
    place_index = lax.axis_index("ctx")
    own_positions = lax.dynamic_slice_in_dim(positions, place_index * local_rows, local_rows)
    cos_table, sin_table = rope_tables(own_positions, head_dim)
    query = projected[:, :query_width].reshape(local_rows, head_count, head_dim)
    query_heads = rotate(query, cos_table[:, None, :], sin_table[:, None, :]).astype(jnp.bfloat16)
    key_rot = rotate(
        projected[:, query_width : query_width + head_dim], cos_table, sin_table
    ).astype(jnp.bfloat16)
    value_b = projected[:, query_width + head_dim :].astype(jnp.bfloat16)
    key_value = jnp.concatenate([key_rot, value_b], axis=1)
    keys_values = gather_kv(key_value)
    key_all = keys_values[:, :head_dim]
    value_all = keys_values[:, head_dim:]
    allowed = positions[None, :] <= own_positions[:, None]
    scores = (
        jnp.einsum("qhd,kd->qhk", query_heads, key_all, preferred_element_type=jnp.float32)
        * score_scale
    )
    scores = jnp.where(allowed[:, None, :], scores, MASKED)
    row_max = jnp.max(scores, axis=-1)
    weight = jnp.where(allowed[:, None, :], jnp.exp(scores - row_max[..., None]), 0.0)
    denominator = jnp.sum(weight, axis=-1)
    weighted = jnp.einsum(
        "qhk,kd->qhd", weight.astype(jnp.bfloat16), value_all, preferred_element_type=jnp.float32
    )
    log_total = row_max + jnp.log(denominator)
    attention = (weighted / denominator[..., None]).astype(jnp.bfloat16)
    grad_heads = grad_output[0].reshape(local_rows, head_count, head_dim)
    row_delta = jnp.sum(grad_heads.astype(jnp.float32) * attention.astype(jnp.float32), axis=-1)
    probs = jnp.where(allowed[:, None, :], jnp.exp(scores - log_total[..., None]), 0.0)
    grad_probs = jnp.einsum(
        "qhd,kd->qhk", grad_heads, value_all, preferred_element_type=jnp.float32
    )
    dscore = (probs * (grad_probs - row_delta[..., None])).astype(jnp.bfloat16)
    probs_b = probs.astype(jnp.bfloat16)
    grad_query_rot = (
        jnp.einsum("qhk,kd->qhd", dscore, key_all, preferred_element_type=jnp.float32) * score_scale
    )
    key_term = (
        jnp.einsum("qhk,qhd->kd", dscore, query_heads, preferred_element_type=jnp.float32)
        * score_scale
    )
    value_term = jnp.einsum("qhk,qhd->kd", probs_b, grad_heads, preferred_element_type=jnp.float32)
    keyval_term = jnp.concatenate([key_term, value_term], axis=1)
    keyval_grad = scatter_kv(keyval_term.astype(jnp.bfloat16))
    grad_query = unrotate(grad_query_rot, cos_table[:, None, :], sin_table[:, None, :]).reshape(
        local_rows, query_width
    )
    grad_key = unrotate(keyval_grad[:, :head_dim], cos_table, sin_table)
    grad_proj = jnp.concatenate([grad_query, grad_key, keyval_grad[:, head_dim:]], axis=1).astype(
        jnp.bfloat16
    )
    weight_grads = scatter_grads(token_rows, tokens_twin, grad_proj)
    grad_input = sum(
        lax.dot_general(
            grad_proj[:, k * 256 : k * 256 + 256],
            w_all[k],
            (((1,), (1,)), ((), ())),
            preferred_element_type=jnp.float32,
        )
        for k in range(3)
    ).astype(jnp.bfloat16)
    query_grad = weight_grads[:, :query_width]
    key_grad = weight_grads[:, query_width : query_width + head_dim]
    value_grad = weight_grads[:, query_width + head_dim :]
    attention_rows = attention.reshape(local_rows, query_width)
    return (attention_rows[None], grad_input[None], query_grad, key_grad, value_grad)


def solution(mesh):
    in_specs = (
        P("dp", "ctx", None),
        P(),
        P(("dp", "ctx"), None),
        P(("dp", "ctx"), None),
        P(("dp", "ctx"), None),
        P("dp", "ctx", None),
    )
    out_specs = (
        P("dp", "ctx", None),
        P("dp", "ctx", None),
        P(("dp", "ctx"), None),
        P(("dp", "ctx"), None),
        P(("dp", "ctx"), None),
    )
    return jax.shard_map(body, mesh=mesh, in_specs=in_specs, out_specs=out_specs, check_vma=False)
```

time: 1180 us -> 191 us (0.16)
  waiting for transfers between devices: 1070 us -> 0 us
  Pallas kernels: 0 us -> 123 us
  matrix products: 49.8 us -> 34.6 us
  local copies, waits for them, and re-layouts: 32.3 us -> 18.3 us
  between operations: 14 us -> 0.97 us
    unnamed x5 -> x0, waiting for transfers between devices: 672 us -> none
    all_gather x2 -> x0, waiting for transfers between devices: 360 us -> none  [the longest x1 323 us: body(): lax.all_gather(local_weights, ('dp', 'ctx'), axis=0, tiled=True)]
    pallas_call x0 -> x4, Pallas kernels: none -> 123 us  [the longest x1 45.4 us: scatter_grads(): pl.pallas_call(scatter_kernel, out_shape=jax.ShapeDtypeStruct((64, 768),...]
    reduce_scatter x1 -> x0, waiting for transfers between devices: 36.8 us -> none  [body(): lax.psum_scatter(keyval_term.astype(jnp.bfloat16), 'ctx', scatter_dimensi...]
    dot_general x5 -> x8, matrix products: 40 us -> 23.8 us  [the longest x3 8.93 us: body(): jnp.dot(token_rows, w_all[k], preferred_element_type=jnp.float32)]
    unnamed x11 -> x40, local copies, waits for them, and re-layouts: 27.7 us -> 12.3 us
  transfers between devices with their start and end apart: 4 -> 0, of which waited for: 4 -> 0; matrix products, arithmetic and copies ran while one was open for 2% -> 0% of each run, Pallas kernels for 0% -> 0%
where the time goes in v1:
time: 191 us; the launch traced here: 190 us
  Pallas kernels  123 us (64%)
  matrix products  34.6 us (18%)
  local copies, waits for them, and re-layouts  18.3 us (10%)
  other arithmetic  13.8 us (7%)
    pallas_call x1, Pallas kernels, scatter_grads(): pl.pallas_call(scatter_kernel, out_shape=jax.ShapeDtypeStruct((64, 768),...  45.4 us
    pallas_call x1, Pallas kernels, gather_weights(): pl.pallas_call(gather_kernel, out_shape=(jax.ShapeDtypeStruct((3, 2, 4, 2...  45.1 us
    pallas_call x1, Pallas kernels, gather_kv(): pl.pallas_call(gather_kv_kernel, out_shape=jax.ShapeDtypeStruct((8, 256,...  16.3 us
    pallas_call x1, Pallas kernels, scatter_kv(): pl.pallas_call(scatter_kv_kernel, out_shape=jax.ShapeDtypeStruct((256, 25...  16 us
    unnamed x40, local copies, waits for them, and re-layouts  12.3 us
    dot_general x3, matrix products, body(): jnp.dot(token_rows, w_all[k], preferred_element_type=jnp.float32)  8.93 us
    dot_general x3, matrix products, body(): lax.dot_general(grad_proj[:, k * 256:k * 256 + 256], w_all[k], (((1,), (1...  8.56 us
    dot_general x1, matrix products, body(): jnp.einsum('qhd,kd->qhk', grad_heads, value_all, preferred_element_type=j...  5.83 us

profile of v1, /device:TPU:0, one launch (start us, length us, event | category | flops | bytes accessed | tf_op | source)
XLA Modules:
  0.0 190.4 jit_solution(7014729607904895572)
XLA Ops:
  1.4 1.8 copy.16
  3.2 1.8 broadcast_compare_fusion.1
  5.0 1.9 broadcast_compare_fusion
  6.9 2.2 %copy-done = bf16[1,256,8192]{2,1,0:T(8,128)(2,1)S(1)} copy-done((bf16[1,256,8192]{2,1,0:T(8,128)(2,1)S(1)}, bf16[1,256,8192]{2,1,0:T(8,128)(2,1)}, u32[]{:S(2)}) %copy-start) | copy-done | bytes 4194328
  11.5 45.1 %gather_weights.1 = (bf16[3,2,4,2,2,4,64,256]{7,6,5,4,3,2,1,0:T(8,128)(2,1)S(1)}, bf16[256,4096]{1,0:T(8,128)(2,1)S(1)}) custom-call(bf16[256,8192]{1,0:T(8,128)(2,1)S(1)} %bitcast.87, f32[64,512]{1,0:T(8,128)S(1)} %copy-done.3, f32[64,128]{1,0:T(8,128)S(1)} %copy-done.4, f32[64,128]{1,0:T(8,128)S(1)} %copy-done.5), custom_call_target="tpu_custom_call" | custom-call | tf_op jit(solution)/shard_map/gather_weights/pallas_call | solution.py:154
  56.6 3.6 %fusion.56 = (bf16[1,2,4,2,2,4,64,256]{7,6,5,4,3,2,1,0:T(8,128)(2,1)}, bf16[1,2,4,2,2,4,64,256]{7,6,5,4,3,2,1,0:T(8,128)(2,1)S(1)}, bf16[1,2,4,2,2,4,64,256]{7,6,5,4,3,2,1,0:T(8,128)(2,1)S(1)}) fusion(bf16[3,2,4,2,2,4,64,256]{7,6,5,4,3,2,1,0:T(8,128)(2,1)S(1)} %get-tuple-element.7), kind=kLoop, calls=%fused_computation.83 | loop fusion | bytes 25165824 | tf_op jit(solution)/shard_map/slice | solution.py:446
  60.3 6.3 %convolution_bitcast_fusion.1 = f32[256,256]{1,0:T(8,128)S(1)} fusion(bf16[8192,256]{1,0:T(8,128)(2,1)} %bitcast.97, bf16[1,256,8192]{2,1,0:T(8,128)(2,1)S(1)} %copy-done.1), kind=kOutput, calls=%fused_computation.26 | convolution fusion | flops 1073741824 | bytes 8650752 | tf_op jit(solution)/shard_map/dot_general | solution.py:446
  66.6 1.3 convolution_bitcast_fusion.2
  67.9 1.3 convolution_bitcast_fusion.3
  72.0 16.3 %gather_kv.1 = bf16[8,256,256]{2,1,0:T(8,128)(2,1)S(1)} custom-call(bf16[256,256]{1,0:T(8,128)(2,1)S(1)} %pad_maximum_fusion.4.kv), custom_call_target="tpu_custom_call" | custom-call | tf_op jit(solution)/shard_map/gather_kv/pallas_call | solution.py:206
  88.3 3.1 %fusion.9 = (f32[256,4]{0,1:T(4,128)S(1)}, f32[256,4,2048]{2,0,1:T(8,128)S(1)}) fusion(pred[256,2048]{1,0:T(8,128)(4,1)} %broadcast_compare_fusion.1, bf16[256,4,128]{0,2,1:T(8,128)(2,1)S(1)} %fusion.31, bf16[2048,256]{1,0:T(8,128)(2,1)S(1)} %bitcast.89), kind=kOutput, calls=%fused_computation.15 | convolution fusion | flops 543161344 | bytes 9703424 | tf_op jit(solution)/shard_map/qhd,kd->qhk/dot_general | solution.py:463
  91.4 2.5 %fusion.7 = f32[256,4]{0,1:T(4,128)S(1)} fusion(f32[256,4,2048]{2,0,1:T(8,128)S(1)} %get-tuple-element.35, f32[256,4]{0,1:T(4,128)S(1)} %get-tuple-element.34, pred[256,2048]{1,0:T(8,128)(4,1)S(1)} %copy-done.12), kind=kLoop, calls=%fused_computation.13 | loop fusion | flops 10484736 | bytes 8921088 | tf_op jit(solution)/shard_map/reduce_sum | solution.py:469
  94.6 3.3 %multiply_reduce_fusion = (f32[256,4]{0,1:T(4,128)S(1)}, bf16[256,4,128]{0,2,1:T(8,128)(2,1)}) fusion(bf16[256,4,128]{0,2,1:T(8,128)(2,1)S(1)} %bitcast.105, f32[256,4]{0,1:T(4,128)S(1)} %fusion.7, bf16[2048,256]{1,0:T(8,128)(2,1)S(1)} %bitcast.90, f32[256,4,2048]{2,0,1:T(8,128)S(1)} %get-tuple-element.35, f32[256,4]{0,1:T(4,128)S(1)} %get-tuple-element.34, ...), kind=kOutput, calls=%fused_computation.43 | convolution fusion | flops 548142080 | bytes 9973760 | tf_op jit(solution)/shard_map/qhk,kd->qhd/dot_general | solution.py:470
  97.9 1.8 copy.26
  99.7 5.8 %fusion.6 = bf16[256,4,2048]{2,0,1:T(8,128)(2,1)S(1)} fusion(f32[256,4,2048]{2,0,1:T(8,128)} %copy-done.6, bf16[256,4,128]{0,2,1:T(8,128)(2,1)} %bitcast.104, f32[256,4]{0,1:T(4,128)S(1)} %get-tuple-element.36, f32[256,4]{0,1:T(4,128)S(1)} %log_add_fusion, pred[256,2048]{1,0:T(8,128)(4,1)} %broadcast_compare_fusion.1, bf16[2048,256]{1,0:T(8,128)(2,1)S(1)} %bitcast.91), kind=kOutput, calls=%fused_computation.10 | convolution fusion | flops 551550976 | bytes 13901824 | tf_op jit(solution)/shard_map/qhd,kd->qhk/dot_general | solution.py:478
  105.8 2.4 %fusion.5 = bf16[2048,4,256]{0,2,1:T(8,128)(2,1)S(1)} fusion(f32[256,4,2048]{2,0,1:T(8,128)S(1)} %copy-done.7, f32[4,256]{1,0:T(4,128)S(1)} %bitcast.108, pred[2048,256]{0,1:T(8,128)(4,1)S(1)} %copy-done.13), kind=kLoop, calls=%fused_computation.8 | loop fusion | flops 10485760 | bytes 13111296 | tf_op jit(solution)/shard_map/convert_element_type | solution.py:482
  108.2 1.3 fusion.21
  109.5 2.3 %broadcast_multiply_fusion = (f32[256,4,128]{0,2,1:T(8,128)S(1)}, f32[256,4,128]{0,2,1:T(8,128)}) fusion(bf16[256,4,2048]{2,0,1:T(8,128)(2,1)S(1)} %fusion.6, bf16[2048,256]{1,0:T(8,128)(2,1)S(1)} %bitcast.92), kind=kOutput, calls=%fused_computation.49 | convolution fusion | flops 537001984 | bytes 5767168 | tf_op jit(solution)/shard_map/qhk,kd->qhd/dot_general | solution.py:484
  111.8 1.3 fusion.17
  113.3 16.0 %scatter_kv.1 = f32[256,256]{1,0:T(8,128)S(1)} custom-call(bf16[8,256,256]{2,1,0:T(8,128)(2,1)S(1)} %pad_maximum_fusion.terms), custom_call_target="tpu_custom_call" | custom-call | tf_op jit(solution)/shard_map/scatter_kv/pallas_call | solution.py:245
  132.1 2.2 %copy-done.2 = bf16[1,256,8192]{2,1,0:T(8,128)(2,1)S(1)} copy-done((bf16[1,256,8192]{2,1,0:T(8,128)(2,1)S(1)}, bf16[1,256,8192]{2,1,0:T(8,128)(2,1)}, u32[]{:S(2)}) %copy-start.2) | copy-done | bytes 4194328
  134.3 45.4 %scatter_grads.1 = f32[64,768]{1,0:T(8,128)S(1)} custom-call(bf16[256,8192]{1,0:T(8,128)(2,1)S(1)} %bitcast.88, bf16[256,4096]{1,0:T(8,128)(2,1)S(1)} %get-tuple-element.8.tokens_twin, bf16[256,768]{1,0:T(8,128)(2,1)S(1)} %pad_maximum_fusion.2.grad_proj), custom_call_target="tpu_custom_call" | custom-call | tf_op jit(solution)/shard_map/scatter_grads/pallas_call | solution.py:387
  183.1 1.6 convolution_add_fusion.1
  184.7 5.7 %fusion.1 = bf16[1,256,8192]{2,1,0:T(8,128)(2,1)} fusion(f32[256,8192]{1,0:T(8,128)S(1)} %convolution_add_fusion.1, bf16[8192,256]{1,0:T(8,128)(2,1)} %bitcast.98, bf16[256,128]{1,0:T(8,128)(2,1)S(1)} %slice.139, bf16[256,128]{1,0:T(8,128)(2,1)S(1)} %get-tuple-element.29), kind=kOutput, calls=%fused_computation.3 | convolution fusion | flops 1078198272 | bytes 16908288 | tf_op jit(solution)/shard_map/dot_general | solution.py:502
  (60 shorter events, 13.2 us)
Async XLA Ops:
  6.9 2.2 %copy-start = (bf16[1,256,8192]{2,1,0:T(8,128)(2,1)S(1)}, bf16[1,256,8192]{2,1,0:T(8,128)(2,1)}, u32[]{:S(2)}) copy-start(bf16[1,256,8192]{2,1,0:T(8,128)(2,1)} %param.6) | copy-start | bytes 12582916
  9.1 0.9 copy-start.3
  10.0 0.8 copy-start.4
  10.8 0.8 copy-start.5
  56.6 3.6 %copy-start.1 = (bf16[1,256,8192]{2,1,0:T(8,128)(2,1)S(1)}, bf16[1,256,8192]{2,1,0:T(8,128)(2,1)}, u32[]{:S(2)}) copy-start(bf16[1,256,8192]{2,1,0:T(8,128)(2,1)} %param.6) | copy-start | bytes 12582916
  60.2 6.4 %copy-start.8 = (bf16[1,2,4,2,2,4,64,256]{7,6,5,4,3,2,1,0:T(8,128)(2,1)}, bf16[1,2,4,2,2,4,64,256]{7,6,5,4,3,2,1,0:T(8,128)(2,1)S(1)}, u32[]{:S(2)}) copy-start(bf16[1,2,4,2,2,4,64,256]{7,6,5,4,3,2,1,0:T(8,128)(2,1)S(1)} %get-tuple-element.17) | copy-start | bytes 12582916
  60.2 7.7 %copy-start.10 = (bf16[1,2,4,2,2,4,64,256]{7,6,5,4,3,2,1,0:T(8,128)(2,1)}, bf16[1,2,4,2,2,4,64,256]{7,6,5,4,3,2,1,0:T(8,128)(2,1)S(1)}, u32[]{:S(2)}) copy-start(bf16[1,2,4,2,2,4,64,256]{7,6,5,4,3,2,1,0:T(8,128)(2,1)S(1)} %get-tuple-element.18) | copy-start | bytes 12582916
  71.9 19.4 %copy-start.15 = (bf16[256,4,128]{0,2,1:T(8,128)(2,1)}, bf16[256,4,128]{0,2,1:T(8,128)(2,1)S(1)}, u32[]{:S(2)}) copy-start(bf16[256,4,128]{0,2,1:T(8,128)(2,1)S(1)} %fusion.31) | copy-start | bytes 786436
  88.2 3.1 %copy-start.12 = (pred[256,2048]{1,0:T(8,128)(4,1)S(1)}, pred[256,2048]{1,0:T(8,128)(4,1)}, u32[]{:S(2)}) copy-start(pred[256,2048]{1,0:T(8,128)(4,1)} %broadcast_compare_fusion.1) | copy-start | bytes 1572868
  91.3 3.3 %copy-start.6 = (f32[256,4,2048]{2,0,1:T(8,128)}, f32[256,4,2048]{2,0,1:T(8,128)S(1)}, u32[]{:S(2)}) copy-start(f32[256,4,2048]{2,0,1:T(8,128)S(1)} %get-tuple-element.35) | copy-start | bytes 25165828
  91.4 3.2 %copy-start.17 = (bf16[1,256,512]{1,2,0:T(8,128)(2,1)S(1)}, bf16[1,256,512]{1,2,0:T(8,128)(2,1)}, u32[]{:S(2)}) copy-start(bf16[1,256,512]{1,2,0:T(8,128)(2,1)} %copy.16) | copy-start | bytes 786436
  99.7 6.1 %copy-start.7 = (f32[256,4,2048]{2,0,1:T(8,128)S(1)}, f32[256,4,2048]{2,0,1:T(8,128)}, u32[]{:S(2)}) copy-start(f32[256,4,2048]{2,0,1:T(8,128)} %copy-done.6) | copy-start | bytes 25165828
  99.7 6.1 %copy-start.13 = (pred[2048,256]{0,1:T(8,128)(4,1)S(1)}, pred[2048,256]{0,1:T(8,128)(4,1)}, u32[]{:S(2)}) copy-start(pred[2048,256]{0,1:T(8,128)(4,1)} %broadcast_compare_fusion) | copy-start | bytes 1572868
  105.8 2.4 %copy-start.18 = (bf16[1,256,512]{1,2,0:T(8,128)(2,1)S(1)}, bf16[1,256,512]{1,2,0:T(8,128)(2,1)}, u32[]{:S(2)}) copy-start(bf16[1,256,512]{1,2,0:T(8,128)(2,1)} %copy.16) | copy-start | bytes 786436
  109.5 2.3 %copy-start.16 = (bf16[256,4,128]{0,2,1:T(8,128)(2,1)S(1)}, bf16[256,4,128]{0,2,1:T(8,128)(2,1)}, u32[]{:S(2)}) copy-start(bf16[256,4,128]{0,2,1:T(8,128)(2,1)} %copy-done.15) | copy-start | bytes 786436
  113.2 17.7 %copy-start.14 = (f32[256,4,128]{0,2,1:T(8,128)S(1)}, f32[256,4,128]{0,2,1:T(8,128)}, u32[]{:S(2)}) copy-start(f32[256,4,128]{0,2,1:T(8,128)} %get-tuple-element.39) | copy-start | bytes 1572868
  132.1 2.2 %copy-start.2 = (bf16[1,256,8192]{2,1,0:T(8,128)(2,1)S(1)}, bf16[1,256,8192]{2,1,0:T(8,128)(2,1)}, u32[]{:S(2)}) copy-start(bf16[1,256,8192]{2,1,0:T(8,128)(2,1)} %param.6) | copy-start | bytes 12582916
  134.3 46.7 %copy-start.11 = (bf16[1,2,4,2,2,4,64,256]{7,6,5,4,3,2,1,0:T(8,128)(2,1)S(1)}, bf16[1,2,4,2,2,4,64,256]{7,6,5,4,3,2,1,0:T(8,128)(2,1)}, u32[]{:S(2)}) copy-start(bf16[1,2,4,2,2,4,64,256]{7,6,5,4,3,2,1,0:T(8,128)(2,1)} %copy-done.10) | copy-start | bytes 12582916
  180.9 2.2 %copy-start.9 = (bf16[1,2,4,2,2,4,64,256]{7,6,5,4,3,2,1,0:T(8,128)(2,1)S(1)}, bf16[1,2,4,2,2,4,64,256]{7,6,5,4,3,2,1,0:T(8,128)(2,1)}, u32[]{:S(2)}) copy-start(bf16[1,2,4,2,2,4,64,256]{7,6,5,4,3,2,1,0:T(8,128)(2,1)} %copy-done.8) | copy-start | bytes 12582916

commit v2 on v0

v2 whole, which is shorter than its diff:
```python
import functools

import jax
import jax.numpy as jnp
from jax import lax
from jax.experimental import pallas as pl
from jax.experimental.pallas import tpu as pltpu
from jax.sharding import PartitionSpec as P

ROPE_BASE = 1000000.0
MASKED = -1e30
MESH = pl.DeviceIdType.MESH
BF16 = jnp.bfloat16
F32 = jnp.float32
AXES = ("x", "y", "z")
PIECES = (
    (2, 0, 64, 0, 128, ("y", "x", "z")),
    (2, 0, 32, 128, 128, ("z", "y", "x")),
    (2, 32, 32, 128, 128, ("z", "x", "y")),
    (0, 0, 64, 0, 256, ("z", "y", "x")),
    (1, 0, 64, 0, 256, ("z", "x", "y")),
)
KV_PIECES = (0, 1, 2)
Q_PIECES = (3, 4)
SCALE = 128 ** (-0.5)
LOG2E = 1.4426950408889634


def place():
    dp, ctx = lax.axis_index("dp"), lax.axis_index("ctx")
    return {
        "x": lax.div(dp, 8) * 2 + lax.div(ctx, 4),
        "y": lax.rem(lax.div(dp, 2), 4),
        "z": lax.rem(ctx, 4),
        "core": lax.rem(dp, 2),
    }


def device(at):
    return (
        lax.div(at["x"], 2) * 8 + at["y"] * 2 + at["core"],
        lax.rem(at["x"], 2) * 4 + at["z"],
    )


def moved(at, axis, by):
    return {**at, axis: lax.rem(at[axis] + 4 + by, 4)}


def sibling(at):
    return {**at, "core": 1 - at["core"]}


def greet(targets):
    barrier = pltpu.get_barrier_semaphore()
    for target in targets:
        pl.semaphore_signal(barrier, inc=1, device_id=target, device_id_type=MESH)
    pl.semaphore_wait(barrier, len(targets))


def partners(at):
    near = [device(moved(at, axis, by)) for axis in AXES for by in (1, -1, 2)]
    return near + [device(sibling(at))] + ctx_peers()


def ctx_peers():
    dp, ctx = lax.axis_index("dp"), lax.axis_index("ctx")
    return [(dp, lax.rem(ctx + k, 8)) for k in range(1, 8)]


def remote(src, dst, send, recv, target):
    return pltpu.make_async_remote_copy(
        src_ref=src, dst_ref=dst, send_sem=send, recv_sem=recv, device_id=target, device_id_type=MESH
    )


class Links:
    def __init__(self, send, recv, twin):
        self.send, self.recv, self.twin = send, recv, twin
        self.slots, self.started = {}, []

    def slot(self, key):
        return self.slots.setdefault(key, len(self.slots))

    def launch(self, key, src, dst, target):
        k = self.slot(key)
        copy = remote(src, dst, self.send.at[k], self.recv.at[k], target)
        copy.start()
        self.started.append(copy)

    def arrival(self, key, ref):
        k = self.slot(key)
        remote(ref, ref, self.send.at[k], self.recv.at[k], self.twin).wait_recv()

    def finish(self):
        for copy in self.started:
            copy.wait_send()


def turn_half(a):
    return pltpu.roll(a, 64, 1)


def gather_kernel(
    tokens, wq, wk, wv, cos_table, sin_table,
    w_out, turned_out, q_out, kv_out,
    w, tok, twin_tok, turned, copy_sem, send, recv,
):
    me = place()
    core = me["core"]
    twin = device(sibling(me))
    links = Links(send, recv, twin)
    load = pltpu.make_async_copy(tokens, tok, copy_sem.at[0])
    load.start()
    x_hi, x_lo = lax.div(me["x"], 2), lax.rem(me["x"], 2)
    w[2, x_hi, me["y"], core, x_lo, me["z"], :, 0:128] = wk[...].astype(BF16)
    w[2, x_hi, me["y"], core, x_lo, me["z"], :, 128:256] = wv[...].astype(BF16)
    w[0, x_hi, me["y"], core, x_lo, me["z"]] = wq[:, 0:256].astype(BF16)
    w[1, x_hi, me["y"], core, x_lo, me["z"]] = wq[:, 256:512].astype(BF16)

    def block(n, first, second, third, core_at=core, half=None):
        part, row, rows, col, cols, order = PIECES[n]
        at = dict(zip(order, (first, second, third)))
        x, y, z = (at[axis] for axis in AXES)
        if half is not None:
            rows = rows // 2
            row = row + half * rows
        return w.at[
            part,
            slice(None) if x is None else lax.div(x, 2),
            slice(None) if y is None else y,
            core_at,
            slice(None) if x is None else lax.rem(x, 2),
            slice(None) if z is None else z,
            pl.ds(row, rows),
            pl.ds(col, cols),
        ]

    def shifted(n, phase, by):
        axis = PIECES[n][5][phase]
        return moved(me, axis, by)

    def index(n, phase, by=0):
        axis = PIECES[n][5][phase]
        return moved(me, axis, by)[axis]

    greet(partners(me))
    everything = KV_PIECES + Q_PIECES
    for n in everything:
        mine = block(n, *(me[axis] for axis in PIECES[n][5]))
        for by in (1, -1, 2):
            links.launch((n, 0, by), mine, mine, device(shifted(n, 0, by)))
    for k in range(8):
        columns = tokens.at[:, pl.ds(pl.multiple_of(k * 1024 + (1 - core) * 512, 512), 512)]
        links.launch(("tokens", k), columns, twin_tok.at[k], twin)

    def spread(n, key, axis_at, ref):
        for by in (1, -1):
            links.launch((n, key, by), ref, ref, device(shifted(n, axis_at, by)))

    def pass_on(n, key, axis_at, where):
        for d, by in enumerate((1, -1)):
            source = index(n, axis_at, -by)
            links.arrival((n, key, by), block(n, *where(source)))
            half = block(n, *where(source), half=d)
            links.launch((n, key, "far", by), half, half, device(shifted(n, axis_at, by)))

    def far_arrival(n, key, axis_at, where):
        far = index(n, axis_at, 2)
        for d, by in enumerate((1, -1)):
            links.arrival((n, key, "far", by), block(n, *where(far), half=d))

    SHIFTS = (0, -1, 1, 2)

    def chunk(n, c):
        return lambda third: (None, index(n, 1, SHIFTS[c]), third)

    def to_twin(n, key, where):
        links.launch((n, "twin", key), block(n, *where), block(n, *where), twin)

    def from_twin(n):
        for key in range(3):
            links.arrival((n, "twin", key), block(n, None, None, index(n, 2, (0, -1, 1)[key]), 1 - core))
        for c in range(4):
            where = (None, index(n, 1, SHIFTS[c]), index(n, 2, 2))
            links.arrival((n, "twin", 3 + c), block(n, *where, core_at=1 - core))

    def step_first(n):
        second, third = index(n, 1), index(n, 2)
        for by in (1, -1, 2):
            links.arrival((n, 0, by), block(n, index(n, 0, -by), second, third))
        line = block(n, None, second, third)
        spread(n, 1, 1, line)
        spread(n, (2, 0), 2, line)

    def step_second(n):
        third = index(n, 2)
        second_at = lambda second: (None, second, third)
        pass_on(n, 1, 1, second_at)
        for c in (1, 2):
            spread(n, (2, c), 2, block(n, *chunk(n, c)(third)))

    def step_third(n):
        third = index(n, 2)
        pass_on(n, (2, 0), 2, chunk(n, 0))
        far_arrival(n, 1, 1, lambda second: (None, second, third))
        spread(n, (2, 3), 2, block(n, *chunk(n, 3)(third)))
        to_twin(n, 0, (None, None, third))

    def step_chunks(n, cs):
        for c in cs:
            pass_on(n, (2, c), 2, chunk(n, c))

    def step_near_twin(n):
        for key, by in ((1, -1), (2, 1)):
            to_twin(n, key, (None, None, index(n, 2, by)))

    def step_far(n, c):
        far_arrival(n, (2, c), 2, chunk(n, c))
        to_twin(n, 3 + c, chunk(n, c)(index(n, 2, 2)))

    for step in (step_first, step_second, step_third):
        for n in everything:
            step(n)

    load.wait()
    for k in range(8):
        links.arrival(("tokens", k), twin_tok.at[k])

    def turn(k):
        at = pl.multiple_of(k * 1024 + core * 512, 512)
        turned[k, :, 0:256] = tok[:, pl.ds(at, 512)].T
        turned[k, :, 256:512] = twin_tok[k].T

    def finish_piece(n):
        for c in range(4):
            step_far(n, c)

    for n in KV_PIECES:
        step_chunks(n, (1, 2, 3))
    for n in Q_PIECES:
        step_chunks(n, (1,))
    for n in KV_PIECES:
        step_near_twin(n)
        finish_piece(n)
    for n in Q_PIECES:
        step_chunks(n, (2,))
    for n in KV_PIECES:
        from_twin(n)

    def project(part):
        def add(k, total):
            lhs = tok[:, pl.ds(pl.multiple_of(k * 2048, 2048), 2048)]
            rows = w[part, lax.div(k, 2), pl.ds(lax.rem(k, 2) * 2, 2)].reshape(2048, 256)
            return total + jnp.dot(lhs, rows, preferred_element_type=F32)

        return lax.fori_loop(0, 4, add, jnp.zeros((256, 256), F32))

    cos, sin = cos_table[...], sin_table[...]
    keep = []

    def store(part):
        copy = pltpu.make_async_copy(w.at[part], w_out.at[part], copy_sem.at[1 + part])
        copy.start()
        keep.append(copy)

    ctx = lax.axis_index("ctx")
    both = project(2)
    key = both[:, 0:128]
    kv_out[ctx, :, 0:128] = (key * cos + turn_half(key) * sin).astype(BF16)
    kv_out[ctx, :, 128:256] = both[:, 128:256].astype(BF16)
    peers = ctx_peers()
    for k in (4, 2, 6, 1, 3, 5, 7):
        links.launch(("kv", k), kv_out.at[ctx], kv_out.at[ctx], peers[k - 1])
    store(2)
    for n in Q_PIECES:
        step_chunks(n, (3,))
    for n in Q_PIECES:
        step_near_twin(n)

    def turn_step(k, _):
        turn(k)
        return 0

    lax.fori_loop(0, 8, turn_step, 0)
    copy = pltpu.make_async_copy(turned, turned_out, copy_sem.at[4])
    copy.start()
    keep.append(copy)
    for c in range(4):
        for n in Q_PIECES:
            step_far(n, c)
    for n in Q_PIECES:
        from_twin(n)
        part = PIECES[n][0]
        store(part)
        both = project(part)
        for h in range(2):
            query = both[:, h * 128 : h * 128 + 128]
            rotated = (query * cos + turn_half(query) * sin).astype(BF16)
            q_out[:, part * 256 + h * 128 : part * 256 + h * 128 + 128] = rotated
    for k in range(1, 8):
        links.arrival(("kv", k), kv_out.at[lax.rem(ctx + 8 - k, 8)])
    for copy in keep:
        copy.wait()
    links.finish()


def gather_weights(tokens, wq, wk, wv, cos_table, sin_table):
    vmem, anywhere = pl.BlockSpec(memory_space=pltpu.VMEM), pl.BlockSpec(memory_space=pl.ANY)
    shape = jax.ShapeDtypeStruct
    return pl.pallas_call(
        gather_kernel,
        out_shape=(
            shape((3, 2, 4, 2, 2, 4, 64, 256), BF16),
            shape((8, 512, 512), BF16),
            shape((256, 512), BF16),
            shape((8, 256, 256), BF16),
        ),
        in_specs=[anywhere, vmem, vmem, vmem, vmem, vmem],
        out_specs=(anywhere, anywhere, vmem, vmem),
        scratch_shapes=[
            pltpu.VMEM((3, 2, 4, 2, 2, 4, 64, 256), BF16),
            pltpu.VMEM((256, 8192), BF16),
            pltpu.VMEM((8, 256, 512), BF16),
            pltpu.VMEM((8, 512, 512), BF16),
            pltpu.SemaphoreType.DMA((5,)),
            pltpu.SemaphoreType.DMA((176,)),
            pltpu.SemaphoreType.DMA((176,)),
        ],
        compiler_params=pltpu.CompilerParams(
            collective_id=0, has_side_effects=True, vmem_limit_bytes=44 * 2**20
        ),
        name="gather_weights",
    )(tokens, wq, wk, wv, cos_table, sin_table)


def attention_kernel(
    positions, own_positions, q, kv, grad, cos_table, sin_table,
    attention, grad_q, terms,
    qs, gs, gs_t, keys_t, values_t, scores, top, total, att_t, gq_t,
):
    for h in range(4):
        rows = slice(h * 256, h * 256 + 256)
        qs[rows] = q[:, h * 128 : h * 128 + 128]
        gs[rows] = grad[:, h * 128 : h * 128 + 128]
        gs_t[:, rows] = grad[:, h * 128 : h * 128 + 128].T
    for k in range(8):
        cols = slice(k * 256, k * 256 + 256)
        keys_t[:, cols] = kv[k, :, 0:128].T
        values_t[:, cols] = kv[k, :, 128:256].T
    nt = (((1,), (1,)), ((), ()))
    lead = own_positions[...] - lax.broadcasted_iota(jnp.int32, (128, 256), 0)
    top[...] = jnp.full(top.shape, MASKED, F32)

    def score(k, _):
        for h in range(4):
            cols = slice(h * 256, h * 256 + 256)
            s = lax.dot_general(kv[k, :, 0:128], qs[cols], nt, preferred_element_type=F32)
            upper = jnp.where(lead >= positions[k * 256], s[0:128], MASKED)
            lower = jnp.where(lead >= positions[k * 256 + 128], s[128:256], MASKED)
            scores[k, 0:128, cols] = upper
            scores[k, 128:256, cols] = lower
            high = jnp.max(jnp.maximum(upper, lower), axis=0, keepdims=True)
            top[:, cols] = jnp.maximum(top[:, cols], high)
        return 0

    lax.fori_loop(0, 8, score, 0)
    total[...] = jnp.zeros(total.shape, F32)
    att_t[...] = jnp.zeros(att_t.shape, F32)

    def weigh(k, _):
        at = pl.ds(pl.multiple_of(k * 256, 256), 256)
        for h in range(4):
            cols = slice(h * 256, h * 256 + 256)
            weight = jnp.exp2((scores[k, :, cols] - top[:, cols]) * (SCALE * LOG2E))
            scores[k, :, cols] = weight
            total[:, cols] += jnp.sum(weight, axis=0, keepdims=True)
            att_t[:, cols] += jnp.dot(values_t[:, at], weight.astype(BF16), preferred_element_type=F32)
        return 0

    lax.fori_loop(0, 8, weigh, 0)
    for h in range(4):
        cols = slice(h * 256, h * 256 + 256)
        inverse = 1.0 / total[:, cols]
        out = (att_t[:, cols] / total[:, cols]).astype(BF16)
        attention[:, h * 128 : h * 128 + 128] = out.T
        total[:, cols] = inverse
        top[:, cols] = jnp.sum(gs_t[:, cols].astype(F32) * out.astype(F32), axis=0, keepdims=True)
    gq_t[...] = jnp.zeros(gq_t.shape, F32)

    def back(k, _):
        at = pl.ds(pl.multiple_of(k * 256, 256), 256)
        key_term = jnp.zeros((256, 128), F32)
        value_term = jnp.zeros((256, 128), F32)
        for h in range(4):
            cols = slice(h * 256, h * 256 + 256)
            probs = scores[k, :, cols] * total[:, cols]
            grad_probs = lax.dot_general(kv[k, :, 128:256], gs[cols], nt, preferred_element_type=F32)
            dscore = (probs * (grad_probs - top[:, cols])).astype(BF16)
            key_term += jnp.dot(dscore, qs[cols], preferred_element_type=F32)
            value_term += jnp.dot(probs.astype(BF16), gs[cols], preferred_element_type=F32)
            gq_t[:, cols] += jnp.dot(keys_t[:, at], dscore, preferred_element_type=F32)
        terms[k, :, 0:128] = (key_term * SCALE).astype(BF16)
        terms[k, :, 128:256] = value_term.astype(BF16)
        return 0

    lax.fori_loop(0, 8, back, 0)
    for h in range(4):
        a = gq_t[:, h * 256 : h * 256 + 256].T * SCALE
        unrotated = a * cos_table[...] - turn_half(a) * sin_table[...]
        grad_q[:, h * 128 : h * 128 + 128] = unrotated.astype(BF16)


def attend(positions, own_positions, q, kv, grad, cos_table, sin_table):
    vmem = pl.BlockSpec(memory_space=pltpu.VMEM)
    shape = jax.ShapeDtypeStruct
    return pl.pallas_call(
        attention_kernel,
        out_shape=(shape((256, 512), BF16), shape((256, 512), BF16), shape((8, 256, 256), BF16)),
        in_specs=[pl.BlockSpec(memory_space=pltpu.SMEM)] + [vmem] * 6,
        out_specs=(vmem, vmem, vmem),
        scratch_shapes=[
            pltpu.VMEM((1024, 128), BF16),
            pltpu.VMEM((1024, 128), BF16),
            pltpu.VMEM((128, 1024), BF16),
            pltpu.VMEM((128, 2048), BF16),
            pltpu.VMEM((128, 2048), BF16),
            pltpu.VMEM((8, 256, 1024), F32),
            pltpu.VMEM((1, 1024), F32),
            pltpu.VMEM((1, 1024), F32),
            pltpu.VMEM((128, 1024), F32),
            pltpu.VMEM((128, 1024), F32),
        ],
        compiler_params=pltpu.CompilerParams(vmem_limit_bytes=32 * 2**20),
        name="attend",
    )(positions, own_positions, q, kv, grad, cos_table, sin_table)


def scatter_kernel(
    turned, w_all, grad_q, terms, cos_table, sin_table,
    tokens_out, out,
    held, w, grads, landed, grad_tok, copy_sem, send, recv, *buffers,
):
    me = place()
    core = me["core"]
    ctx = lax.axis_index("ctx")
    twin = device(sibling(me))
    links = Links(send, recv, twin)
    accs = [buffers[9 * n : 9 * n + 3] for n in range(len(PIECES))]
    vias = [buffers[9 * n + 3 : 9 * n + 5] for n in range(len(PIECES))]
    ends = [buffers[9 * n + 5 : 9 * n + 8] for n in range(len(PIECES))]
    load = pltpu.make_async_copy(turned, held, copy_sem.at[0])
    load.start()
    load_w = pltpu.make_async_copy(w_all, w, copy_sem.at[1])
    load_w.start()
    greet(partners(me))
    links.launch("grad_q", grad_q, grads.at[1, :, pl.ds(0, 512)], twin)
    peers = ctx_peers()
    for k in (4, 2, 6, 1, 3, 5, 7):
        links.launch(("kv", k), terms.at[lax.rem(ctx + k, 8)], landed.at[k - 1], peers[k - 1])
    grads[0, :, 0:512] = grad_q[...]
    load.wait()
    links.arrival("grad_q", grads.at[1, :, pl.ds(0, 512)])

    def axes(n):
        return tuple(reversed(PIECES[n][5]))

    def near(n, phase, by):
        return device(moved(me, axes(n)[phase], by))

    def at(n, phase, by=0):
        axis = axes(n)[phase]
        return moved(me, axis, by)[axis]

    def product(pieces, x, y):
        part = PIECES[pieces[0]][0]
        k = lax.div(x, 2) * 4 + y
        lhs = held[k, pl.ds(pl.multiple_of(lax.rem(x, 2) * 256, 256), 256)]
        rhs = grads[:, :, part * 256 : part * 256 + 256].reshape(512, 256)
        term = jnp.dot(lhs, rhs, preferred_element_type=F32).astype(BF16)
        for n in pieces:
            _, row, rows, col, cols, _ = PIECES[n]
            for z in range(4):
                first, second, third = ({"x": x, "y": y, "z": z}[axis] for axis in axes(n))
                for half in range(2):
                    start = z * 64 + row + half * rows // 2
                    accs[n][0][first, half, second, third] = term[
                        start : start + rows // 2, col : col + cols
                    ]

    SHIFTS = (2, 1, -1, 0)

    def send_far(n):
        for c in range(4):
            j = at(n, 1, SHIFTS[c])
            for d, by in enumerate((1, -1)):
                src = accs[n][0].at[at(n, 0, 2), d, j]
                links.launch((n, "via", c, d), src, vias[n][0].at[d, j], near(n, 0, by))

    def send_near(n, d, by):
        for c in range(4):
            j = at(n, 1, SHIFTS[c])
            src = accs[n][0].at[at(n, 0, by), 1 - d, j]
            links.launch((n, "end", c, d, 1 - d), src, ends[n][0].at[d, 1 - d, j], near(n, 0, by))

    def relay(n, c):
        j = at(n, 1, SHIFTS[c])
        acc, via, end = accs[n][0], vias[n][0], ends[n][0]
        for d, by in enumerate((1, -1)):
            links.arrival((n, "via", c, d), via.at[d, j])
            i = at(n, 0, by)
            acc[i, d, j] = (acc[i, d, j].astype(F32) + via[d, j].astype(F32)).astype(BF16)
            links.launch((n, "end", c, d, d), acc.at[i, d, j], end.at[d, d, j], near(n, 0, by))

    def gathered(n, c):
        j = at(n, 1, SHIFTS[c])
        acc, end, later = accs[n][0], ends[n][0], accs[n][1]
        for h in range(2):
            for d in range(2):
                links.arrival((n, "end", c, d, h), end.at[d, h, j])
            mine = acc[at(n, 0), h, j].astype(F32)
            later[j, h] = (mine + end[0, h, j].astype(F32) + end[1, h, j].astype(F32)).astype(BF16)
        if c == 0:
            for d, by in enumerate((1, -1)):
                links.launch((n, "via2", d), later.at[j, d], vias[n][1].at[d], near(n, 1, by))
        elif c < 3:
            d, by = c - 1, SHIFTS[c]
            src = later.at[j, 1 - d]
            links.launch((n, "end2", d, 1 - d), src, ends[n][1].at[d, 1 - d], near(n, 1, by))

    def second(n):
        acc, via, end = accs[n][1], vias[n][1], ends[n][1]
        for d, by in enumerate((1, -1)):
            links.arrival((n, "via2", d), via.at[d])
            i = at(n, 1, by)
            acc[i, d] = (acc[i, d].astype(F32) + via[d].astype(F32)).astype(BF16)
            links.launch((n, "end2", d, d), acc.at[i, d], end.at[d, d], near(n, 1, by))

    def third(n):
        acc, end, later = accs[n][1], ends[n][1], accs[n][2]
        for h in range(2):
            for d in range(2):
                links.arrival((n, "end2", d, h), end.at[d, h])
            mine = acc[at(n, 1), h].astype(F32)
            total = (mine + end[0, h].astype(F32) + end[1, h].astype(F32)).astype(BF16)
            for k in range(4):
                later[k, h] = total[k]
        for s, by in enumerate((1, -1, 2)):
            links.launch((n, "last", s), later.at[at(n, 2, by)], ends[n][2].at[s], near(n, 2, by))

    def last(n):
        part, row, rows, col, cols, _ = PIECES[n]
        acc, end = accs[n][2], ends[n][2]
        for s in range(3):
            links.arrival((n, "last", s), end.at[s])
        for h in range(2):
            total = acc[at(n, 2), h].astype(F32)
            for s in range(3):
                total = total + end[s, h].astype(F32)
            start = row + h * (rows // 2)
            out[start : start + rows // 2, part * 256 + col : part * 256 + col + cols] = total

    def products(n, by):
        axis = axes(n)[0]
        other = "y" if axis == "x" else "x"
        i = at(n, 0, by)

        def one(j, _):
            where = {axis: i, other: j}
            product((n,), where["x"], where["y"])
            return 0

        lax.fori_loop(0, 4, one, 0)

    for n in Q_PIECES:
        products(n, 2)
        send_far(n)
    for d, by in enumerate((1, -1)):
        for n in Q_PIECES:
            products(n, by)
            send_near(n, d, by)
    for n in Q_PIECES:
        products(n, 0)
    for c in range(4):
        for n in Q_PIECES:
            relay(n, c)

    for k in range(1, 8):
        links.arrival(("kv", k), landed.at[k - 1])
    keyval = terms[ctx].astype(F32)
    for k in range(7):
        keyval = keyval + landed[k].astype(F32)
    key = keyval[:, 0:128]
    grads[0, :, 512:640] = (key * cos_table[...] - turn_half(key) * sin_table[...]).astype(BF16)
    grads[0, :, 640:768] = keyval[:, 128:256].astype(BF16)
    columns = pl.ds(512, 256)
    links.launch("grad_kv", grads.at[0, :, columns], grads.at[1, :, columns], twin)
    load_w.wait()

    def input_slice(k, _):
        total = None
        for part in range(3):
            lhs = grads[0, :, part * 256 : part * 256 + 256]
            rows = w[part, lax.div(k, 8), lax.rem(lax.div(k, 2), 4), lax.rem(k, 2)].reshape(512, 256)
            term = lax.dot_general(lhs, rows, (((1,), (1,)), ((), ())), preferred_element_type=F32)
            total = term if total is None else total + term
        grad_tok[:, pl.ds(pl.multiple_of(k * 512, 512), 512)] = total.astype(BF16)
        return 0

    stores = []

    def inputs(quarter):
        lax.fori_loop(quarter * 4, quarter * 4 + 4, input_slice, 0)
        cols = pl.ds(quarter * 2048, 2048)
        copy = pltpu.make_async_copy(grad_tok.at[:, cols], tokens_out.at[:, cols], copy_sem.at[2 + quarter])
        copy.start()
        stores.append(copy)

    inputs(0)
    links.arrival("grad_kv", grads.at[1, :, columns])

    def kv_product(k, _):
        product(KV_PIECES, lax.div(k, 4), lax.rem(k, 4))
        return 0

    lax.fori_loop(0, 16, kv_product, 0)
    for n in KV_PIECES:
        send_far(n)
    for d, by in enumerate((1, -1)):
        for n in KV_PIECES:
            send_near(n, d, by)
    for n in Q_PIECES:
        gathered(n, 0)
    inputs(1)
    for c in range(4):
        for n in KV_PIECES:
            relay(n, c)
        if c < 3:
            for n in Q_PIECES:
                gathered(n, c + 1)
    inputs(2)
    for n in Q_PIECES:
        second(n)
    inputs(3)
    for n in Q_PIECES:
        third(n)
    for c in range(4):
        for n in KV_PIECES:
            gathered(n, c)
    for n in Q_PIECES:
        last(n)
    for step in (second, third, last):
        for n in KV_PIECES:
            step(n)
    for copy in stores:
        copy.wait()
    links.finish()


def scatter_grads(turned, w_all, grad_q, terms, cos_table, sin_table):
    vmem, anywhere = pl.BlockSpec(memory_space=pltpu.VMEM), pl.BlockSpec(memory_space=pl.ANY)
    shape = jax.ShapeDtypeStruct
    buffers = []
    for _, _, rows, _, cols, _ in PIECES:
        tile = (rows // 2, cols)
        for lead in (
            (4, 2, 4, 4), (4, 2, 4), (4, 2), (2, 4, 4), (2, 4), (2, 2, 4, 4), (2, 2, 4), (3, 2), (1,),
        ):
            buffers.append(pltpu.VMEM(lead + tile, BF16))
    return pl.pallas_call(
        scatter_kernel,
        out_shape=(shape((256, 8192), BF16), shape((64, 768), F32)),
        in_specs=[anywhere, anywhere, vmem, vmem, vmem, vmem],
        out_specs=(anywhere, vmem),
        scratch_shapes=[
            pltpu.VMEM((8, 512, 512), BF16),
            pltpu.VMEM((3, 2, 4, 2, 2, 4, 64, 256), BF16),
            pltpu.VMEM((2, 256, 768), BF16),
            pltpu.VMEM((7, 256, 256), BF16),
            pltpu.VMEM((256, 8192), BF16),
            pltpu.SemaphoreType.DMA((6,)),
            pltpu.SemaphoreType.DMA((176,)),
            pltpu.SemaphoreType.DMA((176,)),
            *buffers,
        ],
        compiler_params=pltpu.CompilerParams(
            collective_id=1, has_side_effects=True, vmem_limit_bytes=56 * 2**20
        ),
        name="scatter_grads",
    )(turned, w_all, grad_q, terms, cos_table, sin_table)


def rope_tables(positions_in, head_dim):
    half_width = head_dim // 2
    exponent = jnp.arange(half_width).astype(F32) * (2.0 / head_dim)
    frequency = jnp.power(ROPE_BASE, -exponent)
    angles = positions_in.astype(F32)[:, None] * frequency[None, :]
    cos, sin = jnp.cos(angles), jnp.sin(angles)
    return jnp.concatenate([cos, cos], axis=1), jnp.concatenate([-sin, sin], axis=1)


def body(tokens, positions, query_weight, key_weight, value_weight, grad_output):
    own_positions = lax.dynamic_slice_in_dim(positions, lax.axis_index("ctx") * 256, 256)
    cos_table, sin_table = rope_tables(own_positions, 128)
    w_all, turned, q, kv = gather_weights(
        tokens[0], query_weight, key_weight, value_weight, cos_table, sin_table
    )
    attention, grad_q, terms = attend(
        positions, own_positions[None], q, kv, grad_output[0], cos_table, sin_table
    )
    grad_tokens, grads = scatter_grads(turned, w_all, grad_q, terms, cos_table, sin_table)
    return attention[None], grad_tokens[None], grads[:, :512], grads[:, 512:640], grads[:, 640:]


def solution(mesh):
    in_specs = (
        P("dp", "ctx", None),
        P(),
        P(("dp", "ctx"), None),
        P(("dp", "ctx"), None),
        P(("dp", "ctx"), None),
        P("dp", "ctx", None),
    )
    out_specs = (
        P("dp", "ctx", None),
        P("dp", "ctx", None),
        P(("dp", "ctx"), None),
        P(("dp", "ctx"), None),
        P(("dp", "ctx"), None),
    )
    return jax.shard_map(body, mesh=mesh, in_specs=in_specs, out_specs=out_specs, check_vma=False)
```

time: 1180 us -> 155 us (0.13)
  waiting for transfers between devices: 1070 us -> 0 us
  Pallas kernels: 0 us -> 137 us
  matrix products: 49.8 us -> 0 us
  local copies, waits for them, and re-layouts: 32.3 us -> 16 us
  between operations: 14 us -> 0.74 us
    unnamed x5 -> x0, waiting for transfers between devices: 672 us -> none
    all_gather x2 -> x0, waiting for transfers between devices: 360 us -> none  [the longest x1 323 us: body(): lax.all_gather(local_weights, ('dp', 'ctx'), axis=0, tiled=True)]
    pallas_call x0 -> x3, Pallas kernels: none -> 137 us  [the longest x1 62.8 us: gather_weights(): pl.pallas_call(gather_kernel, out_shape=(shape((3, 2, 4, 2, 2, 4, 64, 256...]
    dot_general x9 -> x0, matrix products: 49.8 us -> none  [the longest x1 14.4 us: body(): lax.dot_general(grad_proj, weights_all, (((1,), (1,)), ((), ())), preferr...]
    reduce_scatter x1 -> x0, waiting for transfers between devices: 36.8 us -> none  [body(): lax.psum_scatter(keyval_term.astype(jnp.bfloat16), 'ctx', scatter_dimensi...]
    unnamed x11 -> x23, local copies, waits for them, and re-layouts: 27.7 us -> 13.1 us
  transfers between devices with their start and end apart: 4 -> 0, of which waited for: 4 -> 0; matrix products, arithmetic and copies ran while one was open for 2% -> 0% of each run, Pallas kernels for 0% -> 0%
where the time goes in v2:
time: 155 us
  Pallas kernels  137 us (88%)
  local copies, waits for them, and re-layouts  16 us (10%)
    pallas_call x1, Pallas kernels, gather_weights(): pl.pallas_call(gather_kernel, out_shape=(shape((3, 2, 4, 2, 2, 4, 64, 256...  62.8 us
    pallas_call x1, Pallas kernels, scatter_grads(): pl.pallas_call(scatter_kernel, out_shape=(shape((256, 8192), BF16), shape...  58 us
    pallas_call x1, Pallas kernels, attend(): pl.pallas_call(attention_kernel, out_shape=(shape((256, 512), BF16), shap...  15.7 us
    unnamed x23, local copies, waits for them, and re-layouts  13.1 us

profile of v2, /device:TPU:0, one launch (start us, length us, event | category | flops | bytes accessed | tf_op | source)
XLA Modules:
  0.0 154.8 jit_solution(6293110125102614636)
XLA Ops:
  0.6 0.0 copy-start.10
  0.6 0.0 copy-start.6
  0.7 0.8 fusion.1
  1.5 0.5 fusion
  2.0 0.1 pad_maximum_fusion
  2.2 0.0 copy-start.2
  2.2 0.0 copy-start.3
  2.2 0.0 copy-start
  2.2 2.3 %copy-done = bf16[1,256,8192]{2,1,0:T(8,128)(2,1)S(1)} copy-done((bf16[1,256,8192]{2,1,0:T(8,128)(2,1)S(1)}, bf16[1,256,8192]{2,1,0:T(8,128)(2,1)}, u32[]{:S(2)}) %copy-start) | copy-done | bytes 4194328
  4.5 0.9 copy-done.7
  5.4 0.8 copy-done.8
  6.1 0.8 copy-done.9
  6.9 62.8 %gather_weights.1 = (bf16[3,2,4,2,2,4,64,256]{7,6,5,4,3,2,1,0:T(8,128)(2,1)}, bf16[8,512,512]{2,1,0:T(8,128)(2,1)S(1)}, bf16[256,512]{1,0:T(8,128)(2,1)S(1)}, bf16[8,256,256]{2,1,0:T(8,128)(2,1)S(1)}) custom-call(bf16[256,8192]{1,0:T(8,128)(2,1)S(1)} %bitcast.5, f32[64,512]{1,0:T(8,128)S(1)} %copy-done.7, f32[64,128]{1,0:T(8,128)S(1)} %copy-done.8, ...), custom_call_target="tpu_custom_call" | custom-call | tf_op jit(solution)/shard_map/gather_weights/pallas_call | solution.py:311
  69.7 0.0 copy-start.1
  69.7 2.0 %copy-done.1 = bf16[8,512,512]{2,1,0:T(8,128)(2,1)} copy-done((bf16[8,512,512]{2,1,0:T(8,128)(2,1)}, bf16[8,512,512]{2,1,0:T(8,128)(2,1)S(1)}, u32[]{:S(2)}) %copy-start.1) | copy-done | bytes 4194328
  71.7 0.0 copy-done.10
  71.7 0.0 copy-done.6
  71.7 15.7 %attend.1 = (bf16[256,512]{1,0:T(8,128)(2,1)}, bf16[256,512]{1,0:T(8,128)(2,1)S(1)}, bf16[8,256,256]{2,1,0:T(8,128)(2,1)S(1)}) custom-call(s32[2048]{0:T(1024)S(1)} %copy-done.10, s32[1,256]{1,0:T(1,128)S(1)} %bitcast.7, bf16[256,512]{1,0:T(8,128)(2,1)S(1)} %get-tuple-element.14.q, bf16[8,256,256]{2,1,0:T(8,128)(2,1)S(1)} %get-tuple-element.15.kv, ...), custom_call_target="tpu_custom_call" | custom-call | tf_op jit(solution)/shard_map/attend/pallas_call | solution.py:417
  87.4 1.0 copy-done.4
  88.4 0.7 copy-done.5
  89.1 58.0 %scatter_grads.1 = (bf16[256,8192]{1,0:T(8,128)(2,1)}, f32[64,768]{1,0:T(8,128)}) custom-call(bf16[8,512,512]{2,1,0:T(8,128)(2,1)} %copy-done.1, bf16[3,2,4,2,2,4,64,256]{7,6,5,4,3,2,1,0:T(8,128)(2,1)} %get-tuple-element.18.w_all, bf16[256,512]{1,0:T(8,128)(2,1)} %copy-done.5, bf16[8,256,256]{2,1,0:T(8,128)(2,1)} %copy-done.4, f32[256,128]{1,0:T(8,128)} %copy-done.2, ...), custom_call_target="tpu_custom_call" | custom-call | tf_op jit(solution)/shard_map/scatter_grads/pallas_call | solution.py:670
  147.2 1.6 %slice.9 = f32[64,512]{1,0:T(8,128)} slice(f32[64,768]{1,0:T(8,128)} %get-tuple-element.22), slice={[0:64], [0:512]} | slice | bytes 262144 | tf_op jit(solution)/shard_map/slice | solution.py:712
  148.8 1.4 fusion.2
  150.2 4.6 %copy.12 = bf16[1,256,8192]{2,1,0:T(8,128)(2,1)} copy(bf16[1,256,8192]{2,1,0:T(8,128)(2,1)} %bitcast.8) | data formatting | bytes 8388608
  (8 shorter events, 0.0 us)
Async XLA Ops:
  0.6 71.1 %copy-start.10 = (s32[2048]{0:T(1024)S(1)}, s32[2048]{0:T(1024)}, u32[]{:S(2)}) copy-start(s32[2048]{0:T(1024)} %positions.1) | copy-start | bytes 24580
  0.6 71.1 %copy-start.6 = (bf16[1,256,512]{2,1,0:T(8,128)(2,1)S(1)}, bf16[1,256,512]{2,1,0:T(8,128)(2,1)}, u32[]{:S(2)}) copy-start(bf16[1,256,512]{2,1,0:T(8,128)(2,1)} %param.11) | copy-start | bytes 786436
  2.2 87.0 %copy-start.2 = (f32[256,128]{1,0:T(8,128)}, f32[256,128]{1,0:T(8,128)S(1)}, u32[]{:S(2)}) copy-start(f32[256,128]{1,0:T(8,128)S(1)} %get-tuple-element.30.cos_table) | copy-start | bytes 393220
  2.2 87.0 %copy-start.3 = (f32[256,128]{1,0:T(8,128)}, f32[256,128]{1,0:T(8,128)S(1)}, u32[]{:S(2)}) copy-start(f32[256,128]{1,0:T(8,128)S(1)} %get-tuple-element.31.sin_table) | copy-start | bytes 393220
  2.2 2.3 %copy-start = (bf16[1,256,8192]{2,1,0:T(8,128)(2,1)S(1)}, bf16[1,256,8192]{2,1,0:T(8,128)(2,1)}, u32[]{:S(2)}) copy-start(bf16[1,256,8192]{2,1,0:T(8,128)(2,1)} %param.6) | copy-start | bytes 12582916
  4.5 0.9 copy-start.7
  5.4 0.8 copy-start.8
  6.1 0.8 copy-start.9
  69.7 2.0 %copy-start.1 = (bf16[8,512,512]{2,1,0:T(8,128)(2,1)}, bf16[8,512,512]{2,1,0:T(8,128)(2,1)S(1)}, u32[]{:S(2)}) copy-start(bf16[8,512,512]{2,1,0:T(8,128)(2,1)S(1)} %get-tuple-element.17.turned) | copy-start | bytes 12582916
  87.4 1.0 copy-start.4
  88.4 0.7 copy-start.5

commit v3 on v2

v3 whole, which is shorter than its diff:
```python
import functools

import jax
import jax.numpy as jnp
from jax import lax
from jax.experimental import pallas as pl
from jax.experimental.pallas import tpu as pltpu
from jax.sharding import PartitionSpec as P

ROPE_BASE = 1000000.0
MASKED = -1e30
MESH = pl.DeviceIdType.MESH
BF16 = jnp.bfloat16
F32 = jnp.float32
AXES = ("x", "y", "z")
PIECES = (
    (2, 0, 64, 0, 128, ("y", "x", "z")),
    (2, 0, 32, 128, 128, ("z", "y", "x")),
    (2, 32, 32, 128, 128, ("z", "x", "y")),
    (0, 0, 64, 0, 256, ("z", "y", "x")),
    (1, 0, 64, 0, 256, ("z", "x", "y")),
)
KV_PIECES = (0, 1, 2)
Q_PIECES = (3, 4)
SCALE = 128 ** (-0.5)
LOG2E = 1.4426950408889634


def place():
    dp, ctx = lax.axis_index("dp"), lax.axis_index("ctx")
    return {
        "x": lax.div(dp, 8) * 2 + lax.div(ctx, 4),
        "y": lax.rem(lax.div(dp, 2), 4),
        "z": lax.rem(ctx, 4),
        "core": lax.rem(dp, 2),
    }


def device(at):
    return (
        lax.div(at["x"], 2) * 8 + at["y"] * 2 + at["core"],
        lax.rem(at["x"], 2) * 4 + at["z"],
    )


def moved(at, axis, by):
    return {**at, axis: lax.rem(at[axis] + 4 + by, 4)}


def sibling(at):
    return {**at, "core": 1 - at["core"]}


def greet(targets):
    barrier = pltpu.get_barrier_semaphore()
    for target in targets:
        pl.semaphore_signal(barrier, inc=1, device_id=target, device_id_type=MESH)
    pl.semaphore_wait(barrier, len(targets))


def partners(at):
    near = [device(moved(at, axis, by)) for axis in AXES for by in (1, -1, 2)]
    return near + [device(sibling(at))] + ctx_peers()


def ctx_peers():
    dp, ctx = lax.axis_index("dp"), lax.axis_index("ctx")
    return [(dp, lax.rem(ctx + k, 8)) for k in range(1, 8)]


def remote(src, dst, send, recv, target):
    return pltpu.make_async_remote_copy(
        src_ref=src, dst_ref=dst, send_sem=send, recv_sem=recv, device_id=target, device_id_type=MESH
    )


class Links:
    def __init__(self, send, recv, twin):
        self.send, self.recv, self.twin = send, recv, twin
        self.slots, self.started = {}, []

    def slot(self, key):
        return self.slots.setdefault(key, len(self.slots))

    def launch(self, key, src, dst, target):
        k = self.slot(key)
        copy = remote(src, dst, self.send.at[k], self.recv.at[k], target)
        copy.start()
        self.started.append(copy)

    def arrival(self, key, ref):
        k = self.slot(key)
        remote(ref, ref, self.send.at[k], self.recv.at[k], self.twin).wait_recv()

    def finish(self):
        for copy in self.started:
            copy.wait_send()


def turn_half(a):
    return pltpu.roll(a, 64, 1)


BYS = (2, 1, -1)


def gather_kernel(
    tokens, wq_hbm, wk_hbm, wv_hbm, tables_hbm,
    w_out, turned_out, q_out, kv_out,
    w, tok, twin_tok, turned, wq, wk, wv, tables, sums, copy_sem, send, recv,
):
    me = place()
    core = me["core"]
    twin = device(sibling(me))
    links = Links(send, recv, twin)
    loads = [
        pltpu.make_async_copy(src, dst, copy_sem.at[k])
        for k, (src, dst) in enumerate(
            ((wq_hbm, wq), (wk_hbm, wk), (wv_hbm, wv), (tables_hbm, tables), (tokens, tok))
        )
    ]
    for copy in loads:
        copy.start()
    for copy in loads[:3]:
        copy.wait()
    x_hi, x_lo = lax.div(me["x"], 2), lax.rem(me["x"], 2)
    w[2, x_hi, me["y"], core, x_lo, me["z"], :, 0:128] = wk[...].astype(BF16)
    w[2, x_hi, me["y"], core, x_lo, me["z"], :, 128:256] = wv[...].astype(BF16)
    w[0, x_hi, me["y"], core, x_lo, me["z"]] = wq[:, 0:256].astype(BF16)
    w[1, x_hi, me["y"], core, x_lo, me["z"]] = wq[:, 256:512].astype(BF16)

    def block(n, first, second, third, core_at=core):
        part, row, rows, col, cols, order = PIECES[n]
        at = dict(zip(order, (first, second, third)))
        x, y, z = (at[axis] for axis in AXES)
        return w.at[
            part,
            slice(None) if x is None else lax.div(x, 2),
            slice(None) if y is None else y,
            core_at,
            slice(None) if x is None else lax.rem(x, 2),
            slice(None) if z is None else z,
            pl.ds(row, rows),
            pl.ds(col, cols),
        ]

    def to(n, phase, by):
        return device(moved(me, PIECES[n][5][phase], by))

    def index(n, phase, by=0):
        axis = PIECES[n][5][phase]
        return moved(me, axis, by)[axis]

    greet(partners(me))
    everything = KV_PIECES + Q_PIECES
    for n in everything:
        mine = block(n, index(n, 0), index(n, 1), index(n, 2))
        for by in BYS:
            links.launch((n, 0, by), mine, mine, to(n, 0, by))
    for k in range(8):
        columns = tokens.at[:, pl.ds(pl.multiple_of(k * 1024 + (1 - core) * 512, 512), 512)]
        links.launch(("tokens", k), columns, twin_tok.at[k], twin)

    def send_chunk(n, c):
        chunk = block(n, None, index(n, 1, c), index(n, 2))
        for by in BYS:
            links.launch((n, 2, c, by), chunk, chunk, to(n, 2, by))

    for n in everything:
        second, third = index(n, 1), index(n, 2)
        for by in BYS:
            links.arrival((n, 0, by), block(n, index(n, 0, -by), second, third))
        line = block(n, None, second, third)
        for by in BYS:
            links.launch((n, 1, by), line, line, to(n, 1, by))
        send_chunk(n, 0)
    for n in everything:
        for by in BYS:
            links.arrival((n, 1, by), block(n, None, index(n, 1, -by), index(n, 2)))
            send_chunk(n, -by)

    CHUNKS = (0,) + tuple(-by for by in BYS)

    def chunk_in(n, c):
        second = index(n, 1, c)
        for by in BYS:
            links.arrival((n, 2, c, by), block(n, None, second, index(n, 2, -by)))
        whole = block(n, None, second, None)
        links.launch((n, "twin", c), whole, whole, twin)

    def twin_in(n, c):
        links.arrival((n, "twin", c), block(n, None, index(n, 1, c), None, 1 - core))

    for copy in loads[3:]:
        copy.wait()
    for k in range(8):
        links.arrival(("tokens", k), twin_tok.at[k])

    def turn(k, _):
        at = pl.multiple_of(k * 1024 + core * 512, 512)
        turned[k, :, 0:256] = tok[:, pl.ds(at, 512)].T
        turned[k, :, 256:512] = twin_tok[k].T
        return 0

    lax.fori_loop(0, 4, turn, 0)
    keep = []

    def store(k, src, dst):
        copy = pltpu.make_async_copy(src, dst, copy_sem.at[k])
        copy.start()
        keep.append(copy)

    for c in CHUNKS:
        for n in KV_PIECES:
            chunk_in(n, c)
    for c in CHUNKS:
        for n in KV_PIECES:
            twin_in(n, c)
    store(5, w.at[2], w_out.at[2])

    def add_kv(k, total):
        lhs = tok[:, pl.ds(pl.multiple_of(k * 2048, 2048), 2048)]
        rows = w[2, lax.div(k, 2), pl.ds(lax.rem(k, 2) * 2, 2)].reshape(2048, 256)
        return total + jnp.dot(lhs, rows, preferred_element_type=F32)

    both = lax.fori_loop(0, 4, add_kv, jnp.zeros((256, 256), F32))
    cos, sin = tables[0], tables[1]
    ctx = lax.axis_index("ctx")
    key = both[:, 0:128]
    kv_out[ctx, :, 0:128] = (key * cos + turn_half(key) * sin).astype(BF16)
    kv_out[ctx, :, 128:256] = both[:, 128:256].astype(BF16)
    peers = ctx_peers()
    for k in (4, 2, 6, 1, 3, 5, 7):
        links.launch(("kv", k), kv_out.at[ctx], kv_out.at[ctx], peers[k - 1])

    def project(c):
        y = index(3, 1, c)
        total = None
        for x_hi in range(2):
            lhs = tok[:, pl.ds(pl.multiple_of((x_hi * 4 + y) * 1024, 1024), 1024)]
            term = jnp.dot(lhs, w[0, x_hi, y].reshape(1024, 256), preferred_element_type=F32)
            total = term if total is None else total + term
        sums[0] = total if c == CHUNKS[0] else sums[0] + total
        x = index(4, 1, c)
        x_hi, x_lo = lax.div(x, 2), lax.rem(x, 2)
        total = None
        for y in range(4):
            for half in range(2):
                at = (x_hi * 4 + y) * 1024 + half * 512 + x_lo * 256
                lhs = tok[:, pl.ds(pl.multiple_of(at, 256), 256)]
                rows = w[1, x_hi, y, half, x_lo].reshape(256, 256)
                term = jnp.dot(lhs, rows, preferred_element_type=F32)
                total = term if total is None else total + term
        sums[1] = total if c == CHUNKS[0] else sums[1] + total

    def finish_chunk(c):
        for n in Q_PIECES:
            twin_in(n, c)
        k = CHUNKS.index(c)
        y = index(3, 1, c)
        store(6 + k, w.at[0, :, y], w_out.at[0, :, y])
        x = index(4, 1, c)
        x_hi, x_lo = lax.div(x, 2), lax.rem(x, 2)
        store(10 + k, w.at[1, x_hi, :, :, x_lo], w_out.at[1, x_hi, :, :, x_lo])
        project(c)

    for n in Q_PIECES:
        chunk_in(n, CHUNKS[0])
    lax.fori_loop(4, 8, turn, 0)
    store(14, turned, turned_out)
    for k in range(1, 4):
        for n in Q_PIECES:
            chunk_in(n, CHUNKS[k])
        finish_chunk(CHUNKS[k - 1])
    finish_chunk(CHUNKS[3])
    for part in range(2):
        for h in range(2):
            query = sums[part, :, h * 128 : h * 128 + 128]
            rotated = (query * cos + turn_half(query) * sin).astype(BF16)
            q_out[:, part * 256 + h * 128 : part * 256 + h * 128 + 128] = rotated
    for k in range(1, 8):
        links.arrival(("kv", k), kv_out.at[lax.rem(ctx + 8 - k, 8)])
    for copy in keep:
        copy.wait()
    links.finish()


def gather_weights(tokens, wq, wk, wv, tables):
    vmem, anywhere = pl.BlockSpec(memory_space=pltpu.VMEM), pl.BlockSpec(memory_space=pl.ANY)
    shape = jax.ShapeDtypeStruct
    return pl.pallas_call(
        gather_kernel,
        out_shape=(
            shape((3, 2, 4, 2, 2, 4, 64, 256), BF16),
            shape((8, 512, 512), BF16),
            shape((256, 512), BF16),
            shape((8, 256, 256), BF16),
        ),
        in_specs=[anywhere] * 5,
        out_specs=(anywhere, anywhere, vmem, vmem),
        scratch_shapes=[
            pltpu.VMEM((3, 2, 4, 2, 2, 4, 64, 256), BF16),
            pltpu.VMEM((256, 8192), BF16),
            pltpu.VMEM((8, 256, 512), BF16),
            pltpu.VMEM((8, 512, 512), BF16),
            pltpu.VMEM((64, 512), F32),
            pltpu.VMEM((64, 128), F32),
            pltpu.VMEM((64, 128), F32),
            pltpu.VMEM((2, 256, 128), F32),
            pltpu.VMEM((2, 256, 256), F32),
            pltpu.SemaphoreType.DMA((15,)),
            pltpu.SemaphoreType.DMA((128,)),
            pltpu.SemaphoreType.DMA((128,)),
        ],
        compiler_params=pltpu.CompilerParams(
            collective_id=0, has_side_effects=True, vmem_limit_bytes=60 * 2**20
        ),
        name="gather_weights",
    )(tokens, wq, wk, wv, tables)


def attention_kernel(
    positions, own_positions, q, kv, grad, tables,
    attention, grad_q, terms,
    qs, gs, gs_t, keys_t, values_t, scores, top, total, att_t, gq_t,
):
    for h in range(4):
        rows = slice(h * 256, h * 256 + 256)
        qs[rows] = q[:, h * 128 : h * 128 + 128]
        gs[rows] = grad[:, h * 128 : h * 128 + 128]
        gs_t[:, rows] = grad[:, h * 128 : h * 128 + 128].T
    for k in range(8):
        cols = slice(k * 256, k * 256 + 256)
        keys_t[:, cols] = kv[k, :, 0:128].T
        values_t[:, cols] = kv[k, :, 128:256].T
    nt = (((1,), (1,)), ((), ()))
    lead = own_positions[...] - lax.broadcasted_iota(jnp.int32, (128, 256), 0)
    top[...] = jnp.full(top.shape, MASKED, F32)

    def score(k, _):
        for h in range(4):
            cols = slice(h * 256, h * 256 + 256)
            s = lax.dot_general(kv[k, :, 0:128], qs[cols], nt, preferred_element_type=F32)
            upper = jnp.where(lead >= positions[k * 256], s[0:128], MASKED)
            lower = jnp.where(lead >= positions[k * 256 + 128], s[128:256], MASKED)
            scores[k, 0:128, cols] = upper
            scores[k, 128:256, cols] = lower
            high = jnp.max(jnp.maximum(upper, lower), axis=0, keepdims=True)
            top[:, cols] = jnp.maximum(top[:, cols], high)
        return 0

    lax.fori_loop(0, 8, score, 0)
    total[...] = jnp.zeros(total.shape, F32)
    att_t[...] = jnp.zeros(att_t.shape, F32)

    def weigh(k, _):
        at = pl.ds(pl.multiple_of(k * 256, 256), 256)
        for h in range(4):
            cols = slice(h * 256, h * 256 + 256)
            weight = jnp.exp2((scores[k, :, cols] - top[:, cols]) * (SCALE * LOG2E))
            scores[k, :, cols] = weight
            total[:, cols] += jnp.sum(weight, axis=0, keepdims=True)
            att_t[:, cols] += jnp.dot(values_t[:, at], weight.astype(BF16), preferred_element_type=F32)
        return 0

    lax.fori_loop(0, 8, weigh, 0)
    for h in range(4):
        cols = slice(h * 256, h * 256 + 256)
        inverse = 1.0 / total[:, cols]
        out = (att_t[:, cols] / total[:, cols]).astype(BF16)
        attention[:, h * 128 : h * 128 + 128] = out.T
        total[:, cols] = inverse
        top[:, cols] = jnp.sum(gs_t[:, cols].astype(F32) * out.astype(F32), axis=0, keepdims=True)
    gq_t[...] = jnp.zeros(gq_t.shape, F32)

    def back(k, _):
        at = pl.ds(pl.multiple_of(k * 256, 256), 256)
        key_term = jnp.zeros((256, 128), F32)
        value_term = jnp.zeros((256, 128), F32)
        for h in range(4):
            cols = slice(h * 256, h * 256 + 256)
            probs = scores[k, :, cols] * total[:, cols]
            grad_probs = lax.dot_general(kv[k, :, 128:256], gs[cols], nt, preferred_element_type=F32)
            dscore = (probs * (grad_probs - top[:, cols])).astype(BF16)
            key_term += jnp.dot(dscore, qs[cols], preferred_element_type=F32)
            value_term += jnp.dot(probs.astype(BF16), gs[cols], preferred_element_type=F32)
            gq_t[:, cols] += jnp.dot(keys_t[:, at], dscore, preferred_element_type=F32)
        terms[k, :, 0:128] = (key_term * SCALE).astype(BF16)
        terms[k, :, 128:256] = value_term.astype(BF16)
        return 0

    lax.fori_loop(0, 8, back, 0)
    for h in range(4):
        a = gq_t[:, h * 256 : h * 256 + 256].T * SCALE
        unrotated = a * tables[0] - turn_half(a) * tables[1]
        grad_q[:, h * 128 : h * 128 + 128] = unrotated.astype(BF16)


def attend(positions, own_positions, q, kv, grad, tables):
    vmem = pl.BlockSpec(memory_space=pltpu.VMEM)
    shape = jax.ShapeDtypeStruct
    return pl.pallas_call(
        attention_kernel,
        out_shape=(shape((256, 512), BF16), shape((256, 512), BF16), shape((8, 256, 256), BF16)),
        in_specs=[pl.BlockSpec(memory_space=pltpu.SMEM)] + [vmem] * 5,
        out_specs=(vmem, vmem, vmem),
        scratch_shapes=[
            pltpu.VMEM((1024, 128), BF16),
            pltpu.VMEM((1024, 128), BF16),
            pltpu.VMEM((128, 1024), BF16),
            pltpu.VMEM((128, 2048), BF16),
            pltpu.VMEM((128, 2048), BF16),
            pltpu.VMEM((8, 256, 1024), F32),
            pltpu.VMEM((1, 1024), F32),
            pltpu.VMEM((1, 1024), F32),
            pltpu.VMEM((128, 1024), F32),
            pltpu.VMEM((128, 1024), F32),
        ],
        compiler_params=pltpu.CompilerParams(vmem_limit_bytes=32 * 2**20),
        name="attend",
    )(positions, own_positions, q, kv, grad, tables)


def scatter_kernel(
    turned, w_all, grad_q, terms, tables,
    tokens_out, out,
    held, w, grads, landed, grad_tok, copy_sem, send, recv, *buffers,
):
    me = place()
    core = me["core"]
    ctx = lax.axis_index("ctx")
    twin = device(sibling(me))
    links = Links(send, recv, twin)
    accs = [buffers[6 * n : 6 * n + 3] for n in range(len(PIECES))]
    ends = [buffers[6 * n + 3 : 6 * n + 6] for n in range(len(PIECES))]
    load = pltpu.make_async_copy(turned, held, copy_sem.at[0])
    load.start()
    load_w = pltpu.make_async_copy(w_all, w, copy_sem.at[1])
    load_w.start()
    greet(partners(me))
    links.launch("grad_q", grad_q, grads.at[1, :, pl.ds(0, 512)], twin)
    peers = ctx_peers()
    for k in (4, 2, 6, 1, 3, 5, 7):
        links.launch(("kv", k), terms.at[lax.rem(ctx + k, 8)], landed.at[k - 1], peers[k - 1])
    grads[0, :, 0:512] = grad_q[...]
    load.wait()
    links.arrival("grad_q", grads.at[1, :, pl.ds(0, 512)])

    def axes(n):
        return tuple(reversed(PIECES[n][5]))

    def to(n, phase, by):
        return device(moved(me, axes(n)[phase], by))

    def at(n, phase, by=0):
        axis = axes(n)[phase]
        return moved(me, axis, by)[axis]

    def product(pieces, x, y):
        part = PIECES[pieces[0]][0]
        k = lax.div(x, 2) * 4 + y
        lhs = held[k, pl.ds(pl.multiple_of(lax.rem(x, 2) * 256, 256), 256)]
        rhs = grads[:, :, part * 256 : part * 256 + 256].reshape(512, 256)
        term = jnp.dot(lhs, rhs, preferred_element_type=F32).astype(BF16)
        for n in pieces:
            _, row, rows, col, cols, _ = PIECES[n]
            for z in range(4):
                first, second, third = ({"x": x, "y": y, "z": z}[axis] for axis in axes(n))
                start = z * 64 + row
                accs[n][0][first, second, third] = term[start : start + rows, col : col + cols]

    CHUNKS = (2, 1, -1, 0)

    def products(n, c):
        axis, other = axes(n)[:2]
        j = at(n, 1, c)

        def one(i, _):
            where = {axis: i, other: j}
            product((n,), where["x"], where["y"])
            return 0

        lax.fori_loop(0, 4, one, 0)

    def send_chunk(n, c):
        j = at(n, 1, c)
        for s, by in enumerate(BYS):
            links.launch((n, 0, c, s), accs[n][0].at[at(n, 0, by), j], ends[n][0].at[s, j], to(n, 0, by))

    def summed(n, phase, index):
        lead = (at(n, phase),) + index
        total = accs[n][phase][lead].astype(F32)
        for s in range(3):
            total = total + ends[n][phase][(s,) + index].astype(F32)
        return total

    def chunk_in(n, c):
        j = at(n, 1, c)
        for s in range(3):
            links.arrival((n, 0, c, s), ends[n][0].at[s, j])
        accs[n][1][j] = summed(n, 0, (j,)).astype(BF16)
        if c != 0:
            s = BYS.index(c)
            links.launch((n, 1, s), accs[n][1].at[j], ends[n][1].at[s], to(n, 1, c))

    def second(n):
        for s in range(3):
            links.arrival((n, 1, s), ends[n][1].at[s])
        accs[n][2][...] = summed(n, 1, ()).astype(BF16)
        for s, by in enumerate(BYS):
            links.launch((n, 2, s), accs[n][2].at[at(n, 2, by)], ends[n][2].at[s], to(n, 2, by))

    def last(n):
        part, row, rows, col, cols, _ = PIECES[n]
        for s in range(3):
            links.arrival((n, 2, s), ends[n][2].at[s])
        out[row : row + rows, part * 256 + col : part * 256 + col + cols] = summed(n, 2, ())

    for c in CHUNKS:
        for n in Q_PIECES:
            products(n, c)
            send_chunk(n, c)

    load_w.wait()

    def input_slice(k, _):
        total = None
        for part in range(3):
            lhs = grads[0, :, part * 256 : part * 256 + 256]
            rows = w[part, lax.div(k, 8), lax.rem(lax.div(k, 2), 4), lax.rem(k, 2)].reshape(512, 256)
            term = lax.dot_general(lhs, rows, (((1,), (1,)), ((), ())), preferred_element_type=F32)
            total = term if total is None else total + term
        grad_tok[:, pl.ds(pl.multiple_of(k * 512, 512), 512)] = total.astype(BF16)
        return 0

    stores = []

    def inputs(quarter):
        lax.fori_loop(quarter * 4, quarter * 4 + 4, input_slice, 0)
        cols = pl.ds(quarter * 2048, 2048)
        copy = pltpu.make_async_copy(grad_tok.at[:, cols], tokens_out.at[:, cols], copy_sem.at[2 + quarter])
        copy.start()
        stores.append(copy)

    for k in range(1, 8):
        links.arrival(("kv", k), landed.at[k - 1])
    keyval = terms[ctx].astype(F32)
    for k in range(7):
        keyval = keyval + landed[k].astype(F32)
    key = keyval[:, 0:128]
    grads[0, :, 512:640] = (key * tables[0] - turn_half(key) * tables[1]).astype(BF16)
    grads[0, :, 640:768] = keyval[:, 128:256].astype(BF16)
    columns = pl.ds(512, 256)
    links.launch("grad_kv", grads.at[0, :, columns], grads.at[1, :, columns], twin)
    inputs(0)
    links.arrival("grad_kv", grads.at[1, :, columns])

    def kv_product(k, _):
        product(KV_PIECES, lax.div(k, 4), lax.rem(k, 4))
        return 0

    lax.fori_loop(0, 16, kv_product, 0)
    for c in CHUNKS:
        for n in KV_PIECES:
            send_chunk(n, c)
    for k, c in enumerate(CHUNKS):
        for n in Q_PIECES:
            chunk_in(n, c)
        if k < 3:
            inputs(k + 1)
    for c in CHUNKS:
        for n in KV_PIECES:
            chunk_in(n, c)
    for step in (second, last):
        for n in Q_PIECES + KV_PIECES:
            step(n)
    for copy in stores:
        copy.wait()
    links.finish()


def scatter_grads(turned, w_all, grad_q, terms, tables):
    vmem, anywhere = pl.BlockSpec(memory_space=pltpu.VMEM), pl.BlockSpec(memory_space=pl.ANY)
    shape = jax.ShapeDtypeStruct
    buffers = []
    for _, _, rows, _, cols, _ in PIECES:
        for lead in ((4, 4, 4), (4, 4), (4,), (3, 4, 4), (3, 4), (3,)):
            buffers.append(pltpu.VMEM(lead + (rows, cols), BF16))
    return pl.pallas_call(
        scatter_kernel,
        out_shape=(shape((256, 8192), BF16), shape((64, 768), F32)),
        in_specs=[anywhere, anywhere, vmem, vmem, vmem],
        out_specs=(anywhere, vmem),
        scratch_shapes=[
            pltpu.VMEM((8, 512, 512), BF16),
            pltpu.VMEM((3, 2, 4, 2, 2, 4, 64, 256), BF16),
            pltpu.VMEM((2, 256, 768), BF16),
            pltpu.VMEM((7, 256, 256), BF16),
            pltpu.VMEM((256, 8192), BF16),
            pltpu.SemaphoreType.DMA((6,)),
            pltpu.SemaphoreType.DMA((100,)),
            pltpu.SemaphoreType.DMA((100,)),
            *buffers,
        ],
        compiler_params=pltpu.CompilerParams(
            collective_id=1, has_side_effects=True, vmem_limit_bytes=48 * 2**20
        ),
        name="scatter_grads",
    )(turned, w_all, grad_q, terms, tables)


def rope_tables(positions_in, head_dim):
    half_width = head_dim // 2
    exponent = jnp.arange(half_width).astype(F32) * (2.0 / head_dim)
    frequency = jnp.power(ROPE_BASE, -exponent)
    angles = positions_in.astype(F32)[:, None] * frequency[None, :]
    cos, sin = jnp.cos(angles), jnp.sin(angles)
    return jnp.stack([jnp.concatenate([cos, cos], axis=1), jnp.concatenate([-sin, sin], axis=1)])


def body(tokens, positions, query_weight, key_weight, value_weight, grad_output):
    own_positions = lax.dynamic_slice_in_dim(positions, lax.axis_index("ctx") * 256, 256)
    tables = rope_tables(own_positions, 128)
    w_all, turned, q, kv = gather_weights(
        tokens[0], query_weight, key_weight, value_weight, tables
    )
    attention, grad_q, terms = attend(
        positions, own_positions[None], q, kv, grad_output[0], tables
    )
    grad_tokens, grads = scatter_grads(turned, w_all, grad_q, terms, tables)
    return attention[None], grad_tokens[None], grads[:, :512], grads[:, 512:640], grads[:, 640:]


def solution(mesh):
    in_specs = (
        P("dp", "ctx", None),
        P(),
        P(("dp", "ctx"), None),
        P(("dp", "ctx"), None),
        P(("dp", "ctx"), None),
        P("dp", "ctx", None),
    )
    out_specs = (
        P("dp", "ctx", None),
        P("dp", "ctx", None),
        P(("dp", "ctx"), None),
        P(("dp", "ctx"), None),
        P(("dp", "ctx"), None),
    )
    return jax.shard_map(body, mesh=mesh, in_specs=in_specs, out_specs=out_specs, check_vma=False)
```

time: 155 us -> 147 us (0.948)
  local copies, waits for them, and re-layouts: 16 us -> 5.49 us
  Pallas kernels: 137 us -> 139 us
    unnamed x23 -> x11, local copies, waits for them, and re-layouts: 13.1 us -> 4.19 us
where the time goes in v3:
time: 147 us
  Pallas kernels  139 us (95%)
  local copies, waits for them, and re-layouts  5.49 us (4%)
  other arithmetic  2.21 us (2%)
    pallas_call x1, Pallas kernels, gather_weights(): pl.pallas_call(gather_kernel, out_shape=(shape((3, 2, 4, 2, 2, 4, 64, 256...  64.3 us
    pallas_call x1, Pallas kernels, scatter_grads(): pl.pallas_call(scatter_kernel, out_shape=(shape((256, 8192), BF16), shape...  58.7 us
    pallas_call x1, Pallas kernels, attend(): pl.pallas_call(attention_kernel, out_shape=(shape((256, 512), BF16), shap...  15.8 us
    unnamed x11, local copies, waits for them, and re-layouts  4.19 us

profile of v3, /device:TPU:0, one launch (start us, length us, event | category | flops | bytes accessed | tf_op | source)
XLA Modules:
  0.0 147.3 jit_solution(7724045690552012835)
XLA Ops:
  0.6 0.0 copy-start.4
  0.6 0.0 copy-start.2
  0.7 0.8 fusion.1
  1.5 0.5 multiply_cosine_fusion
  2.0 0.1 maximum_bitcast_fusion
  2.2 0.7 pad_maximum_fusion.tables_hbm.tables
  2.9 0.0 copy-start
  2.9 64.3 %gather_weights.1 = (bf16[3,2,4,2,2,4,64,256]{7,6,5,4,3,2,1,0:T(8,128)(2,1)}, bf16[8,512,512]{2,1,0:T(8,128)(2,1)}, bf16[256,512]{1,0:T(8,128)(2,1)}, bf16[8,256,256]{2,1,0:T(8,128)(2,1)}) custom-call(bf16[256,8192]{1,0:T(8,128)(2,1)} %bitcast.12, f32[64,512]{1,0:T(8,128)} %wq_hbm.1, f32[64,128]{1,0:T(8,128)} %wk_hbm.1, f32[64,128]{1,0:T(8,128)} %wv_hbm.1, ...), custom_call_target="tpu_custom_call" | custom-call | tf_op jit(solution)/shard_map/gather_weights/pallas_call | solution.py:291
  67.2 0.0 copy-done.4
  67.2 0.0 copy-done.2
  67.3 0.0 copy-done
  67.3 0.0 copy-start.1
  67.3 1.2 copy-done.1
  68.5 0.0 copy-start.3
  68.5 0.9 copy-done.3
  69.4 15.8 %attend.1 = (bf16[256,512]{1,0:T(8,128)(2,1)}, bf16[256,512]{1,0:T(8,128)(2,1)S(1)}, bf16[8,256,256]{2,1,0:T(8,128)(2,1)S(1)}) custom-call(s32[2048]{0:T(1024)S(1)} %copy-done.4, s32[1,256]{1,0:T(1,128)S(1)} %bitcast.11, bf16[256,512]{1,0:T(8,128)(2,1)S(1)} %copy-done.3, bf16[8,256,256]{2,1,0:T(8,128)(2,1)S(1)} %copy-done.1, bf16[256,512]{1,0:T(8,128)(2,1)S(1)} %bitcast.10, ...), custom_call_target="tpu_custom_call" | custom-call | tf_op jit(solution)/shard_map/attend/pallas_call | solution.py:402
  85.2 58.7 %scatter_grads.1 = (bf16[256,8192]{1,0:T(8,128)(2,1)S(1)}, f32[64,768]{1,0:T(8,128)S(1)}) custom-call(bf16[8,512,512]{2,1,0:T(8,128)(2,1)} %get-tuple-element.17.turned, bf16[3,2,4,2,2,4,64,256]{7,6,5,4,3,2,1,0:T(8,128)(2,1)} %get-tuple-element.18.w_all, bf16[256,512]{1,0:T(8,128)(2,1)S(1)} %get-tuple-element.19.grad_q, ...), custom_call_target="tpu_custom_call" | custom-call | tf_op jit(solution)/shard_map/scatter_grads/pallas_call | solution.py:589
  144.0 0.7 slice.9
  144.6 0.6 fusion.2
  145.3 2.0 %copy.12 = bf16[1,256,8192]{2,1,0:T(8,128)(2,1)} copy(bf16[1,256,8192]{2,1,0:T(8,128)(2,1)S(1)} %bitcast.9) | data formatting | bytes 8388608
  (1 shorter events, 0.0 us)
Async XLA Ops:
  0.6 66.6 %copy-start.4 = (s32[2048]{0:T(1024)S(1)}, s32[2048]{0:T(1024)}, u32[]{:S(2)}) copy-start(s32[2048]{0:T(1024)} %positions.1) | copy-start | bytes 24580
  0.6 66.6 %copy-start.2 = (bf16[1,256,512]{2,1,0:T(8,128)(2,1)S(1)}, bf16[1,256,512]{2,1,0:T(8,128)(2,1)}, u32[]{:S(2)}) copy-start(bf16[1,256,512]{2,1,0:T(8,128)(2,1)} %param.11) | copy-start | bytes 786436
  2.9 64.4 %copy-start = (f32[2,256,128]{2,1,0:T(8,128)S(1)}, f32[2,256,128]{2,1,0:T(8,128)}, u32[]{:S(2)}) copy-start(f32[2,256,128]{2,1,0:T(8,128)} %pad_maximum_fusion.tables_hbm.tables) | copy-start | bytes 786436
  67.3 1.2 copy-start.1
  68.5 0.9 copy-start.3

commit v4 on v3

--- a/solution.py
+++ b/solution.py
@@ -129,8 +129,11 @@
     w[0, x_hi, me["y"], core, x_lo, me["z"]] = wq[:, 0:256].astype(BF16)
     w[1, x_hi, me["y"], core, x_lo, me["z"]] = wq[:, 256:512].astype(BF16)
 
-    def block(n, first, second, third, core_at=core):
+    def block(n, first, second, third, core_at=core, half=None):
         part, row, rows, col, cols, order = PIECES[n]
+        if half is not None:
+            rows = rows // 2
+            row = row + half * rows
         at = dict(zip(order, (first, second, third)))
         x, y, z = (at[axis] for axis in AXES)
         return w.at[
@@ -163,8 +166,17 @@
 
     def send_chunk(n, c):
         chunk = block(n, None, index(n, 1, c), index(n, 2))
-        for by in BYS:
+        for by in (1, -1):
             links.launch((n, 2, c, by), chunk, chunk, to(n, 2, by))
+
+    def pass_on(pieces, c):
+        for n in pieces:
+            second = index(n, 1, c)
+            for half, by in enumerate((1, -1)):
+                third = index(n, 2, -by)
+                links.arrival((n, 2, c, by), block(n, None, second, third))
+                part = block(n, None, second, third, half=half)
+                links.launch((n, 3, c, by), part, part, to(n, 2, by))
 
     for n in everything:
         second, third = index(n, 1), index(n, 2)
@@ -183,8 +195,8 @@
 
     def chunk_in(n, c):
         second = index(n, 1, c)
-        for by in BYS:
-            links.arrival((n, 2, c, by), block(n, None, second, index(n, 2, -by)))
+        for half, by in enumerate((1, -1)):
+            links.arrival((n, 3, c, by), block(n, None, second, index(n, 2, 2), half=half))
         whole = block(n, None, second, None)
         links.launch((n, "twin", c), whole, whole, twin)
 
@@ -210,9 +222,15 @@
         copy.start()
         keep.append(copy)
 
+    pass_on(KV_PIECES, CHUNKS[0])
+    pass_on(Q_PIECES, CHUNKS[0])
+    for c in CHUNKS[1:]:
+        pass_on(KV_PIECES, c)
+    pass_on(Q_PIECES, CHUNKS[1])
     for c in CHUNKS:
         for n in KV_PIECES:
             chunk_in(n, c)
+    pass_on(Q_PIECES, CHUNKS[2])
     for c in CHUNKS:
         for n in KV_PIECES:
             twin_in(n, c)
@@ -264,6 +282,7 @@
         store(10 + k, w.at[1, x_hi, :, :, x_lo], w_out.at[1, x_hi, :, :, x_lo])
         project(c)
 
+    pass_on(Q_PIECES, CHUNKS[3])
     for n in Q_PIECES:
         chunk_in(n, CHUNKS[0])
     lax.fori_loop(4, 8, turn, 0)
@@ -309,8 +328,8 @@
             pltpu.VMEM((2, 256, 128), F32),
             pltpu.VMEM((2, 256, 256), F32),
             pltpu.SemaphoreType.DMA((15,)),
-            pltpu.SemaphoreType.DMA((128,)),
-            pltpu.SemaphoreType.DMA((128,)),
+            pltpu.SemaphoreType.DMA((148,)),
+            pltpu.SemaphoreType.DMA((148,)),
         ],
         compiler_params=pltpu.CompilerParams(
             collective_id=0, has_side_effects=True, vmem_limit_bytes=60 * 2**20
@@ -431,8 +450,9 @@
     ctx = lax.axis_index("ctx")
     twin = device(sibling(me))
     links = Links(send, recv, twin)
-    accs = [buffers[6 * n : 6 * n + 3] for n in range(len(PIECES))]
-    ends = [buffers[6 * n + 3 : 6 * n + 6] for n in range(len(PIECES))]
+    accs = [buffers[7 * n : 7 * n + 3] for n in range(len(PIECES))]
+    ends = [buffers[7 * n + 3 : 7 * n + 6] for n in range(len(PIECES))]
+    vias = [buffers[7 * n + 6] for n in range(len(PIECES))]
     load = pltpu.make_async_copy(turned, held, copy_sem.at[0])
     load.start()
     load_w = pltpu.make_async_copy(w_all, w, copy_sem.at[1])
@@ -466,8 +486,11 @@
             _, row, rows, col, cols, _ = PIECES[n]
             for z in range(4):
                 first, second, third = ({"x": x, "y": y, "z": z}[axis] for axis in axes(n))
-                start = z * 64 + row
-                accs[n][0][first, second, third] = term[start : start + rows, col : col + cols]
+                for half in range(2):
+                    start = z * 64 + row + half * (rows // 2)
+                    accs[n][0][first, half, second, third] = term[
+                        start : start + rows // 2, col : col + cols
+                    ]
 
     CHUNKS = (2, 1, -1, 0)
 
@@ -482,31 +505,51 @@
 
         lax.fori_loop(0, 4, one, 0)
 
-    def send_chunk(n, c):
+    def send_far(n, c):
         j = at(n, 1, c)
-        for s, by in enumerate(BYS):
-            links.launch((n, 0, c, s), accs[n][0].at[at(n, 0, by), j], ends[n][0].at[s, j], to(n, 0, by))
-
-    def summed(n, phase, index):
-        lead = (at(n, phase),) + index
-        total = accs[n][phase][lead].astype(F32)
-        for s in range(3):
-            total = total + ends[n][phase][(s,) + index].astype(F32)
-        return total
+        for d, by in enumerate((1, -1)):
+            src = accs[n][0].at[at(n, 0, 2), d, j]
+            links.launch((n, "via", c, d), src, vias[n].at[d, j], to(n, 0, by))
+
+    def send_near(n, c):
+        j = at(n, 1, c)
+        for d, by in enumerate((1, -1)):
+            src = accs[n][0].at[at(n, 0, by), 1 - d, j]
+            links.launch((n, "end", c, d, 1 - d), src, ends[n][0].at[d, 1 - d, j], to(n, 0, by))
+
+    def relay(n, c):
+        j = at(n, 1, c)
+        acc, via, end = accs[n][0], vias[n], ends[n][0]
+        for d, by in enumerate((1, -1)):
+            links.arrival((n, "via", c, d), via.at[d, j])
+            i = at(n, 0, by)
+            acc[i, d, j] = (acc[i, d, j].astype(F32) + via[d, j].astype(F32)).astype(BF16)
+            links.launch((n, "end", c, d, d), acc.at[i, d, j], end.at[d, d, j], to(n, 0, by))
 
     def chunk_in(n, c):
         j = at(n, 1, c)
-        for s in range(3):
-            links.arrival((n, 0, c, s), ends[n][0].at[s, j])
-        accs[n][1][j] = summed(n, 0, (j,)).astype(BF16)
+        acc, end = accs[n][0], ends[n][0]
+        rows = PIECES[n][2] // 2
+        for h in range(2):
+            for d in range(2):
+                links.arrival((n, "end", c, d, h), end.at[d, h, j])
+            total = acc[at(n, 0), h, j].astype(F32)
+            total = total + end[0, h, j].astype(F32) + end[1, h, j].astype(F32)
+            accs[n][1][j, :, h * rows : h * rows + rows] = total.astype(BF16)
         if c != 0:
             s = BYS.index(c)
             links.launch((n, 1, s), accs[n][1].at[j], ends[n][1].at[s], to(n, 1, c))
 
+    def summed(n, phase):
+        total = accs[n][phase][at(n, phase)].astype(F32)
+        for s in range(3):
+            total = total + ends[n][phase][s].astype(F32)
+        return total
+
     def second(n):
         for s in range(3):
             links.arrival((n, 1, s), ends[n][1].at[s])
-        accs[n][2][...] = summed(n, 1, ()).astype(BF16)
+        accs[n][2][...] = summed(n, 1).astype(BF16)
         for s, by in enumerate(BYS):
             links.launch((n, 2, s), accs[n][2].at[at(n, 2, by)], ends[n][2].at[s], to(n, 2, by))
 
@@ -514,12 +557,18 @@
         part, row, rows, col, cols, _ = PIECES[n]
         for s in range(3):
             links.arrival((n, 2, s), ends[n][2].at[s])
-        out[row : row + rows, part * 256 + col : part * 256 + col + cols] = summed(n, 2, ())
+        out[row : row + rows, part * 256 + col : part * 256 + col + cols] = summed(n, 2)
 
     for c in CHUNKS:
         for n in Q_PIECES:
             products(n, c)
-            send_chunk(n, c)
+            send_far(n, c)
+    for c in CHUNKS:
+        for n in Q_PIECES:
+            send_near(n, c)
+    for c in CHUNKS:
+        for n in Q_PIECES:
+            relay(n, c)
 
     load_w.wait()
 
@@ -560,20 +609,26 @@
         return 0
 
     lax.fori_loop(0, 16, kv_product, 0)
-    for c in CHUNKS:
-        for n in KV_PIECES:
-            send_chunk(n, c)
+    for step in (send_far, send_near):
+        for c in CHUNKS:
+            for n in KV_PIECES:
+                step(n, c)
     for k, c in enumerate(CHUNKS):
         for n in Q_PIECES:
             chunk_in(n, c)
+        for n in KV_PIECES:
+            relay(n, c)
         if k < 3:
             inputs(k + 1)
+    for n in Q_PIECES:
+        second(n)
     for c in CHUNKS:
         for n in KV_PIECES:
             chunk_in(n, c)
-    for step in (second, last):
-        for n in Q_PIECES + KV_PIECES:
-            step(n)
+    for n in KV_PIECES:
+        second(n)
+    for n in Q_PIECES + KV_PIECES:
+        last(n)
     for copy in stores:
         copy.wait()
     links.finish()
@@ -584,8 +639,12 @@
     shape = jax.ShapeDtypeStruct
     buffers = []
     for _, _, rows, _, cols, _ in PIECES:
-        for lead in ((4, 4, 4), (4, 4), (4,), (3, 4, 4), (3, 4), (3,)):
-            buffers.append(pltpu.VMEM(lead + (rows, cols), BF16))
+        half, whole = (rows // 2, cols), (rows, cols)
+        for shape_of in (
+            (4, 2, 4, 4) + half, (4, 4) + whole, (4,) + whole,
+            (2, 2, 4, 4) + half, (3, 4) + whole, (3,) + whole, (2, 4, 4) + half,
+        ):
+            buffers.append(pltpu.VMEM(shape_of, BF16))
     return pl.pallas_call(
         scatter_kernel,
         out_shape=(shape((256, 8192), BF16), shape((64, 768), F32)),
@@ -598,8 +657,8 @@
             pltpu.VMEM((7, 256, 256), BF16),
             pltpu.VMEM((256, 8192), BF16),
             pltpu.SemaphoreType.DMA((6,)),
-            pltpu.SemaphoreType.DMA((100,)),
-            pltpu.SemaphoreType.DMA((100,)),
+            pltpu.SemaphoreType.DMA((160,)),
+            pltpu.SemaphoreType.DMA((160,)),
             *buffers,
         ],
         compiler_params=pltpu.CompilerParams(

time: 147 us -> 144 us (0.980)
  Pallas kernels: 139 us -> 136 us
    pallas_call x1, Pallas kernels: 58.7 us -> 54.8 us  [scatter_grads(): pl.pallas_call(scatter_kernel, out_shape=(shape((256, 8192), BF16), shape...]
where the time goes in v4:
time: 144 us
  Pallas kernels  136 us (94%)
  local copies, waits for them, and re-layouts  5.49 us (4%)
  other arithmetic  2.21 us (2%)
    pallas_call x1, Pallas kernels, gather_weights(): pl.pallas_call(gather_kernel, out_shape=(shape((3, 2, 4, 2, 2, 4, 64, 256...  65.1 us
    pallas_call x1, Pallas kernels, scatter_grads(): pl.pallas_call(scatter_kernel, out_shape=(shape((256, 8192), BF16), shape...  54.8 us
    pallas_call x1, Pallas kernels, attend(): pl.pallas_call(attention_kernel, out_shape=(shape((256, 512), BF16), shap...  15.8 us
    unnamed x11, local copies, waits for them, and re-layouts  4.19 us

profile of v4, /device:TPU:0, one launch (start us, length us, event | category | flops | bytes accessed | tf_op | source)
XLA Modules:
  0.0 144.0 jit_solution(18282085148419186733)
XLA Ops:
  0.6 0.0 copy-start.4
  0.6 0.0 copy-start.2
  0.7 0.8 fusion.1
  1.5 0.5 multiply_cosine_fusion
  2.0 0.1 maximum_bitcast_fusion
  2.2 0.7 pad_maximum_fusion.tables_hbm.tables
  2.9 0.0 copy-start
  2.9 65.1 %gather_weights.1 = (bf16[3,2,4,2,2,4,64,256]{7,6,5,4,3,2,1,0:T(8,128)(2,1)}, bf16[8,512,512]{2,1,0:T(8,128)(2,1)}, bf16[256,512]{1,0:T(8,128)(2,1)}, bf16[8,256,256]{2,1,0:T(8,128)(2,1)}) custom-call(bf16[256,8192]{1,0:T(8,128)(2,1)} %bitcast.12, f32[64,512]{1,0:T(8,128)} %wq_hbm.1, f32[64,128]{1,0:T(8,128)} %wk_hbm.1, f32[64,128]{1,0:T(8,128)} %wv_hbm.1, ...), custom_call_target="tpu_custom_call" | custom-call | tf_op jit(solution)/shard_map/gather_weights/pallas_call | solution.py:310
  68.0 0.0 copy-done.4
  68.0 0.0 copy-done.2
  68.0 0.0 copy-done
  68.0 0.0 copy-start.1
  68.0 1.2 copy-done.1
  69.2 0.0 copy-start.3
  69.2 0.9 copy-done.3
  70.2 15.8 %attend.1 = (bf16[256,512]{1,0:T(8,128)(2,1)}, bf16[256,512]{1,0:T(8,128)(2,1)S(1)}, bf16[8,256,256]{2,1,0:T(8,128)(2,1)S(1)}) custom-call(s32[2048]{0:T(1024)S(1)} %copy-done.4, s32[1,256]{1,0:T(1,128)S(1)} %bitcast.11, bf16[256,512]{1,0:T(8,128)(2,1)S(1)} %copy-done.3, bf16[8,256,256]{2,1,0:T(8,128)(2,1)S(1)} %copy-done.1, bf16[256,512]{1,0:T(8,128)(2,1)S(1)} %bitcast.10, ...), custom_call_target="tpu_custom_call" | custom-call | tf_op jit(solution)/shard_map/attend/pallas_call | solution.py:421
  85.9 54.8 %scatter_grads.1 = (bf16[256,8192]{1,0:T(8,128)(2,1)S(1)}, f32[64,768]{1,0:T(8,128)S(1)}) custom-call(bf16[8,512,512]{2,1,0:T(8,128)(2,1)} %get-tuple-element.17.turned, bf16[3,2,4,2,2,4,64,256]{7,6,5,4,3,2,1,0:T(8,128)(2,1)} %get-tuple-element.18.w_all, bf16[256,512]{1,0:T(8,128)(2,1)S(1)} %get-tuple-element.19.grad_q, ...), custom_call_target="tpu_custom_call" | custom-call | tf_op jit(solution)/shard_map/scatter_grads/pallas_call | solution.py:648
  140.7 0.7 slice.9
  141.4 0.6 fusion.2
  142.0 2.0 %copy.12 = bf16[1,256,8192]{2,1,0:T(8,128)(2,1)} copy(bf16[1,256,8192]{2,1,0:T(8,128)(2,1)S(1)} %bitcast.9) | data formatting | bytes 8388608
  (1 shorter events, 0.0 us)
Async XLA Ops:
  0.6 67.3 %copy-start.4 = (s32[2048]{0:T(1024)S(1)}, s32[2048]{0:T(1024)}, u32[]{:S(2)}) copy-start(s32[2048]{0:T(1024)} %positions.1) | copy-start | bytes 24580
  0.6 67.3 %copy-start.2 = (bf16[1,256,512]{2,1,0:T(8,128)(2,1)S(1)}, bf16[1,256,512]{2,1,0:T(8,128)(2,1)}, u32[]{:S(2)}) copy-start(bf16[1,256,512]{2,1,0:T(8,128)(2,1)} %param.11) | copy-start | bytes 786436
  2.9 65.1 %copy-start = (f32[2,256,128]{2,1,0:T(8,128)S(1)}, f32[2,256,128]{2,1,0:T(8,128)}, u32[]{:S(2)}) copy-start(f32[2,256,128]{2,1,0:T(8,128)} %pad_maximum_fusion.tables_hbm.tables) | copy-start | bytes 786436
  68.0 1.2 copy-start.1
  69.2 0.9 copy-start.3

commit v5 on v4

--- a/solution.py
+++ b/solution.py
@@ -14,14 +14,18 @@
 F32 = jnp.float32
 AXES = ("x", "y", "z")
 PIECES = (
-    (2, 0, 64, 0, 128, ("y", "x", "z")),
-    (2, 0, 32, 128, 128, ("z", "y", "x")),
-    (2, 32, 32, 128, 128, ("z", "x", "y")),
-    (0, 0, 64, 0, 256, ("z", "y", "x")),
-    (1, 0, 64, 0, 256, ("z", "x", "y")),
+    (2, 0, 48, 0, 128, ("z", "y", "x")),
+    (2, 0, 48, 128, 128, ("x", "z", "y")),
+    (2, 48, 16, 0, 256, ("y", "x", "z")),
+    (0, 0, 64, 0, 128, ("z", "y", "x")),
+    (0, 0, 64, 128, 128, ("x", "z", "y")),
+    (1, 0, 64, 0, 128, ("y", "x", "z")),
+    (1, 0, 32, 128, 128, ("y", "z", "x")),
+    (1, 32, 32, 128, 128, ("z", "x", "y")),
 )
 KV_PIECES = (0, 1, 2)
-Q_PIECES = (3, 4)
+Q_PIECES = (3, 4, 5, 6, 7)
+Q_PARTS = ((3, 4), (5, 6, 7))
 SCALE = 128 ** (-0.5)
 LOG2E = 1.4426950408889634
 
@@ -107,7 +111,7 @@
 def gather_kernel(
     tokens, wq_hbm, wk_hbm, wv_hbm, tables_hbm,
     w_out, turned_out, q_out, kv_out,
-    w, tok, twin_tok, turned, wq, wk, wv, tables, sums, copy_sem, send, recv,
+    w, tok, twin_tok, turned, wq, wk, wv, tables, copy_sem, send, recv,
 ):
     me = place()
     core = me["core"]
@@ -166,7 +170,7 @@
 
     def send_chunk(n, c):
         chunk = block(n, None, index(n, 1, c), index(n, 2))
-        for by in (1, -1):
+        for by in BYS if n in KV_PIECES else (1, -1):
             links.launch((n, 2, c, by), chunk, chunk, to(n, 2, by))
 
     def pass_on(pieces, c):
@@ -195,8 +199,12 @@
 
     def chunk_in(n, c):
         second = index(n, 1, c)
-        for half, by in enumerate((1, -1)):
-            links.arrival((n, 3, c, by), block(n, None, second, index(n, 2, 2), half=half))
+        if n in KV_PIECES:
+            for by in BYS:
+                links.arrival((n, 2, c, by), block(n, None, second, index(n, 2, -by)))
+        else:
+            for half, by in enumerate((1, -1)):
+                links.arrival((n, 3, c, by), block(n, None, second, index(n, 2, 2), half=half))
         whole = block(n, None, second, None)
         links.launch((n, "twin", c), whole, whole, twin)
 
@@ -222,26 +230,27 @@
         copy.start()
         keep.append(copy)
 
-    pass_on(KV_PIECES, CHUNKS[0])
+    for n in KV_PIECES:
+        chunk_in(n, CHUNKS[0])
     pass_on(Q_PIECES, CHUNKS[0])
     for c in CHUNKS[1:]:
-        pass_on(KV_PIECES, c)
-    pass_on(Q_PIECES, CHUNKS[1])
-    for c in CHUNKS:
         for n in KV_PIECES:
             chunk_in(n, c)
-    pass_on(Q_PIECES, CHUNKS[2])
+    pass_on(Q_PIECES, CHUNKS[1])
     for c in CHUNKS:
         for n in KV_PIECES:
             twin_in(n, c)
     store(5, w.at[2], w_out.at[2])
 
-    def add_kv(k, total):
-        lhs = tok[:, pl.ds(pl.multiple_of(k * 2048, 2048), 2048)]
-        rows = w[2, lax.div(k, 2), pl.ds(lax.rem(k, 2) * 2, 2)].reshape(2048, 256)
-        return total + jnp.dot(lhs, rows, preferred_element_type=F32)
-
-    both = lax.fori_loop(0, 4, add_kv, jnp.zeros((256, 256), F32))
+    def project(part):
+        def add(k, total):
+            lhs = tok[:, pl.ds(pl.multiple_of(k * 2048, 2048), 2048)]
+            rows = w[part, lax.div(k, 2), pl.ds(lax.rem(k, 2) * 2, 2)].reshape(2048, 256)
+            return total + jnp.dot(lhs, rows, preferred_element_type=F32)
+
+        return lax.fori_loop(0, 4, add, jnp.zeros((256, 256), F32))
+
+    both = project(2)
     cos, sin = tables[0], tables[1]
     ctx = lax.axis_index("ctx")
     key = both[:, 0:128]
@@ -251,50 +260,21 @@
     for k in (4, 2, 6, 1, 3, 5, 7):
         links.launch(("kv", k), kv_out.at[ctx], kv_out.at[ctx], peers[k - 1])
 
-    def project(c):
-        y = index(3, 1, c)
-        total = None
-        for x_hi in range(2):
-            lhs = tok[:, pl.ds(pl.multiple_of((x_hi * 4 + y) * 1024, 1024), 1024)]
-            term = jnp.dot(lhs, w[0, x_hi, y].reshape(1024, 256), preferred_element_type=F32)
-            total = term if total is None else total + term
-        sums[0] = total if c == CHUNKS[0] else sums[0] + total
-        x = index(4, 1, c)
-        x_hi, x_lo = lax.div(x, 2), lax.rem(x, 2)
-        total = None
-        for y in range(4):
-            for half in range(2):
-                at = (x_hi * 4 + y) * 1024 + half * 512 + x_lo * 256
-                lhs = tok[:, pl.ds(pl.multiple_of(at, 256), 256)]
-                rows = w[1, x_hi, y, half, x_lo].reshape(256, 256)
-                term = jnp.dot(lhs, rows, preferred_element_type=F32)
-                total = term if total is None else total + term
-        sums[1] = total if c == CHUNKS[0] else sums[1] + total
-
-    def finish_chunk(c):
+    pass_on(Q_PIECES, CHUNKS[2])
+    pass_on(Q_PIECES, CHUNKS[3])
+    lax.fori_loop(4, 8, turn, 0)
+    store(8, turned, turned_out)
+    for c in CHUNKS:
         for n in Q_PIECES:
-            twin_in(n, c)
-        k = CHUNKS.index(c)
-        y = index(3, 1, c)
-        store(6 + k, w.at[0, :, y], w_out.at[0, :, y])
-        x = index(4, 1, c)
-        x_hi, x_lo = lax.div(x, 2), lax.rem(x, 2)
-        store(10 + k, w.at[1, x_hi, :, :, x_lo], w_out.at[1, x_hi, :, :, x_lo])
-        project(c)
-
-    pass_on(Q_PIECES, CHUNKS[3])
-    for n in Q_PIECES:
-        chunk_in(n, CHUNKS[0])
-    lax.fori_loop(4, 8, turn, 0)
-    store(14, turned, turned_out)
-    for k in range(1, 4):
-        for n in Q_PIECES:
-            chunk_in(n, CHUNKS[k])
-        finish_chunk(CHUNKS[k - 1])
-    finish_chunk(CHUNKS[3])
+            chunk_in(n, c)
     for part in range(2):
+        for c in CHUNKS:
+            for n in Q_PARTS[part]:
+                twin_in(n, c)
+        store(6 + part, w.at[part], w_out.at[part])
+        both = project(part)
         for h in range(2):
-            query = sums[part, :, h * 128 : h * 128 + 128]
+            query = both[:, h * 128 : h * 128 + 128]
             rotated = (query * cos + turn_half(query) * sin).astype(BF16)
             q_out[:, part * 256 + h * 128 : part * 256 + h * 128 + 128] = rotated
     for k in range(1, 8):
@@ -326,10 +306,9 @@
             pltpu.VMEM((64, 128), F32),
             pltpu.VMEM((64, 128), F32),
             pltpu.VMEM((2, 256, 128), F32),
-            pltpu.VMEM((2, 256, 256), F32),
-            pltpu.SemaphoreType.DMA((15,)),
-            pltpu.SemaphoreType.DMA((148,)),
-            pltpu.SemaphoreType.DMA((148,)),
+            pltpu.SemaphoreType.DMA((9,)),
+            pltpu.SemaphoreType.DMA((212,)),
+            pltpu.SemaphoreType.DMA((212,)),
         ],
         compiler_params=pltpu.CompilerParams(
             collective_id=0, has_side_effects=True, vmem_limit_bytes=60 * 2**20
@@ -339,15 +318,22 @@
 
 
 def attention_kernel(
-    positions, own_positions, q, kv, grad, tables,
+    positions, own_positions, q_hbm, kv_hbm, grad, tables,
     attention, grad_q, terms,
-    qs, gs, gs_t, keys_t, values_t, scores, top, total, att_t, gq_t,
+    q, kv, load_sem, qs, gs, gs_t, keys_t, values_t, scores, top, total, att_t, gq_t,
 ):
+    load_kv = pltpu.make_async_copy(kv_hbm, kv, load_sem.at[0])
+    load_q = pltpu.make_async_copy(q_hbm, q, load_sem.at[1])
+    load_kv.start()
+    load_q.start()
     for h in range(4):
         rows = slice(h * 256, h * 256 + 256)
-        qs[rows] = q[:, h * 128 : h * 128 + 128]
         gs[rows] = grad[:, h * 128 : h * 128 + 128]
         gs_t[:, rows] = grad[:, h * 128 : h * 128 + 128].T
+    load_q.wait()
+    for h in range(4):
+        qs[h * 256 : h * 256 + 256] = q[:, h * 128 : h * 128 + 128]
+    load_kv.wait()
     for k in range(8):
         cols = slice(k * 256, k * 256 + 256)
         keys_t[:, cols] = kv[k, :, 0:128].T
@@ -416,14 +402,17 @@
 
 
 def attend(positions, own_positions, q, kv, grad, tables):
-    vmem = pl.BlockSpec(memory_space=pltpu.VMEM)
+    vmem, anywhere = pl.BlockSpec(memory_space=pltpu.VMEM), pl.BlockSpec(memory_space=pl.ANY)
     shape = jax.ShapeDtypeStruct
     return pl.pallas_call(
         attention_kernel,
         out_shape=(shape((256, 512), BF16), shape((256, 512), BF16), shape((8, 256, 256), BF16)),
-        in_specs=[pl.BlockSpec(memory_space=pltpu.SMEM)] + [vmem] * 5,
+        in_specs=[pl.BlockSpec(memory_space=pltpu.SMEM), vmem, anywhere, anywhere, vmem, vmem],
         out_specs=(vmem, vmem, vmem),
         scratch_shapes=[
+            pltpu.VMEM((256, 512), BF16),
+            pltpu.VMEM((8, 256, 256), BF16),
+            pltpu.SemaphoreType.DMA((2,)),
             pltpu.VMEM((1024, 128), BF16),
             pltpu.VMEM((1024, 128), BF16),
             pltpu.VMEM((128, 1024), BF16),
@@ -435,7 +424,7 @@
             pltpu.VMEM((128, 1024), F32),
             pltpu.VMEM((128, 1024), F32),
         ],
-        compiler_params=pltpu.CompilerParams(vmem_limit_bytes=32 * 2**20),
+        compiler_params=pltpu.CompilerParams(vmem_limit_bytes=60 * 2**20),
         name="attend",
     )(positions, own_positions, q, kv, grad, tables)
 
@@ -486,6 +475,10 @@
             _, row, rows, col, cols, _ = PIECES[n]
             for z in range(4):
                 first, second, third = ({"x": x, "y": y, "z": z}[axis] for axis in axes(n))
+                start = z * 64 + row
+                if n in KV_PIECES:
+                    accs[n][0][first, second, third] = term[start : start + rows, col : col + cols]
+                    continue
                 for half in range(2):
                     start = z * 64 + row + half * (rows // 2)
                     accs[n][0][first, half, second, third] = term[
@@ -494,16 +487,18 @@
 
     CHUNKS = (2, 1, -1, 0)
 
-    def products(n, c):
-        axis, other = axes(n)[:2]
+    def products(pieces):
+        def one(k, _):
+            product(pieces, lax.div(k, 4), lax.rem(k, 4))
+            return 0
+
+        lax.fori_loop(0, 16, one, 0)
+
+    def send_direct(n, c):
         j = at(n, 1, c)
-
-        def one(i, _):
-            where = {axis: i, other: j}
-            product((n,), where["x"], where["y"])
-            return 0
-
-        lax.fori_loop(0, 4, one, 0)
+        for s, by in enumerate(BYS):
+            src = accs[n][0].at[at(n, 0, by), j]
+            links.launch((n, 0, c, s), src, ends[n][0].at[s, j], to(n, 0, by))
 
     def send_far(n, c):
         j = at(n, 1, c)
@@ -530,7 +525,14 @@
         j = at(n, 1, c)
         acc, end = accs[n][0], ends[n][0]
         rows = PIECES[n][2] // 2
-        for h in range(2):
+        if n in KV_PIECES:
+            for s in range(3):
+                links.arrival((n, 0, c, s), end.at[s, j])
+            total = acc[at(n, 0), j].astype(F32)
+            for s in range(3):
+                total = total + end[s, j].astype(F32)
+            accs[n][1][j] = total.astype(BF16)
+        for h in range(2) if n in Q_PIECES else ():
             for d in range(2):
                 links.arrival((n, "end", c, d, h), end.at[d, h, j])
             total = acc[at(n, 0), h, j].astype(F32)
@@ -559,10 +561,11 @@
             links.arrival((n, 2, s), ends[n][2].at[s])
         out[row : row + rows, part * 256 + col : part * 256 + col + cols] = summed(n, 2)
 
-    for c in CHUNKS:
-        for n in Q_PIECES:
-            products(n, c)
-            send_far(n, c)
+    for pieces in Q_PARTS:
+        products(pieces)
+        for c in CHUNKS:
+            for n in pieces:
+                send_far(n, c)
     for c in CHUNKS:
         for n in Q_PIECES:
             send_near(n, c)
@@ -604,20 +607,13 @@
     inputs(0)
     links.arrival("grad_kv", grads.at[1, :, columns])
 
-    def kv_product(k, _):
-        product(KV_PIECES, lax.div(k, 4), lax.rem(k, 4))
-        return 0
-
-    lax.fori_loop(0, 16, kv_product, 0)
-    for step in (send_far, send_near):
-        for c in CHUNKS:
-            for n in KV_PIECES:
-                step(n, c)
+    products(KV_PIECES)
+    for c in CHUNKS:
+        for n in KV_PIECES:
+            send_direct(n, c)
     for k, c in enumerate(CHUNKS):
         for n in Q_PIECES:
             chunk_in(n, c)
-        for n in KV_PIECES:
-            relay(n, c)
         if k < 3:
             inputs(k + 1)
     for n in Q_PIECES:
@@ -638,12 +634,14 @@
     vmem, anywhere = pl.BlockSpec(memory_space=pltpu.VMEM), pl.BlockSpec(memory_space=pl.ANY)
     shape = jax.ShapeDtypeStruct
     buffers = []
-    for _, _, rows, _, cols, _ in PIECES:
+    for n, (_, _, rows, _, cols, _) in enumerate(PIECES):
         half, whole = (rows // 2, cols), (rows, cols)
-        for shape_of in (
-            (4, 2, 4, 4) + half, (4, 4) + whole, (4,) + whole,
-            (2, 2, 4, 4) + half, (3, 4) + whole, (3,) + whole, (2, 4, 4) + half,
-        ):
+        later = ((4, 4) + whole, (4,) + whole), ((3, 4) + whole, (3,) + whole)
+        if n in KV_PIECES:
+            first = (4, 4, 4) + whole, (3, 4, 4) + whole, (8, 128)
+        else:
+            first = (4, 2, 4, 4) + half, (2, 2, 4, 4) + half, (2, 4, 4) + half
+        for shape_of in (first[0], *later[0], first[1], *later[1], first[2]):
             buffers.append(pltpu.VMEM(shape_of, BF16))
     return pl.pallas_call(
         scatter_kernel,
@@ -657,8 +655,8 @@
             pltpu.VMEM((7, 256, 256), BF16),
             pltpu.VMEM((256, 8192), BF16),
             pltpu.SemaphoreType.DMA((6,)),
-            pltpu.SemaphoreType.DMA((160,)),
-            pltpu.SemaphoreType.DMA((160,)),
+            pltpu.SemaphoreType.DMA((216,)),
+            pltpu.SemaphoreType.DMA((216,)),
             *buffers,
         ],
         compiler_params=pltpu.CompilerParams(

time: 144 us -> 143 us (level)
  Pallas kernels: 136 us -> 134 us
    pallas_call x1, Pallas kernels: 65.1 us -> 58.6 us  [gather_weights(): pl.pallas_call(gather_kernel, out_shape=(shape((3, 2, 4, 2, 2, 4, 64, 256...]
    pallas_call x1, Pallas kernels: 15.8 us -> 18.4 us  [attend(): pl.pallas_call(attention_kernel, out_shape=(shape((256, 512), BF16), shap...]
    pallas_call x1, Pallas kernels: 54.8 us -> 56.7 us  [scatter_grads(): pl.pallas_call(scatter_kernel, out_shape=(shape((256, 8192), BF16), shape...]
    unnamed x11 -> x7, local copies, waits for them, and re-layouts: 4.19 us -> 4.19 us
where the time goes in v5:
time: 143 us
  Pallas kernels  134 us (94%)
  local copies, waits for them, and re-layouts  5.48 us (4%)
  other arithmetic  2.73 us (2%)
    pallas_call x1, Pallas kernels, gather_weights(): pl.pallas_call(gather_kernel, out_shape=(shape((3, 2, 4, 2, 2, 4, 64, 256...  58.6 us
    pallas_call x1, Pallas kernels, scatter_grads(): pl.pallas_call(scatter_kernel, out_shape=(shape((256, 8192), BF16), shape...  56.7 us
    pallas_call x1, Pallas kernels, attend(): pl.pallas_call(attention_kernel, out_shape=(shape((256, 512), BF16), shap...  18.4 us
    unnamed x7, local copies, waits for them, and re-layouts  4.19 us

profile of v5, /device:TPU:0, one launch (start us, length us, event | category | flops | bytes accessed | tf_op | source)
XLA Modules:
  0.0 142.6 jit_solution(14281261115987995360)
XLA Ops:
  0.6 1.3 fusion.1
  2.0 0.5 multiply_cosine_fusion
  2.5 0.1 maximum_bitcast_fusion
  2.7 0.7 pad_maximum_fusion.tables_hbm.tables
  3.4 0.0 copy-start
  3.4 58.6 %gather_weights.1 = (bf16[3,2,4,2,2,4,64,256]{7,6,5,4,3,2,1,0:T(8,128)(2,1)}, bf16[8,512,512]{2,1,0:T(8,128)(2,1)}, bf16[256,512]{1,0:T(8,128)(2,1)}, bf16[8,256,256]{2,1,0:T(8,128)(2,1)}) custom-call(bf16[256,8192]{1,0:T(8,128)(2,1)} %bitcast.10, f32[64,512]{1,0:T(8,128)} %wq_hbm.1, f32[64,128]{1,0:T(8,128)} %wk_hbm.1, f32[64,128]{1,0:T(8,128)} %wv_hbm.1, ...), custom_call_target="tpu_custom_call" | custom-call | tf_op jit(solution)/shard_map/gather_weights/pallas_call | solution.py:290
  62.0 18.4 %attend.1 = (bf16[256,512]{1,0:T(8,128)(2,1)}, bf16[256,512]{1,0:T(8,128)(2,1)}, bf16[8,256,256]{2,1,0:T(8,128)(2,1)}) custom-call(s32[2048]{0:T(1024)} %positions.1, s32[1,256]{1,0:T(1,128)} %bitcast.12, bf16[256,512]{1,0:T(8,128)(2,1)} %get-tuple-element.14.q_hbm, bf16[8,256,256]{2,1,0:T(8,128)(2,1)} %get-tuple-element.15.kv_hbm, ...), custom_call_target="tpu_custom_call" | custom-call | tf_op jit(solution)/shard_map/attend/pallas_call | solution.py:407
  80.4 0.0 copy-done
  80.4 0.0 copy-start.1
  80.4 1.2 copy-done.1
  81.6 0.0 copy-start.2
  81.6 0.9 copy-done.2
  82.6 56.7 %scatter_grads.1 = (bf16[256,8192]{1,0:T(8,128)(2,1)S(1)}, f32[64,768]{1,0:T(8,128)S(1)}) custom-call(bf16[8,512,512]{2,1,0:T(8,128)(2,1)} %get-tuple-element.17.turned, bf16[3,2,4,2,2,4,64,256]{7,6,5,4,3,2,1,0:T(8,128)(2,1)} %get-tuple-element.18.w_all, bf16[256,512]{1,0:T(8,128)(2,1)S(1)} %copy-done.2, bf16[8,256,256]{2,1,0:T(8,128)(2,1)S(1)} %copy-done.1, ...), custom_call_target="tpu_custom_call" | custom-call | tf_op jit(solution)/shard_map/scatter_grads/pallas_call | solution.py:646
  139.3 0.7 slice.9
  140.0 0.6 fusion.2
  140.6 2.0 %copy.12 = bf16[1,256,8192]{2,1,0:T(8,128)(2,1)} copy(bf16[1,256,8192]{2,1,0:T(8,128)(2,1)S(1)} %bitcast.9) | data formatting | bytes 8388608
  (1 shorter events, 0.0 us)
Async XLA Ops:
  3.4 77.0 %copy-start = (f32[2,256,128]{2,1,0:T(8,128)S(1)}, f32[2,256,128]{2,1,0:T(8,128)}, u32[]{:S(2)}) copy-start(f32[2,256,128]{2,1,0:T(8,128)} %pad_maximum_fusion.tables_hbm.tables) | copy-start | bytes 786436
  80.4 1.2 copy-start.1
  81.6 0.9 copy-start.2

commit v6 on v5

--- a/solution.py
+++ b/solution.py
@@ -182,18 +182,19 @@
                 part = block(n, None, second, third, half=half)
                 links.launch((n, 3, c, by), part, part, to(n, 2, by))
 
-    for n in everything:
-        second, third = index(n, 1), index(n, 2)
-        for by in BYS:
-            links.arrival((n, 0, by), block(n, index(n, 0, -by), second, third))
-        line = block(n, None, second, third)
-        for by in BYS:
-            links.launch((n, 1, by), line, line, to(n, 1, by))
-        send_chunk(n, 0)
-    for n in everything:
-        for by in BYS:
-            links.arrival((n, 1, by), block(n, None, index(n, 1, -by), index(n, 2)))
-            send_chunk(n, -by)
+    for pieces in (KV_PIECES, Q_PIECES):
+        for n in pieces:
+            second, third = index(n, 1), index(n, 2)
+            for by in BYS:
+                links.arrival((n, 0, by), block(n, index(n, 0, -by), second, third))
+            line = block(n, None, second, third)
+            for by in BYS:
+                links.launch((n, 1, by), line, line, to(n, 1, by))
+            send_chunk(n, 0)
+        for n in pieces:
+            for by in BYS:
+                links.arrival((n, 1, by), block(n, None, index(n, 1, -by), index(n, 2)))
+                send_chunk(n, -by)
 
     CHUNKS = (0,) + tuple(-by for by in BYS)
 
@@ -318,22 +319,15 @@
 
 
 def attention_kernel(
-    positions, own_positions, q_hbm, kv_hbm, grad, tables,
+    positions, own_positions, q, kv, grad, tables,
     attention, grad_q, terms,
-    q, kv, load_sem, qs, gs, gs_t, keys_t, values_t, scores, top, total, att_t, gq_t,
+    qs, gs, gs_t, keys_t, values_t, scores, top, total, att_t, gq_t,
 ):
-    load_kv = pltpu.make_async_copy(kv_hbm, kv, load_sem.at[0])
-    load_q = pltpu.make_async_copy(q_hbm, q, load_sem.at[1])
-    load_kv.start()
-    load_q.start()
     for h in range(4):
         rows = slice(h * 256, h * 256 + 256)
+        qs[rows] = q[:, h * 128 : h * 128 + 128]
         gs[rows] = grad[:, h * 128 : h * 128 + 128]
         gs_t[:, rows] = grad[:, h * 128 : h * 128 + 128].T
-    load_q.wait()
-    for h in range(4):
-        qs[h * 256 : h * 256 + 256] = q[:, h * 128 : h * 128 + 128]
-    load_kv.wait()
     for k in range(8):
         cols = slice(k * 256, k * 256 + 256)
         keys_t[:, cols] = kv[k, :, 0:128].T
@@ -402,17 +396,14 @@
 
 
 def attend(positions, own_positions, q, kv, grad, tables):
-    vmem, anywhere = pl.BlockSpec(memory_space=pltpu.VMEM), pl.BlockSpec(memory_space=pl.ANY)
+    vmem = pl.BlockSpec(memory_space=pltpu.VMEM)
     shape = jax.ShapeDtypeStruct
     return pl.pallas_call(
         attention_kernel,
         out_shape=(shape((256, 512), BF16), shape((256, 512), BF16), shape((8, 256, 256), BF16)),
-        in_specs=[pl.BlockSpec(memory_space=pltpu.SMEM), vmem, anywhere, anywhere, vmem, vmem],
+        in_specs=[pl.BlockSpec(memory_space=pltpu.SMEM)] + [vmem] * 5,
         out_specs=(vmem, vmem, vmem),
         scratch_shapes=[
-            pltpu.VMEM((256, 512), BF16),
-            pltpu.VMEM((8, 256, 256), BF16),
-            pltpu.SemaphoreType.DMA((2,)),
             pltpu.VMEM((1024, 128), BF16),
             pltpu.VMEM((1024, 128), BF16),
             pltpu.VMEM((128, 1024), BF16),
@@ -424,7 +415,7 @@
             pltpu.VMEM((128, 1024), F32),
             pltpu.VMEM((128, 1024), F32),
         ],
-        compiler_params=pltpu.CompilerParams(vmem_limit_bytes=60 * 2**20),
+        compiler_params=pltpu.CompilerParams(vmem_limit_bytes=32 * 2**20),
         name="attend",
     )(positions, own_positions, q, kv, grad, tables)
 
@@ -571,9 +562,8 @@
             send_near(n, c)
     for c in CHUNKS:
         for n in Q_PIECES:
-            relay(n, c)
-
-    load_w.wait()
+            if axes(n)[0] != "z":
+                relay(n, c)
 
     def input_slice(k, _):
         total = None
@@ -604,6 +594,11 @@
     grads[0, :, 640:768] = keyval[:, 128:256].astype(BF16)
     columns = pl.ds(512, 256)
     links.launch("grad_kv", grads.at[0, :, columns], grads.at[1, :, columns], twin)
+    for c in CHUNKS:
+        for n in Q_PIECES:
+            if axes(n)[0] == "z":
+                relay(n, c)
+    load_w.wait()
     inputs(0)
     links.arrival("grad_kv", grads.at[1, :, columns])
 

time: 143 us -> 143 us (level)
    pallas_call x1, Pallas kernels: 58.6 us -> 63.8 us  [gather_weights(): pl.pallas_call(gather_kernel, out_shape=(shape((3, 2, 4, 2, 2, 4, 64, 256...]
    pallas_call x1, Pallas kernels: 18.4 us -> 15.8 us  [attend(): pl.pallas_call(attention_kernel, out_shape=(shape((256, 512), BF16), shap...]
    pallas_call x1, Pallas kernels: 56.7 us -> 54.7 us  [scatter_grads(): pl.pallas_call(scatter_kernel, out_shape=(shape((256, 8192), BF16), shape...]
    unnamed x7 -> x11, local copies, waits for them, and re-layouts: 4.19 us -> 4.19 us
where the time goes in v6:
time: 143 us
  Pallas kernels  134 us (94%)
  local copies, waits for them, and re-layouts  5.49 us (4%)
  other arithmetic  2.21 us (2%)
    pallas_call x1, Pallas kernels, gather_weights(): pl.pallas_call(gather_kernel, out_shape=(shape((3, 2, 4, 2, 2, 4, 64, 256...  63.8 us
    pallas_call x1, Pallas kernels, scatter_grads(): pl.pallas_call(scatter_kernel, out_shape=(shape((256, 8192), BF16), shape...  54.7 us
    pallas_call x1, Pallas kernels, attend(): pl.pallas_call(attention_kernel, out_shape=(shape((256, 512), BF16), shap...  15.8 us
    unnamed x11, local copies, waits for them, and re-layouts  4.19 us

profile of v6, /device:TPU:0, one launch (start us, length us, event | category | flops | bytes accessed | tf_op | source)
XLA Modules:
  0.0 142.7 jit_solution(15258915867898439209)
XLA Ops:
  0.6 0.0 copy-start.4
  0.6 0.0 copy-start.2
  0.7 0.8 fusion.1
  1.5 0.5 multiply_cosine_fusion
  2.0 0.1 maximum_bitcast_fusion
  2.2 0.7 pad_maximum_fusion.tables_hbm.tables
  2.9 0.0 copy-start
  2.9 63.8 %gather_weights.1 = (bf16[3,2,4,2,2,4,64,256]{7,6,5,4,3,2,1,0:T(8,128)(2,1)}, bf16[8,512,512]{2,1,0:T(8,128)(2,1)}, bf16[256,512]{1,0:T(8,128)(2,1)}, bf16[8,256,256]{2,1,0:T(8,128)(2,1)}) custom-call(bf16[256,8192]{1,0:T(8,128)(2,1)} %bitcast.12, f32[64,512]{1,0:T(8,128)} %wq_hbm.1, f32[64,128]{1,0:T(8,128)} %wk_hbm.1, f32[64,128]{1,0:T(8,128)} %wv_hbm.1, ...), custom_call_target="tpu_custom_call" | custom-call | tf_op jit(solution)/shard_map/gather_weights/pallas_call | solution.py:291
  66.7 0.0 copy-done.4
  66.7 0.0 copy-done.2
  66.7 0.0 copy-done
  66.7 0.0 copy-start.1
  66.7 1.2 copy-done.1
  68.0 0.0 copy-start.3
  68.0 0.9 copy-done.3
  68.9 15.8 %attend.1 = (bf16[256,512]{1,0:T(8,128)(2,1)}, bf16[256,512]{1,0:T(8,128)(2,1)S(1)}, bf16[8,256,256]{2,1,0:T(8,128)(2,1)S(1)}) custom-call(s32[2048]{0:T(1024)S(1)} %copy-done.4, s32[1,256]{1,0:T(1,128)S(1)} %bitcast.11, bf16[256,512]{1,0:T(8,128)(2,1)S(1)} %copy-done.3, bf16[8,256,256]{2,1,0:T(8,128)(2,1)S(1)} %copy-done.1, bf16[256,512]{1,0:T(8,128)(2,1)S(1)} %bitcast.10, ...), custom_call_target="tpu_custom_call" | custom-call | tf_op jit(solution)/shard_map/attend/pallas_call | solution.py:401
  84.7 54.7 %scatter_grads.1 = (bf16[256,8192]{1,0:T(8,128)(2,1)S(1)}, f32[64,768]{1,0:T(8,128)S(1)}) custom-call(bf16[8,512,512]{2,1,0:T(8,128)(2,1)} %get-tuple-element.17.turned, bf16[3,2,4,2,2,4,64,256]{7,6,5,4,3,2,1,0:T(8,128)(2,1)} %get-tuple-element.18.w_all, bf16[256,512]{1,0:T(8,128)(2,1)S(1)} %get-tuple-element.19.grad_q, ...), custom_call_target="tpu_custom_call" | custom-call | tf_op jit(solution)/shard_map/scatter_grads/pallas_call | solution.py:641
  139.4 0.7 slice.9
  140.0 0.6 fusion.2
  140.7 2.0 %copy.12 = bf16[1,256,8192]{2,1,0:T(8,128)(2,1)} copy(bf16[1,256,8192]{2,1,0:T(8,128)(2,1)S(1)} %bitcast.9) | data formatting | bytes 8388608
  (1 shorter events, 0.0 us)
Async XLA Ops:
  0.6 66.1 %copy-start.4 = (s32[2048]{0:T(1024)S(1)}, s32[2048]{0:T(1024)}, u32[]{:S(2)}) copy-start(s32[2048]{0:T(1024)} %positions.1) | copy-start | bytes 24580
  0.6 66.1 %copy-start.2 = (bf16[1,256,512]{2,1,0:T(8,128)(2,1)S(1)}, bf16[1,256,512]{2,1,0:T(8,128)(2,1)}, u32[]{:S(2)}) copy-start(bf16[1,256,512]{2,1,0:T(8,128)(2,1)} %param.11) | copy-start | bytes 786436
  2.9 63.8 %copy-start = (f32[2,256,128]{2,1,0:T(8,128)S(1)}, f32[2,256,128]{2,1,0:T(8,128)}, u32[]{:S(2)}) copy-start(f32[2,256,128]{2,1,0:T(8,128)} %pad_maximum_fusion.tables_hbm.tables) | copy-start | bytes 786436
  66.7 1.2 copy-start.1
  68.0 0.9 copy-start.3

commit v7 on v6

--- a/solution.py
+++ b/solution.py
@@ -133,11 +133,8 @@
     w[0, x_hi, me["y"], core, x_lo, me["z"]] = wq[:, 0:256].astype(BF16)
     w[1, x_hi, me["y"], core, x_lo, me["z"]] = wq[:, 256:512].astype(BF16)
 
-    def block(n, first, second, third, core_at=core, half=None):
+    def block(n, first, second, third, core_at=core):
         part, row, rows, col, cols, order = PIECES[n]
-        if half is not None:
-            rows = rows // 2
-            row = row + half * rows
         at = dict(zip(order, (first, second, third)))
         x, y, z = (at[axis] for axis in AXES)
         return w.at[
@@ -170,42 +167,28 @@
 
     def send_chunk(n, c):
         chunk = block(n, None, index(n, 1, c), index(n, 2))
-        for by in BYS if n in KV_PIECES else (1, -1):
+        for by in BYS:
             links.launch((n, 2, c, by), chunk, chunk, to(n, 2, by))
 
-    def pass_on(pieces, c):
-        for n in pieces:
-            second = index(n, 1, c)
-            for half, by in enumerate((1, -1)):
-                third = index(n, 2, -by)
-                links.arrival((n, 2, c, by), block(n, None, second, third))
-                part = block(n, None, second, third, half=half)
-                links.launch((n, 3, c, by), part, part, to(n, 2, by))
-
-    for pieces in (KV_PIECES, Q_PIECES):
-        for n in pieces:
-            second, third = index(n, 1), index(n, 2)
-            for by in BYS:
-                links.arrival((n, 0, by), block(n, index(n, 0, -by), second, third))
-            line = block(n, None, second, third)
-            for by in BYS:
-                links.launch((n, 1, by), line, line, to(n, 1, by))
-            send_chunk(n, 0)
-        for n in pieces:
-            for by in BYS:
-                links.arrival((n, 1, by), block(n, None, index(n, 1, -by), index(n, 2)))
-                send_chunk(n, -by)
+    for n in everything:
+        second, third = index(n, 1), index(n, 2)
+        for by in BYS:
+            links.arrival((n, 0, by), block(n, index(n, 0, -by), second, third))
+        line = block(n, None, second, third)
+        for by in BYS:
+            links.launch((n, 1, by), line, line, to(n, 1, by))
+        send_chunk(n, 0)
+    for n in everything:
+        for by in BYS:
+            links.arrival((n, 1, by), block(n, None, index(n, 1, -by), index(n, 2)))
+            send_chunk(n, -by)
 
     CHUNKS = (0,) + tuple(-by for by in BYS)
 
     def chunk_in(n, c):
         second = index(n, 1, c)
-        if n in KV_PIECES:
-            for by in BYS:
-                links.arrival((n, 2, c, by), block(n, None, second, index(n, 2, -by)))
-        else:
-            for half, by in enumerate((1, -1)):
-                links.arrival((n, 3, c, by), block(n, None, second, index(n, 2, 2), half=half))
+        for by in BYS:
+            links.arrival((n, 2, c, by), block(n, None, second, index(n, 2, -by)))
         whole = block(n, None, second, None)
         links.launch((n, "twin", c), whole, whole, twin)
 
@@ -231,13 +214,9 @@
         copy.start()
         keep.append(copy)
 
-    for n in KV_PIECES:
-        chunk_in(n, CHUNKS[0])
-    pass_on(Q_PIECES, CHUNKS[0])
-    for c in CHUNKS[1:]:
+    for c in CHUNKS:
         for n in KV_PIECES:
             chunk_in(n, c)
-    pass_on(Q_PIECES, CHUNKS[1])
     for c in CHUNKS:
         for n in KV_PIECES:
             twin_in(n, c)
@@ -261,8 +240,6 @@
     for k in (4, 2, 6, 1, 3, 5, 7):
         links.launch(("kv", k), kv_out.at[ctx], kv_out.at[ctx], peers[k - 1])
 
-    pass_on(Q_PIECES, CHUNKS[2])
-    pass_on(Q_PIECES, CHUNKS[3])
     lax.fori_loop(4, 8, turn, 0)
     store(8, turned, turned_out)
     for c in CHUNKS:
@@ -336,24 +313,28 @@
     lead = own_positions[...] - lax.broadcasted_iota(jnp.int32, (128, 256), 0)
     top[...] = jnp.full(top.shape, MASKED, F32)
 
+    def tile(k, cols):
+        return kv[pl.ds(k * 2, 2), :, cols].reshape(512, 128)
+
     def score(k, _):
         for h in range(4):
             cols = slice(h * 256, h * 256 + 256)
-            s = lax.dot_general(kv[k, :, 0:128], qs[cols], nt, preferred_element_type=F32)
-            upper = jnp.where(lead >= positions[k * 256], s[0:128], MASKED)
-            lower = jnp.where(lead >= positions[k * 256 + 128], s[128:256], MASKED)
-            scores[k, 0:128, cols] = upper
-            scores[k, 128:256, cols] = lower
-            high = jnp.max(jnp.maximum(upper, lower), axis=0, keepdims=True)
-            top[:, cols] = jnp.maximum(top[:, cols], high)
+            s = lax.dot_general(tile(k, slice(0, 128)), qs[cols], nt, preferred_element_type=F32)
+            high = None
+            for r in range(4):
+                rows = slice(r * 128, r * 128 + 128)
+                run = jnp.where(lead >= positions[k * 512 + r * 128], s[rows], MASKED)
+                scores[k, rows, cols] = run
+                high = run if high is None else jnp.maximum(high, run)
+            top[:, cols] = jnp.maximum(top[:, cols], jnp.max(high, axis=0, keepdims=True))
         return 0
 
-    lax.fori_loop(0, 8, score, 0)
+    lax.fori_loop(0, 4, score, 0)
     total[...] = jnp.zeros(total.shape, F32)
     att_t[...] = jnp.zeros(att_t.shape, F32)
 
     def weigh(k, _):
-        at = pl.ds(pl.multiple_of(k * 256, 256), 256)
+        at = pl.ds(pl.multiple_of(k * 512, 512), 512)
         for h in range(4):
             cols = slice(h * 256, h * 256 + 256)
             weight = jnp.exp2((scores[k, :, cols] - top[:, cols]) * (SCALE * LOG2E))
@@ -362,7 +343,7 @@
             att_t[:, cols] += jnp.dot(values_t[:, at], weight.astype(BF16), preferred_element_type=F32)
         return 0
 
-    lax.fori_loop(0, 8, weigh, 0)
+    lax.fori_loop(0, 4, weigh, 0)
     for h in range(4):
         cols = slice(h * 256, h * 256 + 256)
         inverse = 1.0 / total[:, cols]
@@ -373,22 +354,22 @@
     gq_t[...] = jnp.zeros(gq_t.shape, F32)
 
     def back(k, _):
-        at = pl.ds(pl.multiple_of(k * 256, 256), 256)
-        key_term = jnp.zeros((256, 128), F32)
-        value_term = jnp.zeros((256, 128), F32)
+        at = pl.ds(pl.multiple_of(k * 512, 512), 512)
+        key_term = jnp.zeros((512, 128), F32)
+        value_term = jnp.zeros((512, 128), F32)
         for h in range(4):
             cols = slice(h * 256, h * 256 + 256)
             probs = scores[k, :, cols] * total[:, cols]
-            grad_probs = lax.dot_general(kv[k, :, 128:256], gs[cols], nt, preferred_element_type=F32)
+            grad_probs = lax.dot_general(tile(k, slice(128, 256)), gs[cols], nt, preferred_element_type=F32)
             dscore = (probs * (grad_probs - top[:, cols])).astype(BF16)
             key_term += jnp.dot(dscore, qs[cols], preferred_element_type=F32)
             value_term += jnp.dot(probs.astype(BF16), gs[cols], preferred_element_type=F32)
             gq_t[:, cols] += jnp.dot(keys_t[:, at], dscore, preferred_element_type=F32)
-        terms[k, :, 0:128] = (key_term * SCALE).astype(BF16)
-        terms[k, :, 128:256] = value_term.astype(BF16)
+        terms[pl.ds(k * 2, 2), :, 0:128] = (key_term * SCALE).astype(BF16).reshape(2, 256, 128)
+        terms[pl.ds(k * 2, 2), :, 128:256] = value_term.astype(BF16).reshape(2, 256, 128)
         return 0
 
-    lax.fori_loop(0, 8, back, 0)
+    lax.fori_loop(0, 4, back, 0)
     for h in range(4):
         a = gq_t[:, h * 256 : h * 256 + 256].T * SCALE
         unrotated = a * tables[0] - turn_half(a) * tables[1]
@@ -409,7 +390,7 @@
             pltpu.VMEM((128, 1024), BF16),
             pltpu.VMEM((128, 2048), BF16),
             pltpu.VMEM((128, 2048), BF16),
-            pltpu.VMEM((8, 256, 1024), F32),
+            pltpu.VMEM((4, 512, 1024), F32),
             pltpu.VMEM((1, 1024), F32),
             pltpu.VMEM((1, 1024), F32),
             pltpu.VMEM((128, 1024), F32),

time: 143 us -> 133 us (0.930)
  Pallas kernels: 134 us -> 125 us
    pallas_call x1, Pallas kernels: 63.8 us -> 57.6 us  [gather_weights(): pl.pallas_call(gather_kernel, out_shape=(shape((3, 2, 4, 2, 2, 4, 64, 256...]
    pallas_call x1, Pallas kernels: 15.8 us -> 11.6 us  [attend(): pl.pallas_call(attention_kernel, out_shape=(shape((256, 512), BF16), shap...]
where the time goes in v7:
time: 133 us
  Pallas kernels  125 us (94%)
  local copies, waits for them, and re-layouts  5.49 us (4%)
  other arithmetic  2.21 us (2%)
    pallas_call x1, Pallas kernels, gather_weights(): pl.pallas_call(gather_kernel, out_shape=(shape((3, 2, 4, 2, 2, 4, 64, 256...  57.6 us
    pallas_call x1, Pallas kernels, scatter_grads(): pl.pallas_call(scatter_kernel, out_shape=(shape((256, 8192), BF16), shape...  55.6 us
    pallas_call x1, Pallas kernels, attend(): pl.pallas_call(attention_kernel, out_shape=(shape((256, 512), BF16), shap...  11.6 us
    unnamed x11, local copies, waits for them, and re-layouts  4.19 us

profile of v7, /device:TPU:0, one launch (start us, length us, event | category | flops | bytes accessed | tf_op | source)
XLA Modules:
  0.0 133.2 jit_solution(7365630392597310336)
XLA Ops:
  0.6 0.0 copy-start.4
  0.6 0.0 copy-start.2
  0.7 0.8 fusion.1
  1.5 0.5 multiply_cosine_fusion
  2.0 0.1 maximum_bitcast_fusion
  2.2 0.7 pad_maximum_fusion.tables_hbm.tables
  2.9 0.0 copy-start
  2.9 57.6 %gather_weights.1 = (bf16[3,2,4,2,2,4,64,256]{7,6,5,4,3,2,1,0:T(8,128)(2,1)}, bf16[8,512,512]{2,1,0:T(8,128)(2,1)}, bf16[256,512]{1,0:T(8,128)(2,1)}, bf16[8,256,256]{2,1,0:T(8,128)(2,1)}) custom-call(bf16[256,8192]{1,0:T(8,128)(2,1)} %bitcast.12, f32[64,512]{1,0:T(8,128)} %wq_hbm.1, f32[64,128]{1,0:T(8,128)} %wk_hbm.1, f32[64,128]{1,0:T(8,128)} %wv_hbm.1, ...), custom_call_target="tpu_custom_call" | custom-call | tf_op jit(solution)/shard_map/gather_weights/pallas_call | solution.py:268
  60.5 0.0 copy-done.4
  60.5 0.0 copy-done.2
  60.5 0.0 copy-done
  60.5 0.0 copy-start.1
  60.5 1.2 copy-done.1
  61.8 0.0 copy-start.3
  61.8 0.9 copy-done.3
  62.7 11.6 %attend.1 = (bf16[256,512]{1,0:T(8,128)(2,1)}, bf16[256,512]{1,0:T(8,128)(2,1)S(1)}, bf16[8,256,256]{2,1,0:T(8,128)(2,1)S(1)}) custom-call(s32[2048]{0:T(1024)S(1)} %copy-done.4, s32[1,256]{1,0:T(1,128)S(1)} %bitcast.11, bf16[256,512]{1,0:T(8,128)(2,1)S(1)} %copy-done.3, bf16[8,256,256]{2,1,0:T(8,128)(2,1)S(1)} %copy-done.1, bf16[256,512]{1,0:T(8,128)(2,1)S(1)} %bitcast.10, ...), custom_call_target="tpu_custom_call" | custom-call | tf_op jit(solution)/shard_map/attend/pallas_call | solution.py:382
  74.3 55.6 %scatter_grads.1 = (bf16[256,8192]{1,0:T(8,128)(2,1)S(1)}, f32[64,768]{1,0:T(8,128)S(1)}) custom-call(bf16[8,512,512]{2,1,0:T(8,128)(2,1)} %get-tuple-element.17.turned, bf16[3,2,4,2,2,4,64,256]{7,6,5,4,3,2,1,0:T(8,128)(2,1)} %get-tuple-element.18.w_all, bf16[256,512]{1,0:T(8,128)(2,1)S(1)} %get-tuple-element.19.grad_q, ...), custom_call_target="tpu_custom_call" | custom-call | tf_op jit(solution)/shard_map/scatter_grads/pallas_call | solution.py:622
  129.9 0.7 slice.9
  130.6 0.6 fusion.2
  131.2 2.0 %copy.12 = bf16[1,256,8192]{2,1,0:T(8,128)(2,1)} copy(bf16[1,256,8192]{2,1,0:T(8,128)(2,1)S(1)} %bitcast.9) | data formatting | bytes 8388608
  (1 shorter events, 0.0 us)
Async XLA Ops:
  0.6 59.9 %copy-start.4 = (s32[2048]{0:T(1024)S(1)}, s32[2048]{0:T(1024)}, u32[]{:S(2)}) copy-start(s32[2048]{0:T(1024)} %positions.1) | copy-start | bytes 24580
  0.6 59.9 %copy-start.2 = (bf16[1,256,512]{2,1,0:T(8,128)(2,1)S(1)}, bf16[1,256,512]{2,1,0:T(8,128)(2,1)}, u32[]{:S(2)}) copy-start(bf16[1,256,512]{2,1,0:T(8,128)(2,1)} %param.11) | copy-start | bytes 786436
  2.9 57.6 %copy-start = (f32[2,256,128]{2,1,0:T(8,128)S(1)}, f32[2,256,128]{2,1,0:T(8,128)}, u32[]{:S(2)}) copy-start(f32[2,256,128]{2,1,0:T(8,128)} %pad_maximum_fusion.tables_hbm.tables) | copy-start | bytes 786436
  60.5 1.2 copy-start.1
  61.8 0.9 copy-start.3

commit v8 on v7

--- a/solution.py
+++ b/solution.py
@@ -242,10 +242,14 @@
 
     lax.fori_loop(4, 8, turn, 0)
     store(8, turned, turned_out)
-    for c in CHUNKS:
-        for n in Q_PIECES:
+    for n in Q_PIECES[:3]:
+        for c in CHUNKS:
             chunk_in(n, c)
     for part in range(2):
+        if part == 1:
+            for c in CHUNKS:
+                for n in Q_PIECES[3:]:
+                    chunk_in(n, c)
         for c in CHUNKS:
             for n in Q_PARTS[part]:
                 twin_in(n, c)
@@ -314,27 +318,27 @@
     top[...] = jnp.full(top.shape, MASKED, F32)
 
     def tile(k, cols):
-        return kv[pl.ds(k * 2, 2), :, cols].reshape(512, 128)
+        return kv[pl.ds(k * 4, 4), :, cols].reshape(1024, 128)
 
     def score(k, _):
         for h in range(4):
             cols = slice(h * 256, h * 256 + 256)
             s = lax.dot_general(tile(k, slice(0, 128)), qs[cols], nt, preferred_element_type=F32)
             high = None
-            for r in range(4):
+            for r in range(8):
                 rows = slice(r * 128, r * 128 + 128)
-                run = jnp.where(lead >= positions[k * 512 + r * 128], s[rows], MASKED)
+                run = jnp.where(lead >= positions[k * 1024 + r * 128], s[rows], MASKED)
                 scores[k, rows, cols] = run
                 high = run if high is None else jnp.maximum(high, run)
             top[:, cols] = jnp.maximum(top[:, cols], jnp.max(high, axis=0, keepdims=True))
         return 0
 
-    lax.fori_loop(0, 4, score, 0)
+    lax.fori_loop(0, 2, score, 0)
     total[...] = jnp.zeros(total.shape, F32)
     att_t[...] = jnp.zeros(att_t.shape, F32)
 
     def weigh(k, _):
-        at = pl.ds(pl.multiple_of(k * 512, 512), 512)
+        at = pl.ds(pl.multiple_of(k * 1024, 1024), 1024)
         for h in range(4):
             cols = slice(h * 256, h * 256 + 256)
             weight = jnp.exp2((scores[k, :, cols] - top[:, cols]) * (SCALE * LOG2E))
@@ -343,7 +347,7 @@
             att_t[:, cols] += jnp.dot(values_t[:, at], weight.astype(BF16), preferred_element_type=F32)
         return 0
 
-    lax.fori_loop(0, 4, weigh, 0)
+    lax.fori_loop(0, 2, weigh, 0)
     for h in range(4):
         cols = slice(h * 256, h * 256 + 256)
         inverse = 1.0 / total[:, cols]
@@ -354,9 +358,9 @@
     gq_t[...] = jnp.zeros(gq_t.shape, F32)
 
     def back(k, _):
-        at = pl.ds(pl.multiple_of(k * 512, 512), 512)
-        key_term = jnp.zeros((512, 128), F32)
-        value_term = jnp.zeros((512, 128), F32)
+        at = pl.ds(pl.multiple_of(k * 1024, 1024), 1024)
+        key_term = jnp.zeros((1024, 128), F32)
+        value_term = jnp.zeros((1024, 128), F32)
         for h in range(4):
             cols = slice(h * 256, h * 256 + 256)
             probs = scores[k, :, cols] * total[:, cols]
@@ -365,11 +369,11 @@
             key_term += jnp.dot(dscore, qs[cols], preferred_element_type=F32)
             value_term += jnp.dot(probs.astype(BF16), gs[cols], preferred_element_type=F32)
             gq_t[:, cols] += jnp.dot(keys_t[:, at], dscore, preferred_element_type=F32)
-        terms[pl.ds(k * 2, 2), :, 0:128] = (key_term * SCALE).astype(BF16).reshape(2, 256, 128)
-        terms[pl.ds(k * 2, 2), :, 128:256] = value_term.astype(BF16).reshape(2, 256, 128)
+        terms[pl.ds(k * 4, 4), :, 0:128] = (key_term * SCALE).astype(BF16).reshape(4, 256, 128)
+        terms[pl.ds(k * 4, 4), :, 128:256] = value_term.astype(BF16).reshape(4, 256, 128)
         return 0
 
-    lax.fori_loop(0, 4, back, 0)
+    lax.fori_loop(0, 2, back, 0)
     for h in range(4):
         a = gq_t[:, h * 256 : h * 256 + 256].T * SCALE
         unrotated = a * tables[0] - turn_half(a) * tables[1]
@@ -390,7 +394,7 @@
             pltpu.VMEM((128, 1024), BF16),
             pltpu.VMEM((128, 2048), BF16),
             pltpu.VMEM((128, 2048), BF16),
-            pltpu.VMEM((4, 512, 1024), F32),
+            pltpu.VMEM((2, 1024, 1024), F32),
             pltpu.VMEM((1, 1024), F32),
             pltpu.VMEM((1, 1024), F32),
             pltpu.VMEM((128, 1024), F32),
@@ -411,9 +415,8 @@
     ctx = lax.axis_index("ctx")
     twin = device(sibling(me))
     links = Links(send, recv, twin)
-    accs = [buffers[7 * n : 7 * n + 3] for n in range(len(PIECES))]
-    ends = [buffers[7 * n + 3 : 7 * n + 6] for n in range(len(PIECES))]
-    vias = [buffers[7 * n + 6] for n in range(len(PIECES))]
+    accs = [buffers[6 * n : 6 * n + 3] for n in range(len(PIECES))]
+    ends = [buffers[6 * n + 3 : 6 * n + 6] for n in range(len(PIECES))]
     load = pltpu.make_async_copy(turned, held, copy_sem.at[0])
     load.start()
     load_w = pltpu.make_async_copy(w_all, w, copy_sem.at[1])
@@ -448,14 +451,7 @@
             for z in range(4):
                 first, second, third = ({"x": x, "y": y, "z": z}[axis] for axis in axes(n))
                 start = z * 64 + row
-                if n in KV_PIECES:
-                    accs[n][0][first, second, third] = term[start : start + rows, col : col + cols]
-                    continue
-                for half in range(2):
-                    start = z * 64 + row + half * (rows // 2)
-                    accs[n][0][first, half, second, third] = term[
-                        start : start + rows // 2, col : col + cols
-                    ]
+                accs[n][0][first, second, third] = term[start : start + rows, col : col + cols]
 
     CHUNKS = (2, 1, -1, 0)
 
@@ -472,44 +468,15 @@
             src = accs[n][0].at[at(n, 0, by), j]
             links.launch((n, 0, c, s), src, ends[n][0].at[s, j], to(n, 0, by))
 
-    def send_far(n, c):
-        j = at(n, 1, c)
-        for d, by in enumerate((1, -1)):
-            src = accs[n][0].at[at(n, 0, 2), d, j]
-            links.launch((n, "via", c, d), src, vias[n].at[d, j], to(n, 0, by))
-
-    def send_near(n, c):
-        j = at(n, 1, c)
-        for d, by in enumerate((1, -1)):
-            src = accs[n][0].at[at(n, 0, by), 1 - d, j]
-            links.launch((n, "end", c, d, 1 - d), src, ends[n][0].at[d, 1 - d, j], to(n, 0, by))
-
-    def relay(n, c):
-        j = at(n, 1, c)
-        acc, via, end = accs[n][0], vias[n], ends[n][0]
-        for d, by in enumerate((1, -1)):
-            links.arrival((n, "via", c, d), via.at[d, j])
-            i = at(n, 0, by)
-            acc[i, d, j] = (acc[i, d, j].astype(F32) + via[d, j].astype(F32)).astype(BF16)
-            links.launch((n, "end", c, d, d), acc.at[i, d, j], end.at[d, d, j], to(n, 0, by))
-
     def chunk_in(n, c):
         j = at(n, 1, c)
         acc, end = accs[n][0], ends[n][0]
-        rows = PIECES[n][2] // 2
-        if n in KV_PIECES:
-            for s in range(3):
-                links.arrival((n, 0, c, s), end.at[s, j])
-            total = acc[at(n, 0), j].astype(F32)
-            for s in range(3):
-                total = total + end[s, j].astype(F32)
-            accs[n][1][j] = total.astype(BF16)
-        for h in range(2) if n in Q_PIECES else ():
-            for d in range(2):
-                links.arrival((n, "end", c, d, h), end.at[d, h, j])
-            total = acc[at(n, 0), h, j].astype(F32)
-            total = total + end[0, h, j].astype(F32) + end[1, h, j].astype(F32)
-            accs[n][1][j, :, h * rows : h * rows + rows] = total.astype(BF16)
+        for s in range(3):
+            links.arrival((n, 0, c, s), end.at[s, j])
+        total = acc[at(n, 0), j].astype(F32)
+        for s in range(3):
+            total = total + end[s, j].astype(F32)
+        accs[n][1][j] = total.astype(BF16)
         if c != 0:
             s = BYS.index(c)
             links.launch((n, 1, s), accs[n][1].at[j], ends[n][1].at[s], to(n, 1, c))
@@ -537,14 +504,7 @@
         products(pieces)
         for c in CHUNKS:
             for n in pieces:
-                send_far(n, c)
-    for c in CHUNKS:
-        for n in Q_PIECES:
-            send_near(n, c)
-    for c in CHUNKS:
-        for n in Q_PIECES:
-            if axes(n)[0] != "z":
-                relay(n, c)
+                send_direct(n, c)
 
     def input_slice(k, _):
         total = None
@@ -575,10 +535,6 @@
     grads[0, :, 640:768] = keyval[:, 128:256].astype(BF16)
     columns = pl.ds(512, 256)
     links.launch("grad_kv", grads.at[0, :, columns], grads.at[1, :, columns], twin)
-    for c in CHUNKS:
-        for n in Q_PIECES:
-            if axes(n)[0] == "z":
-                relay(n, c)
     load_w.wait()
     inputs(0)
     links.arrival("grad_kv", grads.at[1, :, columns])
@@ -610,15 +566,9 @@
     vmem, anywhere = pl.BlockSpec(memory_space=pltpu.VMEM), pl.BlockSpec(memory_space=pl.ANY)
     shape = jax.ShapeDtypeStruct
     buffers = []
-    for n, (_, _, rows, _, cols, _) in enumerate(PIECES):
-        half, whole = (rows // 2, cols), (rows, cols)
-        later = ((4, 4) + whole, (4,) + whole), ((3, 4) + whole, (3,) + whole)
-        if n in KV_PIECES:
-            first = (4, 4, 4) + whole, (3, 4, 4) + whole, (8, 128)
-        else:
-            first = (4, 2, 4, 4) + half, (2, 2, 4, 4) + half, (2, 4, 4) + half
-        for shape_of in (first[0], *later[0], first[1], *later[1], first[2]):
-            buffers.append(pltpu.VMEM(shape_of, BF16))
+    for _, _, rows, _, cols, _ in PIECES:
+        for lead in ((4, 4, 4), (4, 4), (4,), (3, 4, 4), (3, 4), (3,)):
+            buffers.append(pltpu.VMEM(lead + (rows, cols), BF16))
     return pl.pallas_call(
         scatter_kernel,
         out_shape=(shape((256, 8192), BF16), shape((64, 768), F32)),

time: 133 us -> 135 us (1.015)
  Pallas kernels: 125 us -> 127 us
    pallas_call x1, Pallas kernels: 55.6 us -> 59.4 us  [scatter_grads(): pl.pallas_call(scatter_kernel, out_shape=(shape((256, 8192), BF16), shape...]
    pallas_call x1, Pallas kernels: 11.6 us -> 9.5 us  [attend(): pl.pallas_call(attention_kernel, out_shape=(shape((256, 512), BF16), shap...]
where the time goes in v8:
time: 135 us
  Pallas kernels  127 us (94%)
  local copies, waits for them, and re-layouts  5.49 us (4%)
  other arithmetic  2.21 us (2%)
    pallas_call x1, Pallas kernels, scatter_grads(): pl.pallas_call(scatter_kernel, out_shape=(shape((256, 8192), BF16), shape...  59.4 us
    pallas_call x1, Pallas kernels, gather_weights(): pl.pallas_call(gather_kernel, out_shape=(shape((3, 2, 4, 2, 2, 4, 64, 256...  57.6 us
    pallas_call x1, Pallas kernels, attend(): pl.pallas_call(attention_kernel, out_shape=(shape((256, 512), BF16), shap...  9.5 us
    unnamed x11, local copies, waits for them, and re-layouts  4.19 us

profile of v8, /device:TPU:0, one launch (start us, length us, event | category | flops | bytes accessed | tf_op | source)
XLA Modules:
  0.0 135.0 jit_solution(1708155839207293430)
XLA Ops:
  0.6 0.0 copy-start.4
  0.6 0.0 copy-start.2
  0.7 0.8 fusion.1
  1.5 0.5 multiply_cosine_fusion
  2.0 0.1 maximum_bitcast_fusion
  2.2 0.7 pad_maximum_fusion.tables_hbm.tables
  2.9 0.0 copy-start
  2.9 57.6 %gather_weights.1 = (bf16[3,2,4,2,2,4,64,256]{7,6,5,4,3,2,1,0:T(8,128)(2,1)}, bf16[8,512,512]{2,1,0:T(8,128)(2,1)}, bf16[256,512]{1,0:T(8,128)(2,1)}, bf16[8,256,256]{2,1,0:T(8,128)(2,1)}) custom-call(bf16[256,8192]{1,0:T(8,128)(2,1)} %bitcast.12, f32[64,512]{1,0:T(8,128)} %wq_hbm.1, f32[64,128]{1,0:T(8,128)} %wk_hbm.1, f32[64,128]{1,0:T(8,128)} %wv_hbm.1, ...), custom_call_target="tpu_custom_call" | custom-call | tf_op jit(solution)/shard_map/gather_weights/pallas_call | solution.py:272
  60.5 0.0 copy-done.4
  60.5 0.0 copy-done.2
  60.5 0.0 copy-done
  60.5 0.0 copy-start.1
  60.5 1.2 copy-done.1
  61.8 0.0 copy-start.3
  61.8 0.9 copy-done.3
  62.7 9.5 %attend.1 = (bf16[256,512]{1,0:T(8,128)(2,1)}, bf16[256,512]{1,0:T(8,128)(2,1)S(1)}, bf16[8,256,256]{2,1,0:T(8,128)(2,1)S(1)}) custom-call(s32[2048]{0:T(1024)S(1)} %copy-done.4, s32[1,256]{1,0:T(1,128)S(1)} %bitcast.11, bf16[256,512]{1,0:T(8,128)(2,1)S(1)} %copy-done.3, bf16[8,256,256]{2,1,0:T(8,128)(2,1)S(1)} %copy-done.1, bf16[256,512]{1,0:T(8,128)(2,1)S(1)} %bitcast.10, ...), custom_call_target="tpu_custom_call" | custom-call | tf_op jit(solution)/shard_map/attend/pallas_call | solution.py:386
  72.2 59.4 %scatter_grads.1 = (bf16[256,8192]{1,0:T(8,128)(2,1)S(1)}, f32[64,768]{1,0:T(8,128)S(1)}) custom-call(bf16[8,512,512]{2,1,0:T(8,128)(2,1)} %get-tuple-element.17.turned, bf16[3,2,4,2,2,4,64,256]{7,6,5,4,3,2,1,0:T(8,128)(2,1)} %get-tuple-element.18.w_all, bf16[256,512]{1,0:T(8,128)(2,1)S(1)} %get-tuple-element.19.grad_q, ...), custom_call_target="tpu_custom_call" | custom-call | tf_op jit(solution)/shard_map/scatter_grads/pallas_call | solution.py:572
  131.7 0.7 slice.9
  132.3 0.6 fusion.2
  132.9 2.0 %copy.12 = bf16[1,256,8192]{2,1,0:T(8,128)(2,1)} copy(bf16[1,256,8192]{2,1,0:T(8,128)(2,1)S(1)} %bitcast.9) | data formatting | bytes 8388608
  (1 shorter events, 0.0 us)
Async XLA Ops:
  0.6 59.9 %copy-start.4 = (s32[2048]{0:T(1024)S(1)}, s32[2048]{0:T(1024)}, u32[]{:S(2)}) copy-start(s32[2048]{0:T(1024)} %positions.1) | copy-start | bytes 24580
  0.6 59.9 %copy-start.2 = (bf16[1,256,512]{2,1,0:T(8,128)(2,1)S(1)}, bf16[1,256,512]{2,1,0:T(8,128)(2,1)}, u32[]{:S(2)}) copy-start(bf16[1,256,512]{2,1,0:T(8,128)(2,1)} %param.11) | copy-start | bytes 786436
  2.9 57.6 %copy-start = (f32[2,256,128]{2,1,0:T(8,128)S(1)}, f32[2,256,128]{2,1,0:T(8,128)}, u32[]{:S(2)}) copy-start(f32[2,256,128]{2,1,0:T(8,128)} %pad_maximum_fusion.tables_hbm.tables) | copy-start | bytes 786436
  60.5 1.2 copy-start.1
  61.8 0.9 copy-start.3

commit v9 on v7

--- a/solution.py
+++ b/solution.py
@@ -242,10 +242,14 @@
 
     lax.fori_loop(4, 8, turn, 0)
     store(8, turned, turned_out)
-    for c in CHUNKS:
-        for n in Q_PIECES:
+    for n in Q_PIECES[:3]:
+        for c in CHUNKS:
             chunk_in(n, c)
     for part in range(2):
+        if part == 1:
+            for c in CHUNKS:
+                for n in Q_PIECES[3:]:
+                    chunk_in(n, c)
         for c in CHUNKS:
             for n in Q_PARTS[part]:
                 twin_in(n, c)
@@ -314,27 +318,27 @@
     top[...] = jnp.full(top.shape, MASKED, F32)
 
     def tile(k, cols):
-        return kv[pl.ds(k * 2, 2), :, cols].reshape(512, 128)
+        return kv[pl.ds(k * 4, 4), :, cols].reshape(1024, 128)
 
     def score(k, _):
         for h in range(4):
             cols = slice(h * 256, h * 256 + 256)
             s = lax.dot_general(tile(k, slice(0, 128)), qs[cols], nt, preferred_element_type=F32)
             high = None
-            for r in range(4):
+            for r in range(8):
                 rows = slice(r * 128, r * 128 + 128)
-                run = jnp.where(lead >= positions[k * 512 + r * 128], s[rows], MASKED)
+                run = jnp.where(lead >= positions[k * 1024 + r * 128], s[rows], MASKED)
                 scores[k, rows, cols] = run
                 high = run if high is None else jnp.maximum(high, run)
             top[:, cols] = jnp.maximum(top[:, cols], jnp.max(high, axis=0, keepdims=True))
         return 0
 
-    lax.fori_loop(0, 4, score, 0)
+    lax.fori_loop(0, 2, score, 0)
     total[...] = jnp.zeros(total.shape, F32)
     att_t[...] = jnp.zeros(att_t.shape, F32)
 
     def weigh(k, _):
-        at = pl.ds(pl.multiple_of(k * 512, 512), 512)
+        at = pl.ds(pl.multiple_of(k * 1024, 1024), 1024)
         for h in range(4):
             cols = slice(h * 256, h * 256 + 256)
             weight = jnp.exp2((scores[k, :, cols] - top[:, cols]) * (SCALE * LOG2E))
@@ -343,7 +347,7 @@
             att_t[:, cols] += jnp.dot(values_t[:, at], weight.astype(BF16), preferred_element_type=F32)
         return 0
 
-    lax.fori_loop(0, 4, weigh, 0)
+    lax.fori_loop(0, 2, weigh, 0)
     for h in range(4):
         cols = slice(h * 256, h * 256 + 256)
         inverse = 1.0 / total[:, cols]
@@ -354,9 +358,9 @@
     gq_t[...] = jnp.zeros(gq_t.shape, F32)
 
     def back(k, _):
-        at = pl.ds(pl.multiple_of(k * 512, 512), 512)
-        key_term = jnp.zeros((512, 128), F32)
-        value_term = jnp.zeros((512, 128), F32)
+        at = pl.ds(pl.multiple_of(k * 1024, 1024), 1024)
+        key_term = jnp.zeros((1024, 128), F32)
+        value_term = jnp.zeros((1024, 128), F32)
         for h in range(4):
             cols = slice(h * 256, h * 256 + 256)
             probs = scores[k, :, cols] * total[:, cols]
@@ -365,11 +369,11 @@
             key_term += jnp.dot(dscore, qs[cols], preferred_element_type=F32)
             value_term += jnp.dot(probs.astype(BF16), gs[cols], preferred_element_type=F32)
             gq_t[:, cols] += jnp.dot(keys_t[:, at], dscore, preferred_element_type=F32)
-        terms[pl.ds(k * 2, 2), :, 0:128] = (key_term * SCALE).astype(BF16).reshape(2, 256, 128)
-        terms[pl.ds(k * 2, 2), :, 128:256] = value_term.astype(BF16).reshape(2, 256, 128)
+        terms[pl.ds(k * 4, 4), :, 0:128] = (key_term * SCALE).astype(BF16).reshape(4, 256, 128)
+        terms[pl.ds(k * 4, 4), :, 128:256] = value_term.astype(BF16).reshape(4, 256, 128)
         return 0
 
-    lax.fori_loop(0, 4, back, 0)
+    lax.fori_loop(0, 2, back, 0)
     for h in range(4):
         a = gq_t[:, h * 256 : h * 256 + 256].T * SCALE
         unrotated = a * tables[0] - turn_half(a) * tables[1]
@@ -390,7 +394,7 @@
             pltpu.VMEM((128, 1024), BF16),
             pltpu.VMEM((128, 2048), BF16),
             pltpu.VMEM((128, 2048), BF16),
-            pltpu.VMEM((4, 512, 1024), F32),
+            pltpu.VMEM((2, 1024, 1024), F32),
             pltpu.VMEM((1, 1024), F32),
             pltpu.VMEM((1, 1024), F32),
             pltpu.VMEM((128, 1024), F32),

time: 133 us -> 131 us (0.985)
  Pallas kernels: 125 us -> 123 us
    pallas_call x1, Pallas kernels: 11.6 us -> 9.5 us  [attend(): pl.pallas_call(attention_kernel, out_shape=(shape((256, 512), BF16), shap...]
where the time goes in v9:
time: 131 us
  Pallas kernels  123 us (94%)
  local copies, waits for them, and re-layouts  5.49 us (4%)
  other arithmetic  2.21 us (2%)
    pallas_call x1, Pallas kernels, gather_weights(): pl.pallas_call(gather_kernel, out_shape=(shape((3, 2, 4, 2, 2, 4, 64, 256...  57.6 us
    pallas_call x1, Pallas kernels, scatter_grads(): pl.pallas_call(scatter_kernel, out_shape=(shape((256, 8192), BF16), shape...  55.7 us
    pallas_call x1, Pallas kernels, attend(): pl.pallas_call(attention_kernel, out_shape=(shape((256, 512), BF16), shap...  9.5 us
    unnamed x11, local copies, waits for them, and re-layouts  4.19 us

profile of v9, /device:TPU:0, one launch (start us, length us, event | category | flops | bytes accessed | tf_op | source)
XLA Modules:
  0.0 131.2 jit_solution(11368852061946225628)
XLA Ops:
  0.6 0.0 copy-start.4
  0.6 0.0 copy-start.2
  0.7 0.8 fusion.1
  1.5 0.5 multiply_cosine_fusion
  2.0 0.1 maximum_bitcast_fusion
  2.2 0.7 pad_maximum_fusion.tables_hbm.tables
  2.9 0.0 copy-start
  2.9 57.6 %gather_weights.1 = (bf16[3,2,4,2,2,4,64,256]{7,6,5,4,3,2,1,0:T(8,128)(2,1)}, bf16[8,512,512]{2,1,0:T(8,128)(2,1)}, bf16[256,512]{1,0:T(8,128)(2,1)}, bf16[8,256,256]{2,1,0:T(8,128)(2,1)}) custom-call(bf16[256,8192]{1,0:T(8,128)(2,1)} %bitcast.12, f32[64,512]{1,0:T(8,128)} %wq_hbm.1, f32[64,128]{1,0:T(8,128)} %wk_hbm.1, f32[64,128]{1,0:T(8,128)} %wv_hbm.1, ...), custom_call_target="tpu_custom_call" | custom-call | tf_op jit(solution)/shard_map/gather_weights/pallas_call | solution.py:272
  60.5 0.0 copy-done.4
  60.5 0.0 copy-done.2
  60.5 0.0 copy-done
  60.5 0.0 copy-start.1
  60.5 1.2 copy-done.1
  61.8 0.0 copy-start.3
  61.8 0.9 copy-done.3
  62.7 9.5 %attend.1 = (bf16[256,512]{1,0:T(8,128)(2,1)}, bf16[256,512]{1,0:T(8,128)(2,1)S(1)}, bf16[8,256,256]{2,1,0:T(8,128)(2,1)S(1)}) custom-call(s32[2048]{0:T(1024)S(1)} %copy-done.4, s32[1,256]{1,0:T(1,128)S(1)} %bitcast.11, bf16[256,512]{1,0:T(8,128)(2,1)S(1)} %copy-done.3, bf16[8,256,256]{2,1,0:T(8,128)(2,1)S(1)} %copy-done.1, bf16[256,512]{1,0:T(8,128)(2,1)S(1)} %bitcast.10, ...), custom_call_target="tpu_custom_call" | custom-call | tf_op jit(solution)/shard_map/attend/pallas_call | solution.py:386
  72.2 55.7 %scatter_grads.1 = (bf16[256,8192]{1,0:T(8,128)(2,1)S(1)}, f32[64,768]{1,0:T(8,128)S(1)}) custom-call(bf16[8,512,512]{2,1,0:T(8,128)(2,1)} %get-tuple-element.17.turned, bf16[3,2,4,2,2,4,64,256]{7,6,5,4,3,2,1,0:T(8,128)(2,1)} %get-tuple-element.18.w_all, bf16[256,512]{1,0:T(8,128)(2,1)S(1)} %get-tuple-element.19.grad_q, ...), custom_call_target="tpu_custom_call" | custom-call | tf_op jit(solution)/shard_map/scatter_grads/pallas_call | solution.py:626
  127.9 0.7 slice.9
  128.6 0.6 fusion.2
  129.2 2.0 %copy.12 = bf16[1,256,8192]{2,1,0:T(8,128)(2,1)} copy(bf16[1,256,8192]{2,1,0:T(8,128)(2,1)S(1)} %bitcast.9) | data formatting | bytes 8388608
  (1 shorter events, 0.0 us)
Async XLA Ops:
  0.6 59.9 %copy-start.4 = (s32[2048]{0:T(1024)S(1)}, s32[2048]{0:T(1024)}, u32[]{:S(2)}) copy-start(s32[2048]{0:T(1024)} %positions.1) | copy-start | bytes 24580
  0.6 59.9 %copy-start.2 = (bf16[1,256,512]{2,1,0:T(8,128)(2,1)S(1)}, bf16[1,256,512]{2,1,0:T(8,128)(2,1)}, u32[]{:S(2)}) copy-start(bf16[1,256,512]{2,1,0:T(8,128)(2,1)} %param.11) | copy-start | bytes 786436
  2.9 57.6 %copy-start = (f32[2,256,128]{2,1,0:T(8,128)S(1)}, f32[2,256,128]{2,1,0:T(8,128)}, u32[]{:S(2)}) copy-start(f32[2,256,128]{2,1,0:T(8,128)} %pad_maximum_fusion.tables_hbm.tables) | copy-start | bytes 786436
  60.5 1.2 copy-start.1
  61.8 0.9 copy-start.3

commit v10 on v9

--- a/solution.py
+++ b/solution.py
@@ -318,27 +318,27 @@
     top[...] = jnp.full(top.shape, MASKED, F32)
 
     def tile(k, cols):
-        return kv[pl.ds(k * 4, 4), :, cols].reshape(1024, 128)
+        return kv[:, :, cols].reshape(2048, 128)
 
     def score(k, _):
         for h in range(4):
             cols = slice(h * 256, h * 256 + 256)
             s = lax.dot_general(tile(k, slice(0, 128)), qs[cols], nt, preferred_element_type=F32)
             high = None
-            for r in range(8):
+            for r in range(16):
                 rows = slice(r * 128, r * 128 + 128)
-                run = jnp.where(lead >= positions[k * 1024 + r * 128], s[rows], MASKED)
+                run = jnp.where(lead >= positions[r * 128], s[rows], MASKED)
                 scores[k, rows, cols] = run
                 high = run if high is None else jnp.maximum(high, run)
             top[:, cols] = jnp.maximum(top[:, cols], jnp.max(high, axis=0, keepdims=True))
         return 0
 
-    lax.fori_loop(0, 2, score, 0)
+    score(0, 0)
     total[...] = jnp.zeros(total.shape, F32)
     att_t[...] = jnp.zeros(att_t.shape, F32)
 
     def weigh(k, _):
-        at = pl.ds(pl.multiple_of(k * 1024, 1024), 1024)
+        at = slice(0, 2048)
         for h in range(4):
             cols = slice(h * 256, h * 256 + 256)
             weight = jnp.exp2((scores[k, :, cols] - top[:, cols]) * (SCALE * LOG2E))
@@ -347,7 +347,7 @@
             att_t[:, cols] += jnp.dot(values_t[:, at], weight.astype(BF16), preferred_element_type=F32)
         return 0
 
-    lax.fori_loop(0, 2, weigh, 0)
+    weigh(0, 0)
     for h in range(4):
         cols = slice(h * 256, h * 256 + 256)
         inverse = 1.0 / total[:, cols]
@@ -358,9 +358,9 @@
     gq_t[...] = jnp.zeros(gq_t.shape, F32)
 
     def back(k, _):
-        at = pl.ds(pl.multiple_of(k * 1024, 1024), 1024)
-        key_term = jnp.zeros((1024, 128), F32)
-        value_term = jnp.zeros((1024, 128), F32)
+        at = slice(0, 2048)
+        key_term = jnp.zeros((2048, 128), F32)
+        value_term = jnp.zeros((2048, 128), F32)
         for h in range(4):
             cols = slice(h * 256, h * 256 + 256)
             probs = scores[k, :, cols] * total[:, cols]
@@ -369,11 +369,11 @@
             key_term += jnp.dot(dscore, qs[cols], preferred_element_type=F32)
             value_term += jnp.dot(probs.astype(BF16), gs[cols], preferred_element_type=F32)
             gq_t[:, cols] += jnp.dot(keys_t[:, at], dscore, preferred_element_type=F32)
-        terms[pl.ds(k * 4, 4), :, 0:128] = (key_term * SCALE).astype(BF16).reshape(4, 256, 128)
-        terms[pl.ds(k * 4, 4), :, 128:256] = value_term.astype(BF16).reshape(4, 256, 128)
+        terms[:, :, 0:128] = (key_term * SCALE).astype(BF16).reshape(8, 256, 128)
+        terms[:, :, 128:256] = value_term.astype(BF16).reshape(8, 256, 128)
         return 0
 
-    lax.fori_loop(0, 2, back, 0)
+    back(0, 0)
     for h in range(4):
         a = gq_t[:, h * 256 : h * 256 + 256].T * SCALE
         unrotated = a * tables[0] - turn_half(a) * tables[1]
@@ -394,7 +394,7 @@
             pltpu.VMEM((128, 1024), BF16),
             pltpu.VMEM((128, 2048), BF16),
             pltpu.VMEM((128, 2048), BF16),
-            pltpu.VMEM((2, 1024, 1024), F32),
+            pltpu.VMEM((1, 2048, 1024), F32),
             pltpu.VMEM((1, 1024), F32),
             pltpu.VMEM((1, 1024), F32),
             pltpu.VMEM((128, 1024), F32),

time: 131 us -> 131 us (level)
  no operation moved by 1% of the time
where the time goes in v10:
time: 131 us
  Pallas kernels  122 us (93%)
  local copies, waits for them, and re-layouts  5.49 us (4%)
  other arithmetic  2.21 us (2%)
    pallas_call x1, Pallas kernels, gather_weights(): pl.pallas_call(gather_kernel, out_shape=(shape((3, 2, 4, 2, 2, 4, 64, 256...  57.6 us
    pallas_call x1, Pallas kernels, scatter_grads(): pl.pallas_call(scatter_kernel, out_shape=(shape((256, 8192), BF16), shape...  55.3 us
    pallas_call x1, Pallas kernels, attend(): pl.pallas_call(attention_kernel, out_shape=(shape((256, 512), BF16), shap...  9.38 us
    unnamed x11, local copies, waits for them, and re-layouts  4.19 us

profile of v10, /device:TPU:0, one launch (start us, length us, event | category | flops | bytes accessed | tf_op | source)
XLA Modules:
  0.0 130.8 jit_solution(9898202720586997507)
XLA Ops:
  0.6 0.0 copy-start.4
  0.6 0.0 copy-start.2
  0.7 0.8 fusion.1
  1.5 0.5 multiply_cosine_fusion
  2.0 0.1 maximum_bitcast_fusion
  2.2 0.7 pad_maximum_fusion.tables_hbm.tables
  2.9 0.0 copy-start
  2.9 57.6 %gather_weights.1 = (bf16[3,2,4,2,2,4,64,256]{7,6,5,4,3,2,1,0:T(8,128)(2,1)}, bf16[8,512,512]{2,1,0:T(8,128)(2,1)}, bf16[256,512]{1,0:T(8,128)(2,1)}, bf16[8,256,256]{2,1,0:T(8,128)(2,1)}) custom-call(bf16[256,8192]{1,0:T(8,128)(2,1)} %bitcast.12, f32[64,512]{1,0:T(8,128)} %wq_hbm.1, f32[64,128]{1,0:T(8,128)} %wk_hbm.1, f32[64,128]{1,0:T(8,128)} %wv_hbm.1, ...), custom_call_target="tpu_custom_call" | custom-call | tf_op jit(solution)/shard_map/gather_weights/pallas_call | solution.py:272
  60.5 0.0 copy-done.4
  60.5 0.0 copy-done.2
  60.5 0.0 copy-done
  60.5 0.0 copy-start.1
  60.5 1.2 copy-done.1
  61.8 0.0 copy-start.3
  61.8 0.9 copy-done.3
  62.7 9.4 %attend.1 = (bf16[256,512]{1,0:T(8,128)(2,1)}, bf16[256,512]{1,0:T(8,128)(2,1)S(1)}, bf16[8,256,256]{2,1,0:T(8,128)(2,1)S(1)}) custom-call(s32[2048]{0:T(1024)S(1)} %copy-done.4, s32[1,256]{1,0:T(1,128)S(1)} %bitcast.11, bf16[256,512]{1,0:T(8,128)(2,1)S(1)} %copy-done.3, bf16[8,256,256]{2,1,0:T(8,128)(2,1)S(1)} %copy-done.1, bf16[256,512]{1,0:T(8,128)(2,1)S(1)} %bitcast.10, ...), custom_call_target="tpu_custom_call" | custom-call | tf_op jit(solution)/shard_map/attend/pallas_call | solution.py:386
  72.1 55.3 %scatter_grads.1 = (bf16[256,8192]{1,0:T(8,128)(2,1)S(1)}, f32[64,768]{1,0:T(8,128)S(1)}) custom-call(bf16[8,512,512]{2,1,0:T(8,128)(2,1)} %get-tuple-element.17.turned, bf16[3,2,4,2,2,4,64,256]{7,6,5,4,3,2,1,0:T(8,128)(2,1)} %get-tuple-element.18.w_all, bf16[256,512]{1,0:T(8,128)(2,1)S(1)} %get-tuple-element.19.grad_q, ...), custom_call_target="tpu_custom_call" | custom-call | tf_op jit(solution)/shard_map/scatter_grads/pallas_call | solution.py:626
  127.5 0.7 slice.9
  128.1 0.6 fusion.2
  128.7 2.0 %copy.12 = bf16[1,256,8192]{2,1,0:T(8,128)(2,1)} copy(bf16[1,256,8192]{2,1,0:T(8,128)(2,1)S(1)} %bitcast.9) | data formatting | bytes 8388608
  (1 shorter events, 0.0 us)
Async XLA Ops:
  0.6 59.9 %copy-start.4 = (s32[2048]{0:T(1024)S(1)}, s32[2048]{0:T(1024)}, u32[]{:S(2)}) copy-start(s32[2048]{0:T(1024)} %positions.1) | copy-start | bytes 24580
  0.6 59.9 %copy-start.2 = (bf16[1,256,512]{2,1,0:T(8,128)(2,1)S(1)}, bf16[1,256,512]{2,1,0:T(8,128)(2,1)}, u32[]{:S(2)}) copy-start(bf16[1,256,512]{2,1,0:T(8,128)(2,1)} %param.11) | copy-start | bytes 786436
  2.9 57.6 %copy-start = (f32[2,256,128]{2,1,0:T(8,128)S(1)}, f32[2,256,128]{2,1,0:T(8,128)}, u32[]{:S(2)}) copy-start(f32[2,256,128]{2,1,0:T(8,128)} %pad_maximum_fusion.tables_hbm.tables) | copy-start | bytes 786436
  60.5 1.2 copy-start.1
  61.8 0.9 copy-start.3
